TPU v7x, 32 devices: a whole 2x2x4 slice. The times are simulated.
32 devices in a mesh: row: 8 (over y, x, core), col: 4 (over z).
Axes of the slice: x: 2, y: 2, z: 4, core: 2. Of those that a mesh axis runs over, the one named last changes fastest.
Arguments:
- vorticity_coefficients: bfloat16 [3, 512, 512, 512], P(None, 'row', 'col'), may hold values from -6 to 6
Outputs:
- enstrophy: float32 [512, 512, 512], P('row', 'col')
- normals: bfloat16 [3, 512, 512, 512], P(None, 'row', 'col')
All inputs are finite; a program needn't handle non-finite values.
Results may differ from a plain program's by a relative error of at most 0.001.
Values sent between devices are 32-bit elements; how exact they have to be, the bound alone decides.
No kernel may reach another device: no remote copies, remote signals or barrier semaphores. Data moves between devices by JAX's collectives and lax.ppermute only.
A program may use at most 256 MiB of HBM per device.

v0:
```python
import math

import jax
import jax.numpy as jnp
from jax import lax
from jax.sharding import PartitionSpec as P

EXACT_MULTIPLY = lax.Precision.HIGHEST


def extended(block, sides, width):
    for axis, dim in sides:
        count = lax.axis_size(axis)
        forward = [(i, i + 1) for i in range(count - 1)]
        forward.append((count - 1, 0))
        backward = [(target, source) for source, target in forward]
        low = lax.ppermute(
            lax.slice_in_dim(block, block.shape[dim] - width, None, axis=dim), axis, forward
        )
        high = lax.ppermute(lax.slice_in_dim(block, 0, width, axis=dim), axis, backward)
        block = jnp.concatenate([low, block, high], axis=dim)
    return block


def fourier_table(length):
    wave_number = jnp.arange(length, dtype=jnp.int32)[:, None]
    position = jnp.arange(length, dtype=jnp.int32)[None, :]
    nyquist = length // 2
    frequency = jnp.where(wave_number <= nyquist, wave_number, wave_number - nyquist)
    phase_index = frequency * position % length
    angle_value = phase_index.astype(jnp.float32) * (2.0 * math.pi / length)
    edge_mode = (wave_number == 0) | (wave_number == nyquist)
    hermitian_weight = jnp.where(
        edge_mode, math.sqrt(1.0 / length), math.sqrt(2.0 / length)
    ).astype(jnp.float32)
    return (
        jnp.where(wave_number <= nyquist, jnp.cos(angle_value), jnp.sin(angle_value))
        * hermitian_weight
    )


def first_axis_transform(flattened_spectrum, twiddle_table):
    product = jnp.einsum("cpk,kx->cxp", flattened_spectrum, twiddle_table, precision=EXACT_MULTIPLY)
    return product[None]


def along_second(received, twiddle_table, inner_cols):
    column_group_count = received.shape[0]
    members = received.shape[1]
    planes = received.shape[2]
    flat_size = received.shape[3]
    shaped = received.reshape(
        column_group_count, members, planes, flat_size // inner_cols, inner_cols
    )
    table_blocks = twiddle_table.reshape(
        column_group_count, flat_size // inner_cols, twiddle_table.shape[1]
    )
    product = jnp.einsum("scakq,sky->cyaq", shaped, table_blocks, precision=EXACT_MULTIPLY)
    return product.reshape(1, members, twiddle_table.shape[1], planes * inner_cols)


def body(vorticity_coefficients):
    members = vorticity_coefficients.shape[0]
    span_second = vorticity_coefficients.shape[1]
    span_third = vorticity_coefficients.shape[2]
    length = vorticity_coefficients.shape[3]
    twiddle_table = fourier_table(length)
    widened_input = vorticity_coefficients.astype(jnp.float32).reshape(
        members, span_second * span_third, length
    )
    gathered_parts = []
    for member in range(members):
        spectral = first_axis_transform(widened_input[member : member + 1], twiddle_table)
        received = lax.all_to_all(spectral, "row", split_axis=2, concat_axis=0, tiled=True)
        second = along_second(received, twiddle_table, span_third)
        gathered_parts.append(
            lax.all_to_all(second, "col", split_axis=2, concat_axis=0, tiled=True)
        )
    pencils = jnp.concatenate(gathered_parts, axis=1)
    col_groups = pencils.shape[0]
    span_y = pencils.shape[2]
    span_x = pencils.shape[3] // span_third
    shaped = pencils.reshape(col_groups, members, span_y, span_x, span_third)
    table_blocks = twiddle_table.reshape(col_groups, span_third, length)
    vort_field = jnp.einsum("scbaq,sqz->cabz", shaped, table_blocks, precision=EXACT_MULTIPLY)
    level_field = 0.5 * jnp.sum(vort_field * vort_field, axis=0)
    padded = extended(level_field, (("row", 0), ("col", 1)), 1)
    centre = padded[1:-1, 1:-1]
    step_x = 0.5 * (padded[2:, 1:-1] - padded[:-2, 1:-1])
    step_y = 0.5 * (padded[1:-1, 2:] - padded[1:-1, :-2])
    step_z = 0.5 * (jnp.roll(centre, -1, axis=2) - jnp.roll(centre, 1, axis=2))
    magnitude = jnp.sqrt(step_x * step_x + step_y * step_y + step_z * step_z)
    inverse = 1.0 / jnp.maximum(magnitude, 1.0)
    normals = jnp.stack([-step_x * inverse, -step_y * inverse, -step_z * inverse], axis=0).astype(
        jnp.bfloat16
    )
    return (centre, normals)


def solution(mesh):
    placed = (P(None, "row", "col", None),)
    return jax.shard_map(
        body,
        mesh=mesh,
        in_specs=placed,
        out_specs=(P("row", "col", None), P(None, "row", "col", None)),
        check_vma=False,
    )
```

profile of v0, /device:TPU:0, one launch (start us, length us, event | category | flops | bytes accessed | tf_op | source)
XLA Modules:
  0.0 2114.5 jit_solution(4791556114427393865)
XLA Ops:
  14.7 37.1 %convolution_bitcast_fusion.5 = f32[1,1,512,8192]{3,2,1,0:T(8,128)} fusion(bf16[8192,512]{1,0:T(8,128)(2,1)S(1)} %bitcast.84, f32[512]{0:T(512)S(1)} %fusion.61, s32[512]{0:T(512)S(1)} %add_select_fusion.4, pred[512]{0:T(512)(128)(4,1)S(1)} %iota_compare_fusion.2), kind=kOutput, calls=%fused_computation.37 | convolution fusion | flops 25773998080 | bytes 25170432 | tf_op jit(solution)/shard_map/cpk,kx->cxp/dot_general | solution.py:43
  51.8 19.9 copy.34
  77.5 40.4 %convolution_bitcast_fusion.3 = f32[1,1,512,8192]{3,2,1,0:T(8,128)} fusion(bf16[8192,512]{1,0:T(8,128)(2,1)} %bitcast.83, f32[512]{0:T(512)S(1)} %fusion.61, s32[512]{0:T(512)S(1)} %add_select_fusion.4, pred[512]{0:T(512)(128)(4,1)S(1)} %iota_compare_fusion.2), kind=kOutput, calls=%fused_computation.35 | convolution fusion | flops 25773998080 | bytes 25170432 | tf_op jit(solution)/shard_map/cpk,kx->cxp/dot_general | solution.py:43
  118.0 19.9 copy.37
  137.8 124.1 %all-to-all-done = f32[1,1,512,8192]{3,1,0,2:T(1,128)} async-done(((f32[1,1,512,8192]{3,1,0,2:T(1,128)}), f32[1,1,512,8192]{3,1,0,2:T(1,128)}, u32[]{:S(2)}, u32[]{:S(2)}) %all-to-all-start) | async-done | bytes 16777248 | tf_op jit(solution)/shard_map/all_to_all | solution.py:74
  267.8 40.4 %convolution_bitcast_fusion.1 = f32[1,1,512,8192]{3,2,1,0:T(8,128)} fusion(bf16[8192,512]{1,0:T(8,128)(2,1)} %bitcast.82, f32[512]{0:T(512)S(1)} %fusion.61, s32[512]{0:T(512)S(1)} %add_select_fusion.4, pred[512]{0:T(512)(128)(4,1)S(1)} %iota_compare_fusion.2), kind=kOutput, calls=%fused_computation.33 | convolution fusion | flops 25773998080 | bytes 25170432 | tf_op jit(solution)/shard_map/cpk,kx->cxp/dot_general | solution.py:43
  308.2 19.9 copy.40
  328.1 123.5 %all-to-all-done.2 = f32[1,1,512,8192]{3,1,0,2:T(1,128)} async-done(((f32[1,1,512,8192]{3,1,0,2:T(1,128)}), f32[1,1,512,8192]{3,1,0,2:T(1,128)}, u32[]{:S(2)}, u32[]{:S(2)}) %all-to-all-start.2) | async-done | bytes 16777248 | tf_op jit(solution)/shard_map/all_to_all | solution.py:74
  457.4 17.8 copy.59
  475.1 18.2 dot_general.41
  493.3 43.4 %convolution_bitcast_fusion.4 = f32[1,1,512,8192]{3,2,1,0:T(8,128)} fusion(f32[8192,64,8]{0,1,2:T(8,128)} %dot_general.41, f32[64,8]{0,1:T(8,128)S(1)} %fusion.54, s32[64,8]{0,1:T(8,128)S(1)} %add_select_fusion.3, pred[64,8]{0,1:T(8,128)(4,1)S(1)} %fusion.52), kind=kOutput, calls=%fused_computation.36 | convolution fusion | flops 25773998080 | bytes 33559040 | tf_op jit(solution)/shard_map/scakq,sky->cyaq/dot_general | solution.py:58
  536.8 19.9 copy.36
  556.7 84.6 %all-to-all-done.4 = f32[1,1,512,8192]{3,1,0,2:T(1,128)} async-done(((f32[1,1,512,8192]{3,1,0,2:T(1,128)}), f32[1,1,512,8192]{3,1,0,2:T(1,128)}, u32[]{:S(2)}, u32[]{:S(2)}) %all-to-all-start.4) | async-done | bytes 16777248 | tf_op jit(solution)/shard_map/all_to_all | solution.py:74
  648.3 17.8 copy.58
  666.0 18.2 dot_general.46
  684.2 43.3 %convolution_bitcast_fusion.2 = f32[1,1,512,8192]{3,2,1,0:T(8,128)} fusion(f32[8192,64,8]{0,1,2:T(8,128)} %dot_general.46, f32[64,8]{0,1:T(8,128)S(1)} %fusion.54, s32[64,8]{0,1:T(8,128)S(1)} %add_select_fusion.3, pred[64,8]{0,1:T(8,128)(4,1)S(1)} %fusion.52), kind=kOutput, calls=%fused_computation.34 | convolution fusion | flops 25773998080 | bytes 33559040 | tf_op jit(solution)/shard_map/scakq,sky->cyaq/dot_general | solution.py:58
  727.5 19.9 copy.39
  747.4 261.9 %all-to-all-done.1 = f32[1,1,512,8192]{3,1,0,2:T(1,128)} async-done(((f32[1,1,512,8192]{3,1,0,2:T(1,128)}), f32[1,1,512,8192]{3,1,0,2:T(1,128)}, u32[]{:S(2)}, u32[]{:S(2)}) %all-to-all-start.1) | async-done | bytes 16777248 | tf_op jit(solution)/shard_map/all_to_all | solution.py:77
  1016.4 17.8 copy.57
  1034.1 18.2 dot_general.51
  1052.3 43.3 %convolution_bitcast_fusion = f32[1,1,512,8192]{3,2,1,0:T(8,128)} fusion(f32[8192,64,8]{0,1,2:T(8,128)} %dot_general.51, f32[64,8]{0,1:T(8,128)S(1)} %fusion.54, s32[64,8]{0,1:T(8,128)S(1)} %add_select_fusion.3, pred[64,8]{0,1:T(8,128)(4,1)S(1)} %fusion.52), kind=kOutput, calls=%fused_computation.32 | convolution fusion | flops 25773998080 | bytes 33559040 | tf_op jit(solution)/shard_map/scakq,sky->cyaq/dot_general | solution.py:58
  1095.6 19.9 copy.42
  1115.5 263.1 %all-to-all-done.3 = f32[1,1,512,8192]{3,1,0,2:T(1,128)} async-done(((f32[1,1,512,8192]{3,1,0,2:T(1,128)}), f32[1,1,512,8192]{3,1,0,2:T(1,128)}, u32[]{:S(2)}, u32[]{:S(2)}) %all-to-all-start.3) | async-done | bytes 16777248 | tf_op jit(solution)/shard_map/all_to_all | solution.py:77
  1389.8 16.0 copy.43
  1421.7 326.3 %all-to-all-done.5 = f32[1,1,512,8192]{3,1,0,2:T(1,128)} async-done(((f32[1,1,512,8192]{3,1,0,2:T(1,128)}), f32[1,1,512,8192]{3,1,0,2:T(1,128)}, u32[]{:S(2)}, u32[]{:S(2)}) %all-to-all-start.5) | async-done | bytes 16777248 | tf_op jit(solution)/shard_map/all_to_all | solution.py:77
  1748.0 16.1 copy.45
  1764.1 92.5 %fusion.6 = f32[512,128,64]{1,0,2:T(8,128)} fusion(f32[4,1,128,64,128]{4,2,0,3,1:T(8,128)} %copy.45, f32[4,1,128,64,128]{4,2,0,3,1:T(8,128)} %copy.44, f32[4,1,128,64,128]{4,2,0,3,1:T(8,128)} %copy.43, f32[4,128,512,1,1]{1,2,0,4,3:T(8,128)S(1)} %fusion.108), kind=kOutput, calls=%fused_computation.7 | convolution fusion | flops 77355548672 | bytes 68157440 | tf_op jit(solution)/shard_map/scbaq,sqz->cabz/dot_general | solution.py:85
  1880.9 17.4 copy.50
  1956.0 58.1 %fusion.16 = (bf16[1,64,128,512]{2,3,1,0:T(8,128)(2,1)}, f32[64,128,512]{1,2,0:T(8,128)}) fusion(f32[64,128,512]{1,2,0:T(8,128)} %copy-done, f32[1,128,512]{1,2,0:T(8,128)S(1)} %collective-permute-done.1, f32[1,128,512]{1,2,0:T(8,128)S(1)} %collective-permute-done, f32[64,128,511]{1,2,0:T(8,128)} %get-tuple-element.18, ...), kind=kLoop, calls=%fused_computation.40 | loop fusion | flops 109051904 | bytes 76292096 | tf_op jit(solution)/shard_map/stack | solution.py:94
  2014.2 49.7 %fusion.14 = (bf16[1,64,128,512]{2,3,1,0:T(8,128)(2,1)}, bf16[1,64,128,512]{2,3,1,0:T(8,128)(2,1)}) fusion(f32[64,128,512]{1,2,0:T(8,128)} %get-tuple-element.9, f32[1,128,512]{1,2,0:T(8,128)S(1)} %collective-permute-done, f32[64,128,512]{1,2,0:T(8,128)} %copy-done, f32[1,128,512]{1,2,0:T(8,128)S(1)} %collective-permute-done.1, f32[66,1,512]{1,2,0:T(8,128)} %copy.49, ...), kind=kLoop, calls=%fused_computation.38 | loop fusion | flops 75497472 | bytes 84680704 | tf_op jit(solution)/shard_map/stack | solution.py:94
  2063.9 17.6 pad_maximum_fusion
  2081.5 32.6 %copy.51 = bf16[3,64,128,512]{3,2,1,0:T(8,128)(2,1)} copy(bf16[3,64,128,512]{2,3,1,0:T(8,128)(2,1)} %pad_maximum_fusion) | data formatting | bytes 50331648
  (38 shorter events, 154.7 us)
Async XLA Ops:
  71.6 190.3 %all-to-all-start = ((f32[1,1,512,8192]{3,1,0,2:T(1,128)}), f32[1,1,512,8192]{3,1,0,2:T(1,128)}, u32[]{:S(2)}, u32[]{:S(2)}) async-start(f32[1,1,512,8192]{3,1,0,2:T(1,128)} %copy.34), calls=%async_computation | async-start | bytes 33554432 | tf_op jit(solution)/shard_map/all_to_all | solution.py:74
  261.9 189.7 %all-to-all-start.2 = ((f32[1,1,512,8192]{3,1,0,2:T(1,128)}), f32[1,1,512,8192]{3,1,0,2:T(1,128)}, u32[]{:S(2)}, u32[]{:S(2)}) async-start(f32[1,1,512,8192]{3,1,0,2:T(1,128)} %copy.37), calls=%async_computation.2 | async-start | bytes 33554432 | tf_op jit(solution)/shard_map/all_to_all | solution.py:74
  451.6 189.7 %all-to-all-start.4 = ((f32[1,1,512,8192]{3,1,0,2:T(1,128)}), f32[1,1,512,8192]{3,1,0,2:T(1,128)}, u32[]{:S(2)}, u32[]{:S(2)}) async-start(f32[1,1,512,8192]{3,1,0,2:T(1,128)} %copy.40), calls=%async_computation.4 | async-start | bytes 33554432 | tf_op jit(solution)/shard_map/all_to_all | solution.py:74
  641.3 368.0 %all-to-all-start.1 = ((f32[1,1,512,8192]{3,1,0,2:T(1,128)}), f32[1,1,512,8192]{3,1,0,2:T(1,128)}, u32[]{:S(2)}, u32[]{:S(2)}) async-start(f32[1,1,512,8192]{3,1,0,2:T(1,128)} %copy.36), calls=%async_computation.1 | async-start | bytes 33554432 | tf_op jit(solution)/shard_map/all_to_all | solution.py:77
  1009.3 369.4 %all-to-all-start.3 = ((f32[1,1,512,8192]{3,1,0,2:T(1,128)}), f32[1,1,512,8192]{3,1,0,2:T(1,128)}, u32[]{:S(2)}, u32[]{:S(2)}) async-start(f32[1,1,512,8192]{3,1,0,2:T(1,128)} %copy.39), calls=%async_computation.3 | async-start | bytes 33554432 | tf_op jit(solution)/shard_map/all_to_all | solution.py:77
  1378.6 369.3 %all-to-all-start.5 = ((f32[1,1,512,8192]{3,1,0,2:T(1,128)}), f32[1,1,512,8192]{3,1,0,2:T(1,128)}, u32[]{:S(2)}, u32[]{:S(2)}) async-start(f32[1,1,512,8192]{3,1,0,2:T(1,128)} %copy.42), calls=%async_computation.5 | async-start | bytes 33554432 | tf_op jit(solution)/shard_map/all_to_all | solution.py:77
  1863.5 5.8 copy-start
  1863.6 34.8 %collective-permute-start = (f32[1,128,512]{1,2,0:T(8,128)S(1)}, f32[1,128,512]{1,2,0:T(8,128)S(1)}, u32[]{:S(2)}, u32[]{:S(2)}) collective-permute-start(f32[1,128,512]{1,2,0:T(8,128)S(1)} %get-tuple-element.21), channel_id=1, source_target_pairs={{4,0},{8,4},{12,8},{16,12},{20,16},{24,20},{28,24},{0,28},{5,1},{9... | collective-permute-start | bytes 786440 | tf_op jit(solution)/shard_map/ppermute | solution.py:20
  1866.0 32.4 %collective-permute-start.1 = (f32[1,128,512]{1,2,0:T(8,128)S(1)}, f32[1,128,512]{1,2,0:T(8,128)S(1)}, u32[]{:S(2)}, u32[]{:S(2)}) collective-permute-start(f32[1,128,512]{1,2,0:T(8,128)S(1)} %get-tuple-element.22), channel_id=1, source_target_pairs={{0,4},{4,8},{8,12},{12,16},{16,20},{20,24},{24,28},{28,0},{1,5},{5... | collective-permute-start | bytes 786440 | tf_op jit(solution)/shard_map/ppermute | solution.py:17
  1927.1 12.4 collective-permute-start.2
  1937.8 9.9 collective-permute-start.3
where the time goes:
time: 2130 us; the launch traced here: 2110 us
  waiting for transfers between devices  1180 us (55%)
  local copies, waits for them, and re-layouts  403 us (19%)
  matrix products  340 us (16%)
  other arithmetic  143 us (7%)
  starting transfers between devices  43.1 us (2%)
    all_to_all x3, waiting for transfers between devices, body(): lax.all_to_all(second, 'col', split_axis=2, concat_axis=0, tiled=True)  851 us
    all_to_all x3, waiting for transfers between devices, body(): lax.all_to_all(spectral, 'row', split_axis=2, concat_axis=0, tiled=True)  332 us
    dot_general x3, matrix products, along_second(): jnp.einsum('scakq,sky->cyaq', shaped, table_blocks, precision=EXACT_MULTI...  130 us
    another operation x3, other arithmetic, body(): jnp.stack([-step_x * inverse, -step_y * inverse, -step_z * inverse], axis=0)  125 us
    dot_general x3, matrix products, first_axis_transform(): jnp.einsum('cpk,kx->cxp', flattened_spectrum, twiddle_table, precision=EX...  118 us
    dot_general x6, local copies, waits for them, and re-layouts, along_second(): jnp.einsum('scakq,sky->cyaq', shaped, table_blocks, precision=EXACT_MULTI...  114 us
    dot_general x1, matrix products, body(): jnp.einsum('scbaq,sqz->cabz', shaped, table_blocks, precision=EXACT_MULTI...  92.5 us
    transpose x3, local copies, waits for them, and re-layouts, first_axis_transform(): return product[None]  59.6 us
  transfers between devices with their start and end apart: 10, of which 6 were waited for; matrix products, arithmetic and copies ran while one was open for 24% of the time, Pallas kernels for 0%

commit v1 on v0

v1 whole, which is shorter than its diff:
```python
import functools
import math

import jax
import jax.numpy as jnp
import ml_dtypes
import numpy as np
from jax import lax
from jax.experimental import pallas as pl
from jax.experimental.pallas import tpu as pltpu
from jax.sharding import PartitionSpec as P

EXACT = lax.Precision.HIGHEST
TABLE_PARTS = (0, 1, 2, 0, 1, 0)
VALUE_PARTS = (0, 0, 0, 1, 1, 2)
VMEM_BYTES = 48 * 1024 * 1024
SCALE = 1.0


def fourier_table(length):
    wave_number = np.arange(length)[:, None]
    position = np.arange(length)[None, :]
    nyquist = length // 2
    frequency = np.where(wave_number <= nyquist, wave_number, wave_number - nyquist)
    angle = (frequency * position % length) * (2.0 * math.pi / length)
    edge = (wave_number == 0) | (wave_number == nyquist)
    weight = np.where(edge, math.sqrt(1.0 / length), math.sqrt(2.0 / length))
    table = np.where(wave_number <= nyquist, np.cos(angle), np.sin(angle)) * weight
    return table.astype(np.float32)


def table_parts(table):
    parts = []
    rest = table
    for _ in range(3):
        part = rest.astype(ml_dtypes.bfloat16)
        parts.append(part)
        rest = rest - part.astype(np.float32)
    return parts


def value_parts(value):
    high = value.astype(jnp.bfloat16)
    rest = value - high.astype(jnp.float32)
    middle = rest.astype(jnp.bfloat16)
    low = (rest - middle.astype(jnp.float32)).astype(jnp.bfloat16)
    return high, middle, low


def partner(me, step, count):
    if count & (count - 1) == 0:
        return me ^ step
    return (me + step) % count


def sender(me, step, count):
    if count & (count - 1) == 0:
        return me ^ step
    return (me + count - step) % count


ANY = pl.BlockSpec(memory_space=pl.ANY)


def cost(time):
    return pl.CostEstimate(flops=0, bytes_accessed=int(SCALE * time * 3.0e6), transcendentals=0)


def params():
    return pltpu.CompilerParams(vmem_limit_bytes=VMEM_BYTES)


def first_kernel(table_ref, x_ref, *rest, groups):
    outs = rest[-groups:]
    rows = table_ref.shape[0] // 3
    width = rows // groups
    tile, inner, length = x_ref.shape
    flat = [out.reshape(width * tile, inner) for out in outs]

    @pl.loop(0, tile // 2)
    def _(pair):
        block = x_ref[pl.ds(2 * pair, 2)].reshape(2 * inner, length)
        product = lax.dot_general(
            table_ref[...], block, (((1,), (1,)), ((), ())), preferred_element_type=jnp.float32
        )
        total = product[2 * rows :] + product[rows : 2 * rows] + product[:rows]
        for step in range(groups):
            for j in range(2):
                flat[step][pl.ds(2 * pair + j, width, stride=tile), :] = total[
                    step * width : (step + 1) * width, j * inner : (j + 1) * inner
                ]


def ordered_blocks(array, axis, blocks):
    return jnp.concatenate(
        [lax.dynamic_slice_in_dim(array, block, 1, axis=axis) for block in blocks], axis=axis
    )


def first_transform(spectrum, table, ordered, blocks, first, width, after):
    members, span_b, span_q, length = spectrum.shape
    groups = len(blocks)
    out_shape = (members, width, span_b, span_q)
    if span_q % 128 or span_b % 8:
        chosen = jnp.asarray(table).reshape(length, groups, -1)[:, :, first : first + width]
        chosen = ordered_blocks(chosen, 1, blocks)
        outs = jnp.einsum("cbqk,ksx->scxbq", spectrum.astype(jnp.float32), chosen, precision=EXACT)
        return [outs[step] for step in range(groups)]
    operand = ordered[:, :, first : first + width].reshape(-1, length)
    tile = 8
    return pl.pallas_call(
        functools.partial(first_kernel, groups=groups),
        grid=(members, span_b // tile),
        in_specs=[
            pl.BlockSpec(operand.shape, lambda c, b: (0, 0)),
            pl.BlockSpec((None, tile, span_q, length), lambda c, b: (c, b, 0, 0)),
        ]
        + [ANY] * len(after),
        out_specs=[pl.BlockSpec((None, width, tile, span_q), lambda c, b: (c, 0, b, 0))] * groups,
        out_shape=[jax.ShapeDtypeStruct(out_shape, jnp.float32)] * groups,
        compiler_params=params(),
        cost_estimate=cost(22 + width),
        name="first",
    )(operand, spectrum, *after)


def second_kernel(sources_ref, table_ref, *rest, count):
    ins, out_ref, value_ref = rest[:count], rest[-2], rest[-1]
    width, span_b, span_q = ins[0].shape
    for step in range(count):
        at = pl.multiple_of(sources_ref[step] * span_b, 8)
        for j in range(width):
            value_ref[pl.ds(at, span_b), j * span_q : (j + 1) * span_q] = ins[step][j]
    parts = value_parts(value_ref[...])
    stacked = jnp.concatenate([parts[p] for p in VALUE_PARTS], axis=0)
    product = jnp.dot(table_ref[...], stacked, preferred_element_type=jnp.float32)
    groups, _, span_y, _ = out_ref.shape
    for j in range(width):
        out_ref[:, j] = product[:, j * span_q : (j + 1) * span_q].reshape(groups, span_y, span_q)


def second_transform(pieces, table, stacked, sources, groups, after):
    count = len(pieces)
    members, width, span_b, span_q = pieces[0].shape
    length = count * span_b
    span_y = length // groups
    if span_q % 128 or span_b % 8 or span_y % 8:
        chosen = ordered_blocks(jnp.asarray(table).reshape(count, span_b, length), 0, sources)
        chosen = chosen.reshape(count, span_b, groups, span_y)
        return jnp.einsum("scabq,sbgy->gcayq", jnp.stack(pieces), chosen, precision=EXACT)
    tile = 2 if width % 2 == 0 else 1
    out_shape = (groups, members, width, span_y, span_q)
    return pl.pallas_call(
        functools.partial(second_kernel, count=count),
        grid=(members, width // tile),
        in_specs=[
            pl.BlockSpec(memory_space=pltpu.SMEM),
            pl.BlockSpec(stacked.shape, lambda c, a: (0, 0)),
        ]
        + [pl.BlockSpec((None, tile, span_b, span_q), lambda c, a: (c, a, 0, 0))] * count
        + [ANY] * len(after),
        out_specs=pl.BlockSpec(
            (groups, None, tile, span_y, span_q), lambda c, a: (0, c, a, 0, 0)
        ),
        out_shape=jax.ShapeDtypeStruct(out_shape, jnp.float32),
        scratch_shapes=[pltpu.VMEM((length, tile * span_q), jnp.float32)],
        compiler_params=params(),
        cost_estimate=cost(1 + 2 * width),
        name="second",
    )(jnp.stack(sources).astype(jnp.int32), stacked, *pieces, *after)


def third_kernel(table_ref, in_ref, *rest):
    out_ref, low_ref, high_ref = rest[-3:]
    member = pl.program_id(1)
    groups, width, span_y, span_q = in_ref.shape
    value = jnp.concatenate(
        [in_ref[g].reshape(width * span_y, span_q) for g in range(groups)], axis=1
    )
    parts = value_parts(value)
    stacked = jnp.concatenate([parts[p] for p in VALUE_PARTS], axis=1)
    field = jnp.dot(stacked, table_ref[...], preferred_element_type=jnp.float32)
    level = (0.5 * (field * field)).reshape(out_ref.shape)

    @pl.when(member == 0)
    def _():
        out_ref[...] = level

    @pl.when(member > 0)
    def _():
        out_ref[...] += level

    @pl.when(member == pl.num_programs(1) - 1)
    def _():
        low_ref[...] = out_ref[:, :1]
        high_ref[...] = out_ref[:, span_y - 1 :]


def third_transform(received, table, stacked, after):
    groups, members, width, span_y, span_q = received.shape
    length = groups * span_q
    if span_q % 128 or span_y % 8:
        chosen = jnp.asarray(table).reshape(groups, span_q, length)
        field = jnp.einsum("scayq,sqz->cayz", received, chosen, precision=EXACT)
        level = 0.5 * jnp.sum(field * field, axis=0)
        return level, level[:, :1], level[:, -1:]
    tile = 2 if width % 2 == 0 else 1
    return pl.pallas_call(
        third_kernel,
        grid=(width // tile, members),
        in_specs=[
            pl.BlockSpec(stacked.shape, lambda a, c: (0, 0)),
            pl.BlockSpec((groups, None, tile, span_y, span_q), lambda a, c: (0, c, a, 0, 0)),
        ]
        + [ANY] * len(after),
        out_specs=[
            pl.BlockSpec((tile, span_y, length), lambda a, c: (a, 0, 0)),
            pl.BlockSpec((tile, 1, length), lambda a, c: (a, 0, 0)),
            pl.BlockSpec((tile, 1, length), lambda a, c: (a, 0, 0)),
        ],
        out_shape=[
            jax.ShapeDtypeStruct((width, span_y, length), jnp.float32),
            jax.ShapeDtypeStruct((width, 1, length), jnp.float32),
            jax.ShapeDtypeStruct((width, 1, length), jnp.float32),
        ],
        compiler_params=params(),
        cost_estimate=cost(1 + 2 * width),
        name="third",
    )(stacked, received, *after)


def normal_kernel(centre_ref, before_ref, behind_ref, low_ref, high_ref, *rest):
    level_ref, normal_ref = rest[-2:]
    width, span_y, length = centre_ref.shape
    i = pl.program_id(0)
    centre = centre_ref[i]
    before = jnp.where(i == 0, before_ref[0], centre_ref[jnp.maximum(i - 1, 0)])
    behind = jnp.where(i == width - 1, behind_ref[0], centre_ref[jnp.minimum(i + 1, width - 1)])
    row = lax.broadcasted_iota(jnp.int32, (span_y, length), 0)
    left = jnp.where(row == 0, low_ref[i], pltpu.roll(centre, 1, 0))
    right = jnp.where(row == span_y - 1, high_ref[i], pltpu.roll(centre, span_y - 1, 0))
    step_x = 0.5 * (behind - before)
    step_y = 0.5 * (right - left)
    step_z = 0.5 * (pltpu.roll(centre, length - 1, 1) - pltpu.roll(centre, 1, 1))
    magnitude = jnp.sqrt(step_x * step_x + step_y * step_y + step_z * step_z)
    inverse = -1.0 / jnp.maximum(magnitude, 1.0)
    level_ref[0] = centre
    normal_ref[0, 0] = (step_x * inverse).astype(jnp.bfloat16)
    normal_ref[1, 0] = (step_y * inverse).astype(jnp.bfloat16)
    normal_ref[2, 0] = (step_z * inverse).astype(jnp.bfloat16)


def write_normals(centre, before, behind, low, high, first, whole, held):
    width, span_y, length = centre.shape
    before, before_at = before
    behind, behind_at = behind
    held = () if held is None else held
    return pl.pallas_call(
        normal_kernel,
        grid=(width,),
        in_specs=[
            pl.BlockSpec((width, span_y, length), lambda i: (0, 0, 0)),
            pl.BlockSpec((1, span_y, length), lambda i: (before_at, 0, 0)),
            pl.BlockSpec((1, span_y, length), lambda i: (behind_at, 0, 0)),
            pl.BlockSpec((width, 1, length), lambda i: (0, 0, 0)),
            pl.BlockSpec((width, 1, length), lambda i: (0, 0, 0)),
        ]
        + [ANY] * len(held),
        out_specs=[
            pl.BlockSpec((1, span_y, length), lambda i: (first + i, 0, 0)),
            pl.BlockSpec((3, 1, span_y, length), lambda i: (0, first + i, 0, 0)),
        ],
        out_shape=[
            jax.ShapeDtypeStruct((whole, span_y, length), jnp.float32),
            jax.ShapeDtypeStruct((3, whole, span_y, length), jnp.bfloat16),
        ],
        input_output_aliases={5 + k: k for k in range(len(held))},
        compiler_params=params(),
        cost_estimate=cost(1 + width / 2),
        name="normals",
    )(centre, before, behind, low, high, *held)


def slab_widths(half):
    widths = []
    left = half
    while left:
        width = min(2 ** (1 + len(widths)), 10, left)
        widths.append(width)
        left -= width
    return widths


def ring(axis, up):
    count = lax.axis_size(axis)
    return [(i, (i + 1) % count if up else (i - 1) % count) for i in range(count)]


def body(spectrum):
    length = spectrum.shape[3]
    rows = lax.axis_size("row")
    cols = lax.axis_size("col")
    planes = length // rows
    table = fourier_table(length)
    parts = table_parts(table)
    first_table = np.stack([part.T.reshape(rows, planes, length) for part in parts])
    second_table = jnp.asarray(np.concatenate([parts[p].T for p in TABLE_PARTS], axis=1))
    third_table = jnp.asarray(np.concatenate([parts[p] for p in TABLE_PARTS], axis=0))

    half = planes // 2
    widths = slab_widths(planes - half) + slab_widths(half)[::-1]
    starts = []
    at = half
    for width in widths:
        starts.append(at % planes)
        at += width
    slabs = len(widths)
    split = len(slab_widths(planes - half))

    me = lax.axis_index("row")
    targets = [partner(me, step, rows) for step in range(rows)]
    sources = [sender(me, step, rows) for step in range(rows)]
    pairs = [[(i, partner(i, step, rows)) for i in range(rows)] for step in range(rows)]
    ordered = ordered_blocks(jnp.asarray(first_table), 1, targets)

    def first(slab, after):
        outs = first_transform(spectrum, table, ordered, targets, starts[slab], widths[slab], after)
        return [outs[0]] + [
            lax.ppermute(outs[step], "row", pairs[step]) for step in range(1, rows)
        ]

    levels, lows, highs = {}, {}, {}
    low_halo, high_halo = {}, {}
    halo = {}

    def exchange_rows(chosen):
        low = jnp.concatenate([lows[s] for s in chosen], axis=0)
        high = jnp.concatenate([highs[s] for s in chosen], axis=0)
        from_before = lax.ppermute(high, "col", ring("col", True))
        from_behind = lax.ppermute(low, "col", ring("col", False))
        at = 0
        for s in chosen:
            low_halo[s] = from_before[at : at + widths[s]]
            high_halo[s] = from_behind[at : at + widths[s]]
            at += widths[s]

    def exchange_planes():
        halo["before"] = lax.ppermute(levels[split - 1][-1:], "row", ring("row", True))
        halo["behind"] = lax.ppermute(levels[split][:1], "row", ring("row", False))

    held = None

    def normals(slab):
        nonlocal held
        before = (levels[(slab - 1) % slabs], widths[(slab - 1) % slabs] - 1)
        behind = (levels[(slab + 1) % slabs], 0)
        if slab == split:
            before = (halo["before"], 0)
        if slab == split - 1:
            behind = (halo["behind"], 0)
        held = write_normals(
            levels[slab], before, behind, low_halo[slab], high_halo[slab], starts[slab], planes, held
        )

    def third(slab, after):
        levels[slab], lows[slab], highs[slab] = third_transform(
            arrived.pop(slab), table, third_table, after
        )

    def second(slab, after):
        return second_transform(pieces.pop(slab), table, second_table, sources, cols, after)

    pieces, arrived = {}, {}
    pieces[0] = first(0, ())
    pieces[1] = first(1, (pieces[0][0],))
    for slab in range(slabs):
        if slab >= 2:
            third(slab - 2, ())
        spread = second(slab, (levels[slab - 2],) if slab >= 2 else ())
        arrived[slab] = lax.all_to_all(spread, "col", split_axis=0, concat_axis=0, tiled=True)
        if slab + 2 < slabs:
            pieces[slab + 2] = first(slab + 2, (spread,))
    third(slabs - 2, ())
    third(slabs - 1, ())
    exchange_planes()
    exchange_rows(list(range(0, split)))
    exchange_rows(list(range(split, slabs - 1)))
    exchange_rows([slabs - 1])
    for slab in list(range(1, slabs)) + [0]:
        normals(slab)
    return tuple(held)


def solution(mesh):
    return jax.shard_map(
        body,
        mesh=mesh,
        in_specs=(P(None, "row", "col", None),),
        out_specs=(P("row", "col", None), P(None, "row", "col", None)),
        check_vma=False,
    )
```

time: 2130 us -> 1410 us (0.66)
  Pallas kernels: 0 us -> 571 us
  waiting for transfers between devices: 1180 us -> 629 us
  local copies, waits for them, and re-layouts: 403 us -> 47.4 us
  matrix products: 340 us -> 0 us
  other arithmetic: 143 us -> 0.75 us
  starting transfers between devices: 43.1 us -> 149 us
    all_to_all x6 -> x10, waiting for transfers between devices: 1180 us -> 206 us  [body(): lax.all_to_all(spread, 'col', split_axis=0, concat_axis=0, tiled=True)]
    pallas_call x0 -> x40, Pallas kernels: none -> 571 us  [the longest x10 285 us: first_transform(): pl.pallas_call(functools.partial(first_kernel, groups=groups), grid=(memb...]
    ppermute x4 -> x78, waiting for transfers between devices: 0.01 us -> 422 us  [the longest x70 399 us: first(): lax.ppermute(outs[step], 'row', pairs[step])]
    dot_general x7 -> x0, matrix products: 340 us -> none  [the longest x3 130 us: along_second(): jnp.einsum('scakq,sky->cyaq', shaped, table_blocks, precision=EXACT_MULTI...]
    another operation x3 -> x0, other arithmetic: 125 us -> none  [body(): jnp.stack([-step_x * inverse, -step_y * inverse, -step_z * inverse], axis=0)]
    dot_general x6 -> x0, local copies, waits for them, and re-layouts: 114 us -> none  [along_second(): jnp.einsum('scakq,sky->cyaq', shaped, table_blocks, precision=EXACT_MULTI...]
    ppermute x4 -> x78, starting transfers between devices: 4.5 us -> 96.6 us  [the longest x70 78.6 us: first(): lax.ppermute(outs[step], 'row', pairs[step])]
    transpose x3 -> x0, local copies, waits for them, and re-layouts: 59.6 us -> none  [first_axis_transform(): return product[None]]
  transfers between devices with their start and end apart: 10 -> 88, of which waited for: 6 -> 34; matrix products, arithmetic and copies ran while one was open for 24% -> 1% of each run, Pallas kernels for 0% -> 38%
where the time goes in v1:
time: 1410 us; the launch traced here: 1400 us
  waiting for transfers between devices  629 us (45%)
  Pallas kernels  571 us (40%)
  starting transfers between devices  149 us (11%)
  local copies, waits for them, and re-layouts  47.4 us (3%)
    ppermute x70, waiting for transfers between devices, first(): lax.ppermute(outs[step], 'row', pairs[step])  399 us
    pallas_call x10, Pallas kernels, first_transform(): pl.pallas_call(functools.partial(first_kernel, groups=groups), grid=(memb...  285 us
    all_to_all x10, waiting for transfers between devices, body(): lax.all_to_all(spread, 'col', split_axis=0, concat_axis=0, tiled=True)  206 us
    pallas_call x10, Pallas kernels, second_transform(): pl.pallas_call(functools.partial(second_kernel, count=count), grid=(membe...  129 us
    pallas_call x10, Pallas kernels, third_transform(): pl.pallas_call(third_kernel, grid=(width // tile, members), in_specs=[pl....  111 us
    ppermute x70, starting transfers between devices, first(): lax.ppermute(outs[step], 'row', pairs[step])  78.6 us
    all_to_all x10, starting transfers between devices, body(): lax.all_to_all(spread, 'col', split_axis=0, concat_axis=0, tiled=True)  52.2 us
    pallas_call x10, Pallas kernels, write_normals(): pl.pallas_call(normal_kernel, grid=(width,), in_specs=[pl.BlockSpec((widt...  46.6 us
  transfers between devices with their start and end apart: 88, of which 34 were waited for; matrix products, arithmetic and copies ran while one was open for 1% of the time, Pallas kernels for 38%

profile of v1, /device:TPU:0, one launch (start us, length us, event | category | flops | bytes accessed | tf_op | source)
XLA Modules:
  0.0 1398.4 jit_solution(13819307903071070836)
XLA Ops:
  9.5 26.3 %first.10 = (f32[3,2,64,128]{3,2,1,0:T(8,128)S(1)}, f32[3,2,64,128]{3,2,1,0:T(8,128)S(1)}, f32[3,2,64,128]{3,2,1,0:T(8,128)S(1)}, f32[3,2,64,128]{3,2,1,0:T(8,12...) custom-call(bf16[48,512]{1,0:T(8,128)(2,1)S(1)} %reshape.34.table_re, ...), custom_call_target="tpu_custom_call" | custom-call | bytes 72000000 | tf_op jit(solution)/shard_map/first/pallas_call | solution.py:111
  71.0 27.3 %first.11 = (f32[3,4,64,128]{3,2,1,0:T(8,128)S(1)}, f32[3,4,64,128]{3,2,1,0:T(8,128)S(1)}, f32[3,4,64,128]{3,2,1,0:T(8,128)S(1)}, f32[3,4,64,128]{3,2,1,0:T(8,12...) custom-call(bf16[96,512]{1,0:T(8,128)(2,1)S(1)} %reshape.39.table_re, ...), custom_call_target="tpu_custom_call" | custom-call | bytes 78000000 | tf_op jit(solution)/shard_map/first/pallas_call | solution.py:111
  117.9 18.4 %collective-permute-done.11.rest_5_ = f32[3,4,64,128]{3,2,1,0:T(8,128)S(1)} collective-permute-done((f32[3,4,64,128]{3,2,1,0:T(8,128)S(1)}, f32[3,4,64,128]{3,2,1,0:T(8,128)S(1)}, u32[]{:S(2)}, u32[]{:S(2)}) %collective-permute-start.11) | collective-permute-done | bytes 393248 | tf_op jit(solution)/shard_map/ppermute | solution.py:329
  151.5 29.3 %first.16 = (f32[3,8,64,128]{3,2,1,0:T(8,128)S(1)}, f32[3,8,64,128]{3,2,1,0:T(8,128)S(1)}, f32[3,8,64,128]{3,2,1,0:T(8,128)S(1)}, f32[3,8,64,128]{3,2,1,0:T(8,12...) custom-call(bf16[192,512]{1,0:T(8,128)(2,1)S(1)} %bitcast.15, ...), custom_call_target="tpu_custom_call" | custom-call | bytes 90000000 | tf_op jit(solution)/shard_map/first/pallas_call | solution.py:111
  217.2 35.3 %collective-permute-done.46.rest_5_ = f32[3,8,64,128]{3,2,1,0:T(8,128)S(1)} collective-permute-done((f32[3,8,64,128]{3,2,1,0:T(8,128)S(1)}, f32[3,8,64,128]{3,2,1,0:T(8,128)S(1)}, u32[]{:S(2)}, u32[]{:S(2)}) %collective-permute-start.46) | collective-permute-done | bytes 786464 | tf_op jit(solution)/shard_map/ppermute | solution.py:329
  253.4 15.5 %second.16.rest_0_ = f32[4,3,8,128,128]{4,3,2,1,0:T(8,128)} custom-call(s32[8]{0:T(128)S(1)} %stack.26.sources_ref, bf16[512,3072]{1,0:T(8,128)(2,1)} %constant.30.clone.table_ref, f32[3,8,64,128]{3,2,1,0:T(8,128)S(1)} %get-tuple-element.186.rest_0_, f32[3,8,64,128]{3,2,1,0:T(8,128)S(1)} %collective-permute-done.42.rest_1_, ...), custom_call_target="tpu_custom_call" | custom-call | bytes 51000000 | tf_op jit(solution)/shard_map/second/pallas_call | solution.py:153
  278.3 30.4 %first.12 = (f32[3,10,64,128]{3,2,1,0:T(8,128)S(1)}, f32[3,10,64,128]{3,2,1,0:T(8,128)S(1)}, f32[3,10,64,128]{3,2,1,0:T(8,128)S(1)}, f32[3,10,64,128]{3,2,1,0:T(...) custom-call(bf16[240,512]{1,0:T(8,128)(2,1)S(1)} %reshape.38.table_r, ...), custom_call_target="tpu_custom_call" | custom-call | bytes 96000000 | tf_op jit(solution)/shard_map/first/pallas_call | solution.py:111
  315.1 18.6 %collective-permute-done.15.rest_2_ = f32[3,10,64,128]{3,2,1,0:T(8,128)S(1)} collective-permute-done((f32[3,10,64,128]{3,2,1,0:T(8,128)S(1)}, f32[3,10,64,128]{3,2,1,0:T(8,128)S(1)}, u32[]{:S(2)}, u32[]{:S(2)}) %collective-permute-start.15) | collective-permute-done | bytes 983072 | tf_op jit(solution)/shard_map/ppermute | solution.py:329
  353.8 44.0 %collective-permute-done.18.rest_5_ = f32[3,10,64,128]{3,2,1,0:T(8,128)S(1)} collective-permute-done((f32[3,10,64,128]{3,2,1,0:T(8,128)S(1)}, f32[3,10,64,128]{3,2,1,0:T(8,128)S(1)}, u32[]{:S(2)}, u32[]{:S(2)}) %collective-permute-start.18) | collective-permute-done | bytes 983072 | tf_op jit(solution)/shard_map/ppermute | solution.py:329
  399.0 18.9 %second.12.rest_0_ = f32[4,3,10,128,128]{4,3,2,1,0:T(8,128)} custom-call(s32[8]{0:T(128)S(1)} %stack.26.sources_ref, bf16[512,3072]{1,0:T(8,128)(2,1)} %constant.30.clone.table_ref, f32[3,10,64,128]{3,2,1,0:T(8,128)S(1)} %get-tuple-element.147.rest_0_, f32[3,10,64,128]{3,2,1,0:T(8,128)S(1)} %collective-permute-done.14.rest_1_, ...), custom_call_target="tpu_custom_call" | custom-call | bytes 63000000 | tf_op jit(solution)/shard_map/second/pallas_call | solution.py:153
  423.6 29.2 %first.17 = (f32[3,8,64,128]{3,2,1,0:T(8,128)S(1)}, f32[3,8,64,128]{3,2,1,0:T(8,128)S(1)}, f32[3,8,64,128]{3,2,1,0:T(8,128)S(1)}, f32[3,8,64,128]{3,2,1,0:T(8,12...) custom-call(bf16[192,512]{1,0:T(8,128)(2,1)S(1)} %bitcast.14, ...), custom_call_target="tpu_custom_call" | custom-call | bytes 90000000 | tf_op jit(solution)/shard_map/first/pallas_call | solution.py:111
  490.3 34.9 %collective-permute-done.53.rest_5_ = f32[3,8,64,128]{3,2,1,0:T(8,128)S(1)} collective-permute-done((f32[3,8,64,128]{3,2,1,0:T(8,128)S(1)}, f32[3,8,64,128]{3,2,1,0:T(8,128)S(1)}, u32[]{:S(2)}, u32[]{:S(2)}) %collective-permute-start.53) | collective-permute-done | bytes 786464 | tf_op jit(solution)/shard_map/ppermute | solution.py:329
  526.2 15.5 %second.17.rest_0_ = f32[4,3,8,128,128]{4,3,2,1,0:T(8,128)} custom-call(s32[8]{0:T(128)S(1)} %stack.26.sources_ref, bf16[512,3072]{1,0:T(8,128)(2,1)} %constant.30.clone.table_ref, f32[3,8,64,128]{3,2,1,0:T(8,128)S(1)} %get-tuple-element.196.rest_0_, f32[3,8,64,128]{3,2,1,0:T(8,128)S(1)} %collective-permute-done.49.rest_1_, ...), custom_call_target="tpu_custom_call" | custom-call | bytes 51000000 | tf_op jit(solution)/shard_map/second/pallas_call | solution.py:153
  541.7 54.8 %all-to-all-done.2.in_ref = f32[4,3,10,128,128]{4,3,2,1,0:T(8,128)} async-done(((f32[4,3,10,128,128]{4,3,2,1,0:T(8,128)}), f32[4,3,10,128,128]{4,3,2,1,0:T(8,128)}, u32[]{:S(2)}, u32[]{:S(2)}) %all-to-all-start.2) | async-done | bytes 7864352 | tf_op jit(solution)/shard_map/all_to_all | solution.py:380
  601.9 29.2 %first.13 = (f32[3,8,64,128]{3,2,1,0:T(8,128)S(1)}, f32[3,8,64,128]{3,2,1,0:T(8,128)S(1)}, f32[3,8,64,128]{3,2,1,0:T(8,128)S(1)}, f32[3,8,64,128]{3,2,1,0:T(8,12...) custom-call(bf16[192,512]{1,0:T(8,128)(2,1)S(1)} %bitcast.13, ...), custom_call_target="tpu_custom_call" | custom-call | bytes 90000000 | tf_op jit(solution)/shard_map/first/pallas_call | solution.py:111
  653.0 16.8 %third.12 = (f32[10,128,512]{2,1,0:T(8,128)S(1)}, f32[10,1,512]{2,1,0:T(1,128)S(1)}, f32[10,1,512]{2,1,0:T(1,128)S(1)}) custom-call(bf16[3072,512]{1,0:T(8,128)(2,1)S(1)} %copy-done, f32[4,3,10,128,128]{4,3,2,1,0:T(8,128)} %all-to-all-done.2.in_ref), custom_call_target="tpu_custom_call" | custom-call | bytes 63000000 | tf_op jit(solution)/shard_map/third/pallas_call | solution.py:208
  671.3 31.0 %collective-permute-done.25.rest_5_ = f32[3,8,64,128]{3,2,1,0:T(8,128)S(1)} collective-permute-done((f32[3,8,64,128]{3,2,1,0:T(8,128)S(1)}, f32[3,8,64,128]{3,2,1,0:T(8,128)S(1)}, u32[]{:S(2)}, u32[]{:S(2)}) %collective-permute-start.25) | collective-permute-done | bytes 786464 | tf_op jit(solution)/shard_map/ppermute | solution.py:329
  703.2 15.5 %second.13.rest_0_ = f32[4,3,8,128,128]{4,3,2,1,0:T(8,128)} custom-call(s32[8]{0:T(128)S(1)} %stack.26.sources_ref, bf16[512,3072]{1,0:T(8,128)(2,1)} %constant.30.clone.table_ref, f32[3,8,64,128]{3,2,1,0:T(8,128)S(1)} %get-tuple-element.156.rest_0_, f32[3,8,64,128]{3,2,1,0:T(8,128)S(1)} %collective-permute-done.21.rest_1_, ...), custom_call_target="tpu_custom_call" | custom-call | bytes 51000000 | tf_op jit(solution)/shard_map/second/pallas_call | solution.py:153
  718.7 21.5 %all-to-all-done.7.in_ref = f32[4,3,8,128,128]{4,3,2,1,0:T(8,128)} async-done(((f32[4,3,8,128,128]{4,3,2,1,0:T(8,128)}), f32[4,3,8,128,128]{4,3,2,1,0:T(8,128)}, u32[]{:S(2)}, u32[]{:S(2)}) %all-to-all-start.7) | async-done | bytes 6291488 | tf_op jit(solution)/shard_map/all_to_all | solution.py:380
  746.5 30.3 %first.18 = (f32[3,10,64,128]{3,2,1,0:T(8,128)S(1)}, f32[3,10,64,128]{3,2,1,0:T(8,128)S(1)}, f32[3,10,64,128]{3,2,1,0:T(8,128)S(1)}, f32[3,10,64,128]{3,2,1,0:T(...) custom-call(bf16[240,512]{1,0:T(8,128)(2,1)S(1)} %reshape.43.table_r, ...), custom_call_target="tpu_custom_call" | custom-call | bytes 96000000 | tf_op jit(solution)/shard_map/first/pallas_call | solution.py:111
  782.9 18.4 %collective-permute-done.59.rest_2_ = f32[3,10,64,128]{3,2,1,0:T(8,128)S(1)} collective-permute-done((f32[3,10,64,128]{3,2,1,0:T(8,128)S(1)}, f32[3,10,64,128]{3,2,1,0:T(8,128)S(1)}, u32[]{:S(2)}, u32[]{:S(2)}) %collective-permute-start.59) | collective-permute-done | bytes 983072 | tf_op jit(solution)/shard_map/ppermute | solution.py:329
  821.6 43.2 %collective-permute-done.62.rest_5_ = f32[3,10,64,128]{3,2,1,0:T(8,128)S(1)} collective-permute-done((f32[3,10,64,128]{3,2,1,0:T(8,128)S(1)}, f32[3,10,64,128]{3,2,1,0:T(8,128)S(1)}, u32[]{:S(2)}, u32[]{:S(2)}) %collective-permute-start.62) | collective-permute-done | bytes 983072 | tf_op jit(solution)/shard_map/ppermute | solution.py:329
  865.8 18.9 %second.18.rest_0_ = f32[4,3,10,128,128]{4,3,2,1,0:T(8,128)} custom-call(s32[8]{0:T(128)S(1)} %stack.26.sources_ref, bf16[512,3072]{1,0:T(8,128)(2,1)} %constant.30.clone.table_ref, f32[3,10,64,128]{3,2,1,0:T(8,128)S(1)} %get-tuple-element.211.rest_0_, f32[3,10,64,128]{3,2,1,0:T(8,128)S(1)} %collective-permute-done.58.rest_1_, ...), custom_call_target="tpu_custom_call" | custom-call | bytes 63000000 | tf_op jit(solution)/shard_map/second/pallas_call | solution.py:153
  890.4 29.2 %first.14 = (f32[3,8,64,128]{3,2,1,0:T(8,128)S(1)}, f32[3,8,64,128]{3,2,1,0:T(8,128)S(1)}, f32[3,8,64,128]{3,2,1,0:T(8,128)S(1)}, f32[3,8,64,128]{3,2,1,0:T(8,12...) custom-call(bf16[192,512]{1,0:T(8,128)(2,1)S(1)} %bitcast.12, ...), custom_call_target="tpu_custom_call" | custom-call | bytes 90000000 | tf_op jit(solution)/shard_map/first/pallas_call | solution.py:111
  957.1 35.6 %collective-permute-done.32.rest_5_ = f32[3,8,64,128]{3,2,1,0:T(8,128)S(1)} collective-permute-done((f32[3,8,64,128]{3,2,1,0:T(8,128)S(1)}, f32[3,8,64,128]{3,2,1,0:T(8,128)S(1)}, u32[]{:S(2)}, u32[]{:S(2)}) %collective-permute-start.32) | collective-permute-done | bytes 786464 | tf_op jit(solution)/shard_map/ppermute | solution.py:329
  993.5 15.5 %second.14.rest_0_ = f32[4,3,8,128,128]{4,3,2,1,0:T(8,128)} custom-call(s32[8]{0:T(128)S(1)} %stack.26.sources_ref, bf16[512,3072]{1,0:T(8,128)(2,1)} %constant.30.clone.table_ref, f32[3,8,64,128]{3,2,1,0:T(8,128)S(1)} %get-tuple-element.165.rest_0_, f32[3,8,64,128]{3,2,1,0:T(8,128)S(1)} %collective-permute-done.28.rest_1_, ...), custom_call_target="tpu_custom_call" | custom-call | bytes 51000000 | tf_op jit(solution)/shard_map/second/pallas_call | solution.py:153
  1009.1 54.4 %all-to-all-done.8.in_ref = f32[4,3,10,128,128]{4,3,2,1,0:T(8,128)} async-done(((f32[4,3,10,128,128]{4,3,2,1,0:T(8,128)}), f32[4,3,10,128,128]{4,3,2,1,0:T(8,128)}, u32[]{:S(2)}, u32[]{:S(2)}) %all-to-all-start.8) | async-done | bytes 7864352 | tf_op jit(solution)/shard_map/all_to_all | solution.py:380
  1068.7 27.3 %first.19 = (f32[3,4,64,128]{3,2,1,0:T(8,128)S(1)}, f32[3,4,64,128]{3,2,1,0:T(8,128)S(1)}, f32[3,4,64,128]{3,2,1,0:T(8,128)S(1)}, f32[3,4,64,128]{3,2,1,0:T(8,12...) custom-call(bf16[96,512]{1,0:T(8,128)(2,1)S(1)} %reshape.42.table_re, ...), custom_call_target="tpu_custom_call" | custom-call | bytes 78000000 | tf_op jit(solution)/shard_map/first/pallas_call | solution.py:111
  1110.1 16.8 %third.18 = (f32[10,128,512]{2,1,0:T(8,128)S(1)}, f32[10,1,512]{2,1,0:T(1,128)S(1)}, f32[10,1,512]{2,1,0:T(1,128)S(1)}) custom-call(bf16[3072,512]{1,0:T(8,128)(2,1)S(1)} %copy-done, f32[4,3,10,128,128]{4,3,2,1,0:T(8,128)} %all-to-all-done.8.in_ref), custom_call_target="tpu_custom_call" | custom-call | bytes 63000000 | tf_op jit(solution)/shard_map/third/pallas_call | solution.py:208
  1144.6 62.8 %all-to-all-done.4.in_ref = f32[4,3,8,128,128]{4,3,2,1,0:T(8,128)} async-done(((f32[4,3,8,128,128]{4,3,2,1,0:T(8,128)}), f32[4,3,8,128,128]{4,3,2,1,0:T(8,128)}, u32[]{:S(2)}, u32[]{:S(2)}) %all-to-all-start.4) | async-done | bytes 6291488 | tf_op jit(solution)/shard_map/all_to_all | solution.py:380
  1212.3 26.3 %first.15 = (f32[3,2,64,128]{3,2,1,0:T(8,128)S(1)}, f32[3,2,64,128]{3,2,1,0:T(8,128)S(1)}, f32[3,2,64,128]{3,2,1,0:T(8,128)S(1)}, f32[3,2,64,128]{3,2,1,0:T(8,12...) custom-call(bf16[48,512]{1,0:T(8,128)(2,1)S(1)} %reshape.35.table_re, ...), custom_call_target="tpu_custom_call" | custom-call | bytes 72000000 | tf_op jit(solution)/shard_map/first/pallas_call | solution.py:111
  1297.5 16.5 %collective-permute-done.57 = f32[32,1,512]{2,1,0:T(1,128)S(1)} collective-permute-done((f32[32,1,512]{2,1,0:T(1,128)S(1)}, f32[32,1,512]{2,1,0:T(1,128)S(1)}, u32[]{:S(2)}, u32[]{:S(2)}) %collective-permute-start.57) | collective-permute-done | bytes 65568 | tf_op jit(solution)/shard_map/ppermute | solution.py:340
  (332 shorter events, 489.6 us)
Async XLA Ops:
  63.9 81.5 %all-to-all-start = ((f32[4,3,2,128,128]{4,3,2,1,0:T(8,128)}), f32[4,3,2,128,128]{4,3,2,1,0:T(8,128)}, u32[]{:S(2)}, u32[]{:S(2)}) async-start(f32[4,3,2,128,128]{4,3,2,1,0:T(8,128)} %second.10.rest_0_), calls=%async_computation | async-start | bytes 3145728 | tf_op jit(solution)/shard_map/all_to_all | solution.py:380
  145.4 124.4 %all-to-all-start.1 = ((f32[4,3,4,128,128]{4,3,2,1,0:T(8,128)}), f32[4,3,4,128,128]{4,3,2,1,0:T(8,128)}, u32[]{:S(2)}, u32[]{:S(2)}) async-start(f32[4,3,4,128,128]{4,3,2,1,0:T(8,128)} %second.11.rest_0_), calls=%async_computation.1 | async-start | bytes 6291456 | tf_op jit(solution)/shard_map/all_to_all | solution.py:380
  184.2 68.3 %collective-permute-start.46 = (f32[3,8,64,128]{3,2,1,0:T(8,128)S(1)}, f32[3,8,64,128]{3,2,1,0:T(8,128)S(1)}, u32[]{:S(2)}, u32[]{:S(2)}) collective-permute-start(f32[3,8,64,128]{3,2,1,0:T(8,128)S(1)} %get-tuple-element.191), channel_id=1, source_target_pairs={{0,20},{4,16},{8,28},{12,24},{16,4},{20,0},{24,12},{28,8},{1,21},{... | collective-permute-start | bytes 2359304 | tf_op jit(solution)/shard_map/ppermute | solution.py:329
  184.4 68.1 %collective-permute-start.47 = (f32[3,8,64,128]{3,2,1,0:T(8,128)S(1)}, f32[3,8,64,128]{3,2,1,0:T(8,128)S(1)}, u32[]{:S(2)}, u32[]{:S(2)}) collective-permute-start(f32[3,8,64,128]{3,2,1,0:T(8,128)S(1)} %get-tuple-element.192), channel_id=1, source_target_pairs={{0,24},{4,28},{8,16},{12,20},{16,8},{20,12},{24,0},{28,4},{1,25},{... | collective-permute-start | bytes 2359304 | tf_op jit(solution)/shard_map/ppermute | solution.py:329
  201.3 51.2 %collective-permute-start.48 = (f32[3,8,64,128]{3,2,1,0:T(8,128)}, f32[3,8,64,128]{3,2,1,0:T(8,128)S(1)}, u32[]{:S(2)}, u32[]{:S(2)}) collective-permute-start(f32[3,8,64,128]{3,2,1,0:T(8,128)} %get-tuple-element.193), channel_id=1, source_target_pairs={{0,28},{4,24},{8,20},{12,16},{16,12},{20,8},{24,4},{28,0},{1,29},{... | collective-permute-start | bytes 2359304 | tf_op jit(solution)/shard_map/ppermute | solution.py:329
  269.8 148.1 %all-to-all-start.6 = ((f32[4,3,8,128,128]{4,3,2,1,0:T(8,128)}), f32[4,3,8,128,128]{4,3,2,1,0:T(8,128)}, u32[]{:S(2)}, u32[]{:S(2)}) async-start(f32[4,3,8,128,128]{4,3,2,1,0:T(8,128)} %second.16.rest_0_), calls=%async_computation.6 | async-start | bytes 12582912 | tf_op jit(solution)/shard_map/all_to_all | solution.py:380
  310.6 43.2 %collective-permute-start.16 = (f32[3,10,64,128]{3,2,1,0:T(8,128)S(1)}, f32[3,10,64,128]{3,2,1,0:T(8,128)S(1)}, u32[]{:S(2)}, u32[]{:S(2)}) collective-permute-start(f32[3,10,64,128]{3,2,1,0:T(8,128)S(1)} %get-tuple-element.150), channel_id=1, source_target_pairs={{0,12},{4,8},{8,4},{12,0},{16,28},{20,24},{24,20},{28,16},{1,13},{... | collective-permute-start | bytes 2949128 | tf_op jit(solution)/shard_map/ppermute | solution.py:329
  312.1 85.6 %collective-permute-start.18 = (f32[3,10,64,128]{3,2,1,0:T(8,128)S(1)}, f32[3,10,64,128]{3,2,1,0:T(8,128)S(1)}, u32[]{:S(2)}, u32[]{:S(2)}) collective-permute-start(f32[3,10,64,128]{3,2,1,0:T(8,128)S(1)} %get-tuple-element.152), channel_id=1, source_target_pairs={{0,20},{4,16},{8,28},{12,24},{16,4},{20,0},{24,12},{28,8},{1,21},{... | collective-permute-start | bytes 2949128 | tf_op jit(solution)/shard_map/ppermute | solution.py:329
  312.5 85.2 %collective-permute-start.19 = (f32[3,10,64,128]{3,2,1,0:T(8,128)}, f32[3,10,64,128]{3,2,1,0:T(8,128)S(1)}, u32[]{:S(2)}, u32[]{:S(2)}) collective-permute-start(f32[3,10,64,128]{3,2,1,0:T(8,128)} %get-tuple-element.153), channel_id=1, source_target_pairs={{0,24},{4,28},{8,16},{12,20},{16,8},{20,12},{24,0},{28,4},{1,25},{... | collective-permute-start | bytes 2949128 | tf_op jit(solution)/shard_map/ppermute | solution.py:329
  333.7 64.1 %collective-permute-start.20 = (f32[3,10,64,128]{3,2,1,0:T(8,128)}, f32[3,10,64,128]{3,2,1,0:T(8,128)S(1)}, u32[]{:S(2)}, u32[]{:S(2)}) collective-permute-start(f32[3,10,64,128]{3,2,1,0:T(8,128)} %get-tuple-element.154), channel_id=1, source_target_pairs={{0,28},{4,24},{8,20},{12,16},{16,12},{20,8},{24,4},{28,0},{1,29},{... | collective-permute-start | bytes 2949128 | tf_op jit(solution)/shard_map/ppermute | solution.py:329
  417.9 178.5 %all-to-all-start.2 = ((f32[4,3,10,128,128]{4,3,2,1,0:T(8,128)}), f32[4,3,10,128,128]{4,3,2,1,0:T(8,128)}, u32[]{:S(2)}, u32[]{:S(2)}) async-start(f32[4,3,10,128,128]{4,3,2,1,0:T(8,128)} %second.12.rest_0_), calls=%async_computation.2 | async-start | bytes 15728640 | tf_op jit(solution)/shard_map/all_to_all | solution.py:380
  456.5 68.8 %collective-permute-start.53 = (f32[3,8,64,128]{3,2,1,0:T(8,128)S(1)}, f32[3,8,64,128]{3,2,1,0:T(8,128)S(1)}, u32[]{:S(2)}, u32[]{:S(2)}) collective-permute-start(f32[3,8,64,128]{3,2,1,0:T(8,128)S(1)} %get-tuple-element.201), channel_id=1, source_target_pairs={{0,20},{4,16},{8,28},{12,24},{16,4},{20,0},{24,12},{28,8},{1,21},{... | collective-permute-start | bytes 2359304 | tf_op jit(solution)/shard_map/ppermute | solution.py:329
  456.9 68.4 %collective-permute-start.54 = (f32[3,8,64,128]{3,2,1,0:T(8,128)S(1)}, f32[3,8,64,128]{3,2,1,0:T(8,128)S(1)}, u32[]{:S(2)}, u32[]{:S(2)}) collective-permute-start(f32[3,8,64,128]{3,2,1,0:T(8,128)S(1)} %get-tuple-element.202), channel_id=1, source_target_pairs={{0,24},{4,28},{8,16},{12,20},{16,8},{20,12},{24,0},{28,4},{1,25},{... | collective-permute-start | bytes 2359304 | tf_op jit(solution)/shard_map/ppermute | solution.py:329
  473.8 51.5 %collective-permute-start.55 = (f32[3,8,64,128]{3,2,1,0:T(8,128)}, f32[3,8,64,128]{3,2,1,0:T(8,128)S(1)}, u32[]{:S(2)}, u32[]{:S(2)}) collective-permute-start(f32[3,8,64,128]{3,2,1,0:T(8,128)} %get-tuple-element.203), channel_id=1, source_target_pairs={{0,28},{4,24},{8,20},{12,16},{16,12},{20,8},{24,4},{28,0},{1,29},{... | collective-permute-start | bytes 2359304 | tf_op jit(solution)/shard_map/ppermute | solution.py:329
  596.4 143.7 %all-to-all-start.7 = ((f32[4,3,8,128,128]{4,3,2,1,0:T(8,128)}), f32[4,3,8,128,128]{4,3,2,1,0:T(8,128)}, u32[]{:S(2)}, u32[]{:S(2)}) async-start(f32[4,3,8,128,128]{4,3,2,1,0:T(8,128)} %second.17.rest_0_), calls=%async_computation.7 | async-start | bytes 12582912 | tf_op jit(solution)/shard_map/all_to_all | solution.py:380
  634.5 67.8 %collective-permute-start.25 = (f32[3,8,64,128]{3,2,1,0:T(8,128)S(1)}, f32[3,8,64,128]{3,2,1,0:T(8,128)S(1)}, u32[]{:S(2)}, u32[]{:S(2)}) collective-permute-start(f32[3,8,64,128]{3,2,1,0:T(8,128)S(1)} %get-tuple-element.161), channel_id=1, source_target_pairs={{0,20},{4,16},{8,28},{12,24},{16,4},{20,0},{24,12},{28,8},{1,21},{... | collective-permute-start | bytes 2359304 | tf_op jit(solution)/shard_map/ppermute | solution.py:329
  634.6 67.7 %collective-permute-start.26 = (f32[3,8,64,128]{3,2,1,0:T(8,128)S(1)}, f32[3,8,64,128]{3,2,1,0:T(8,128)S(1)}, u32[]{:S(2)}, u32[]{:S(2)}) collective-permute-start(f32[3,8,64,128]{3,2,1,0:T(8,128)S(1)} %get-tuple-element.162), channel_id=1, source_target_pairs={{0,24},{4,28},{8,16},{12,20},{16,8},{20,12},{24,0},{28,4},{1,25},{... | collective-permute-start | bytes 2359304 | tf_op jit(solution)/shard_map/ppermute | solution.py:329
  651.5 50.9 %collective-permute-start.27 = (f32[3,8,64,128]{3,2,1,0:T(8,128)}, f32[3,8,64,128]{3,2,1,0:T(8,128)S(1)}, u32[]{:S(2)}, u32[]{:S(2)}) collective-permute-start(f32[3,8,64,128]{3,2,1,0:T(8,128)} %get-tuple-element.163), channel_id=1, source_target_pairs={{0,28},{4,24},{8,20},{12,16},{16,12},{20,8},{24,4},{28,0},{1,29},{... | collective-permute-start | bytes 2359304 | tf_op jit(solution)/shard_map/ppermute | solution.py:329
  740.2 144.5 %all-to-all-start.3 = ((f32[4,3,8,128,128]{4,3,2,1,0:T(8,128)}), f32[4,3,8,128,128]{4,3,2,1,0:T(8,128)}, u32[]{:S(2)}, u32[]{:S(2)}) async-start(f32[4,3,8,128,128]{4,3,2,1,0:T(8,128)} %second.13.rest_0_), calls=%async_computation.3 | async-start | bytes 12582912 | tf_op jit(solution)/shard_map/all_to_all | solution.py:380
  778.3 43.3 %collective-permute-start.60 = (f32[3,10,64,128]{3,2,1,0:T(8,128)S(1)}, f32[3,10,64,128]{3,2,1,0:T(8,128)S(1)}, u32[]{:S(2)}, u32[]{:S(2)}) collective-permute-start(f32[3,10,64,128]{3,2,1,0:T(8,128)S(1)} %get-tuple-element.214), channel_id=1, source_target_pairs={{0,12},{4,8},{8,4},{12,0},{16,28},{20,24},{24,20},{28,16},{1,13},{... | collective-permute-start | bytes 2949128 | tf_op jit(solution)/shard_map/ppermute | solution.py:329
  780.1 84.7 %collective-permute-start.62 = (f32[3,10,64,128]{3,2,1,0:T(8,128)S(1)}, f32[3,10,64,128]{3,2,1,0:T(8,128)S(1)}, u32[]{:S(2)}, u32[]{:S(2)}) collective-permute-start(f32[3,10,64,128]{3,2,1,0:T(8,128)S(1)} %get-tuple-element.216), channel_id=1, source_target_pairs={{0,20},{4,16},{8,28},{12,24},{16,4},{20,0},{24,12},{28,8},{1,21},{... | collective-permute-start | bytes 2949128 | tf_op jit(solution)/shard_map/ppermute | solution.py:329
  780.2 84.5 %collective-permute-start.63 = (f32[3,10,64,128]{3,2,1,0:T(8,128)}, f32[3,10,64,128]{3,2,1,0:T(8,128)S(1)}, u32[]{:S(2)}, u32[]{:S(2)}) collective-permute-start(f32[3,10,64,128]{3,2,1,0:T(8,128)} %get-tuple-element.217), channel_id=1, source_target_pairs={{0,24},{4,28},{8,16},{12,20},{16,8},{20,12},{24,0},{28,4},{1,25},{... | collective-permute-start | bytes 2949128 | tf_op jit(solution)/shard_map/ppermute | solution.py:329
  801.3 63.6 %collective-permute-start.64 = (f32[3,10,64,128]{3,2,1,0:T(8,128)}, f32[3,10,64,128]{3,2,1,0:T(8,128)}, u32[]{:S(2)}, u32[]{:S(2)}) collective-permute-start(f32[3,10,64,128]{3,2,1,0:T(8,128)} %get-tuple-element.218), channel_id=1, source_target_pairs={{0,28},{4,24},{8,20},{12,16},{16,12},{20,8},{24,4},{28,0},{1,29},{... | collective-permute-start | bytes 2949128 | tf_op jit(solution)/shard_map/ppermute | solution.py:329
  884.7 178.8 %all-to-all-start.8 = ((f32[4,3,10,128,128]{4,3,2,1,0:T(8,128)}), f32[4,3,10,128,128]{4,3,2,1,0:T(8,128)}, u32[]{:S(2)}, u32[]{:S(2)}) async-start(f32[4,3,10,128,128]{4,3,2,1,0:T(8,128)} %second.18.rest_0_), calls=%async_computation.8 | async-start | bytes 15728640 | tf_op jit(solution)/shard_map/all_to_all | solution.py:380
  924.1 68.6 %collective-permute-start.32 = (f32[3,8,64,128]{3,2,1,0:T(8,128)S(1)}, f32[3,8,64,128]{3,2,1,0:T(8,128)S(1)}, u32[]{:S(2)}, u32[]{:S(2)}) collective-permute-start(f32[3,8,64,128]{3,2,1,0:T(8,128)S(1)} %get-tuple-element.170), channel_id=1, source_target_pairs={{0,20},{4,16},{8,28},{12,24},{16,4},{20,0},{24,12},{28,8},{1,21},{... | collective-permute-start | bytes 2359304 | tf_op jit(solution)/shard_map/ppermute | solution.py:329
  924.3 68.4 %collective-permute-start.33 = (f32[3,8,64,128]{3,2,1,0:T(8,128)S(1)}, f32[3,8,64,128]{3,2,1,0:T(8,128)S(1)}, u32[]{:S(2)}, u32[]{:S(2)}) collective-permute-start(f32[3,8,64,128]{3,2,1,0:T(8,128)S(1)} %get-tuple-element.171), channel_id=1, source_target_pairs={{0,24},{4,28},{8,16},{12,20},{16,8},{20,12},{24,0},{28,4},{1,25},{... | collective-permute-start | bytes 2359304 | tf_op jit(solution)/shard_map/ppermute | solution.py:329
  941.2 51.5 %collective-permute-start.34 = (f32[3,8,64,128]{3,2,1,0:T(8,128)}, f32[3,8,64,128]{3,2,1,0:T(8,128)S(1)}, u32[]{:S(2)}, u32[]{:S(2)}) collective-permute-start(f32[3,8,64,128]{3,2,1,0:T(8,128)} %get-tuple-element.172), channel_id=1, source_target_pairs={{0,28},{4,24},{8,20},{12,16},{16,12},{20,8},{24,4},{28,0},{1,29},{... | collective-permute-start | bytes 2359304 | tf_op jit(solution)/shard_map/ppermute | solution.py:329
  1063.5 143.9 %all-to-all-start.4 = ((f32[4,3,8,128,128]{4,3,2,1,0:T(8,128)}), f32[4,3,8,128,128]{4,3,2,1,0:T(8,128)}, u32[]{:S(2)}, u32[]{:S(2)}) async-start(f32[4,3,8,128,128]{4,3,2,1,0:T(8,128)} %second.14.rest_0_), calls=%async_computation.4 | async-start | bytes 12582912 | tf_op jit(solution)/shard_map/all_to_all | solution.py:380
  1207.4 75.1 %all-to-all-start.9 = ((f32[4,3,4,128,128]{4,3,2,1,0:T(8,128)}), f32[4,3,4,128,128]{4,3,2,1,0:T(8,128)}, u32[]{:S(2)}, u32[]{:S(2)}) async-start(f32[4,3,4,128,128]{4,3,2,1,0:T(8,128)} %second.19), calls=%async_computation.9 | async-start | bytes 6291456 | tf_op jit(solution)/shard_map/all_to_all | solution.py:380
  1282.5 81.2 %all-to-all-start.5 = ((f32[4,3,2,128,128]{4,3,2,1,0:T(8,128)}), f32[4,3,2,128,128]{4,3,2,1,0:T(8,128)}, u32[]{:S(2)}, u32[]{:S(2)}) async-start(f32[4,3,2,128,128]{4,3,2,1,0:T(8,128)} %copy-done.25), calls=%async_computation.5 | async-start | bytes 3145728 | tf_op jit(solution)/shard_map/all_to_all | solution.py:380
  1288.7 84.0 %collective-permute-start.76 = (f32[1,128,512]{2,1,0:T(8,128)}, f32[1,128,512]{2,1,0:T(8,128)S(1)}, u32[]{:S(2)}, u32[]{:S(2)}) collective-permute-start(f32[1,128,512]{2,1,0:T(8,128)} %slice.108), channel_id=1, source_target_pairs={{0,4},{4,8},{8,12},{12,16},{16,20},{20,24},{24,28},{28,0},{1,5},{5... | collective-permute-start | bytes 786440 | tf_op jit(solution)/shard_map/ppermute | solution.py:348
  1295.0 44.0 %collective-permute-start.77 = (f32[1,128,512]{2,1,0:T(8,128)S(1)}, f32[1,128,512]{2,1,0:T(8,128)S(1)}, u32[]{:S(2)}, u32[]{:S(2)}) collective-permute-start(f32[1,128,512]{2,1,0:T(8,128)S(1)} %slice.111), channel_id=1, source_target_pairs={{0,28},{4,0},{8,4},{12,8},{16,12},{20,16},{24,20},{28,24},{1,29},{... | collective-permute-start | bytes 786440 | tf_op jit(solution)/shard_map/ppermute | solution.py:349
  (107 other events, 1654.7 us)

commit v2 on v1

--- a/solution.py
+++ b/solution.py
@@ -15,6 +15,8 @@
 VALUE_PARTS = (0, 0, 0, 1, 1, 2)
 VMEM_BYTES = 48 * 1024 * 1024
 SCALE = 1.0
+RISING = (2, 4, 6, 10)
+FALLING = (4, 12, 16)
 
 
 def fourier_table(length):
@@ -70,23 +72,23 @@
     return pltpu.CompilerParams(vmem_limit_bytes=VMEM_BYTES)
 
 
-def first_kernel(table_ref, x_ref, *rest, groups):
+def first_kernel(table_ref, x_ref, *rest, groups, chunk):
     outs = rest[-groups:]
     rows = table_ref.shape[0] // 3
     width = rows // groups
     tile, inner, length = x_ref.shape
     flat = [out.reshape(width * tile, inner) for out in outs]
 
-    @pl.loop(0, tile // 2)
-    def _(pair):
-        block = x_ref[pl.ds(2 * pair, 2)].reshape(2 * inner, length)
+    @pl.loop(0, tile // chunk)
+    def _(part):
+        block = x_ref[pl.ds(chunk * part, chunk)].reshape(chunk * inner, length)
         product = lax.dot_general(
             table_ref[...], block, (((1,), (1,)), ((), ())), preferred_element_type=jnp.float32
         )
         total = product[2 * rows :] + product[rows : 2 * rows] + product[:rows]
         for step in range(groups):
-            for j in range(2):
-                flat[step][pl.ds(2 * pair + j, width, stride=tile), :] = total[
+            for j in range(chunk):
+                flat[step][pl.ds(chunk * part + j, width, stride=tile), :] = total[
                     step * width : (step + 1) * width, j * inner : (j + 1) * inner
                 ]
 
@@ -99,27 +101,39 @@
 
 def first_transform(spectrum, table, ordered, blocks, first, width, after):
     members, span_b, span_q, length = spectrum.shape
-    groups = len(blocks)
-    out_shape = (members, width, span_b, span_q)
+    groups = ordered.shape[1]
     if span_q % 128 or span_b % 8:
         chosen = jnp.asarray(table).reshape(length, groups, -1)[:, :, first : first + width]
-        chosen = ordered_blocks(chosen, 1, blocks)
+        chosen = chosen if blocks is None else ordered_blocks(chosen, 1, blocks)
         outs = jnp.einsum("cbqk,ksx->scxbq", spectrum.astype(jnp.float32), chosen, precision=EXACT)
-        return [outs[step] for step in range(groups)]
-    operand = ordered[:, :, first : first + width].reshape(-1, length)
-    tile = 8
+        return outs if blocks is None else [outs[step] for step in range(groups)]
+    operand = jnp.asarray(ordered[:, :, first : first + width].reshape(-1, length))
+    tile = 16 if span_b % 16 == 0 else 8
+    chunk = 8
+    while chunk > 2 and operand.shape[0] * chunk * span_q > 2**18:
+        chunk //= 2
+    if blocks is None:
+        outs = 1
+        out_specs = pl.BlockSpec((groups, None, width, tile, span_q), lambda c, b: (0, c, 0, b, 0))
+        out_shape = jax.ShapeDtypeStruct((groups, members, width, span_b, span_q), jnp.float32)
+    else:
+        outs = groups
+        out_specs = [pl.BlockSpec((None, width, tile, span_q), lambda c, b: (c, 0, b, 0))] * groups
+        out_shape = [
+            jax.ShapeDtypeStruct((members, width, span_b, span_q), jnp.float32)
+        ] * groups
     return pl.pallas_call(
-        functools.partial(first_kernel, groups=groups),
+        functools.partial(first_kernel, groups=outs, chunk=chunk),
         grid=(members, span_b // tile),
         in_specs=[
             pl.BlockSpec(operand.shape, lambda c, b: (0, 0)),
             pl.BlockSpec((None, tile, span_q, length), lambda c, b: (c, b, 0, 0)),
         ]
         + [ANY] * len(after),
-        out_specs=[pl.BlockSpec((None, width, tile, span_q), lambda c, b: (c, 0, b, 0))] * groups,
-        out_shape=[jax.ShapeDtypeStruct(out_shape, jnp.float32)] * groups,
+        out_specs=out_specs,
+        out_shape=out_shape,
         compiler_params=params(),
-        cost_estimate=cost(22 + width),
+        cost_estimate=cost(12 + width),
         name="first",
     )(operand, spectrum, *after)
 
@@ -147,9 +161,18 @@
     if span_q % 128 or span_b % 8 or span_y % 8:
         chosen = ordered_blocks(jnp.asarray(table).reshape(count, span_b, length), 0, sources)
         chosen = chosen.reshape(count, span_b, groups, span_y)
-        return jnp.einsum("scabq,sbgy->gcayq", jnp.stack(pieces), chosen, precision=EXACT)
+        pieces = jnp.stack([pieces[step] for step in range(count)])
+        return jnp.einsum("scabq,sbgy->gcayq", pieces, chosen, precision=EXACT)
     tile = 2 if width % 2 == 0 else 1
     out_shape = (groups, members, width, span_y, span_q)
+    if isinstance(pieces, list):
+        in_specs = [pl.BlockSpec((None, tile, span_b, span_q), lambda c, a: (c, a, 0, 0))] * count
+    else:
+        in_specs = [
+            pl.BlockSpec((None, None, tile, span_b, span_q), lambda c, a, s=s: (s, c, a, 0, 0))
+            for s in range(count)
+        ]
+        pieces = [pieces] * count
     return pl.pallas_call(
         functools.partial(second_kernel, count=count),
         grid=(members, width // tile),
@@ -157,7 +180,7 @@
             pl.BlockSpec(memory_space=pltpu.SMEM),
             pl.BlockSpec(stacked.shape, lambda c, a: (0, 0)),
         ]
-        + [pl.BlockSpec((None, tile, span_b, span_q), lambda c, a: (c, a, 0, 0))] * count
+        + in_specs
         + [ANY] * len(after),
         out_specs=pl.BlockSpec(
             (groups, None, tile, span_y, span_q), lambda c, a: (0, c, a, 0, 0)
@@ -230,7 +253,7 @@
 
 
 def normal_kernel(centre_ref, before_ref, behind_ref, low_ref, high_ref, *rest):
-    level_ref, normal_ref = rest[-2:]
+    level_ref, normal_ref, token_ref = rest[-3:]
     width, span_y, length = centre_ref.shape
     i = pl.program_id(0)
     centre = centre_ref[i]
@@ -245,6 +268,7 @@
     magnitude = jnp.sqrt(step_x * step_x + step_y * step_y + step_z * step_z)
     inverse = -1.0 / jnp.maximum(magnitude, 1.0)
     level_ref[0] = centre
+    token_ref[...] = jnp.zeros_like(token_ref)
     normal_ref[0, 0] = (step_x * inverse).astype(jnp.bfloat16)
     normal_ref[1, 0] = (step_y * inverse).astype(jnp.bfloat16)
     normal_ref[2, 0] = (step_z * inverse).astype(jnp.bfloat16)
@@ -269,10 +293,12 @@
         out_specs=[
             pl.BlockSpec((1, span_y, length), lambda i: (first + i, 0, 0)),
             pl.BlockSpec((3, 1, span_y, length), lambda i: (0, first + i, 0, 0)),
+            pl.BlockSpec((8, 128), lambda i: (0, 0)),
         ],
         out_shape=[
             jax.ShapeDtypeStruct((whole, span_y, length), jnp.float32),
             jax.ShapeDtypeStruct((3, whole, span_y, length), jnp.bfloat16),
+            jax.ShapeDtypeStruct((8, 128), jnp.float32),
         ],
         input_output_aliases={5 + k: k for k in range(len(held))},
         compiler_params=params(),
@@ -281,11 +307,10 @@
     )(centre, before, behind, low, high, *held)
 
 
-def slab_widths(half):
+def slab_widths(left, pattern):
     widths = []
-    left = half
     while left:
-        width = min(2 ** (1 + len(widths)), 10, left)
+        width = min(pattern[min(len(widths), len(pattern) - 1)], left)
         widths.append(width)
         left -= width
     return widths
@@ -308,14 +333,15 @@
     third_table = jnp.asarray(np.concatenate([parts[p] for p in TABLE_PARTS], axis=0))
 
     half = planes // 2
-    widths = slab_widths(planes - half) + slab_widths(half)[::-1]
+    rising = slab_widths(planes - half, RISING)
+    widths = rising + slab_widths(half, FALLING)[::-1]
     starts = []
     at = half
     for width in widths:
         starts.append(at % planes)
         at += width
     slabs = len(widths)
-    split = len(slab_widths(planes - half))
+    split = len(rising)
 
     me = lax.axis_index("row")
     targets = [partner(me, step, rows) for step in range(rows)]
@@ -358,9 +384,10 @@
             before = (halo["before"], 0)
         if slab == split - 1:
             behind = (halo["behind"], 0)
-        held = write_normals(
+        *held, token = write_normals(
             levels[slab], before, behind, low_halo[slab], high_halo[slab], starts[slab], planes, held
         )
+        return token
 
     def third(slab, after):
         levels[slab], lows[slab], highs[slab] = third_transform(
@@ -368,25 +395,41 @@
         )
 
     def second(slab, after):
-        return second_transform(pieces.pop(slab), table, second_table, sources, cols, after)
+        from_whom = sources if slab else [jnp.int32(step) for step in range(rows)]
+        return second_transform(pieces[slab], table, second_table, from_whom, cols, after)
 
     pieces, arrived = {}, {}
-    pieces[0] = first(0, ())
-    pieces[1] = first(1, (pieces[0][0],))
+    spectral = first_transform(spectrum, table, first_table, None, starts[0], widths[0], ())
+    pieces[0] = lax.all_to_all(spectral, "row", split_axis=0, concat_axis=0, tiled=True)
+    pieces[1] = first(1, (spectral,))
     for slab in range(slabs):
+        after = []
         if slab >= 2:
-            third(slab - 2, ())
-        spread = second(slab, (levels[slab - 2],) if slab >= 2 else ())
+            after.append(levels[slab - 2])
+        if slab + 1 < slabs:
+            after.append(pieces[slab + 1][0])
+        early = split - 1 <= slabs - 3
+        if slab == slabs - 1 and early:
+            exchange_rows(list(range(split)))
+            for done in range(1, split - 1):
+                after.append(normals(done))
+        spread = second(slab, after)
         arrived[slab] = lax.all_to_all(spread, "col", split_axis=0, concat_axis=0, tiled=True)
         if slab + 2 < slabs:
-            pieces[slab + 2] = first(slab + 2, (spread,))
-    third(slabs - 2, ())
-    third(slabs - 1, ())
+            pieces[slab + 2] = first(slab + 2, (pieces[slab + 1][rows - 1],))
+        if slab >= 1:
+            third(slab - 1, (pieces[slab + 2][0],) if slab + 2 < slabs else (spread,))
     exchange_planes()
-    exchange_rows(list(range(0, split)))
+    if not early:
+        exchange_rows(list(range(split)))
     exchange_rows(list(range(split, slabs - 1)))
+    after = [
+        normals(done)
+        for done in range(split - 1 if early else 1, slabs - 2)
+    ]
+    third(slabs - 1, after)
     exchange_rows([slabs - 1])
-    for slab in list(range(1, slabs)) + [0]:
+    for slab in list(range(slabs - 2, slabs)) + [0]:
         normals(slab)
     return tuple(held)
 

time: 1410 us -> 1330 us (0.943)
  Pallas kernels: 571 us -> 451 us
  starting transfers between devices: 149 us -> 166 us
    ppermute x70 -> x49, waiting for transfers between devices: 399 us -> 250 us  [first(): lax.ppermute(outs[step], 'row', pairs[step])]
    ppermute x3, waiting for transfers between devices: 18.1 us -> 159 us  [exchange_rows(): from_behind = lax.ppermute(low, 'col', ring('col', False))]
    pallas_call x10 -> x8, Pallas kernels: 285 us -> 155 us  [first_transform(): pl.pallas_call(functools.partial(first_kernel, groups=outs, chunk=chunk),...]
    all_to_all x10 -> x8, starting transfers between devices: 52.2 us -> 90.5 us  [body(): lax.all_to_all(spread, 'col', split_axis=0, concat_axis=0, tiled=True)]
    ppermute x70 -> x49, starting transfers between devices: 78.6 us -> 46.2 us  [first(): lax.ppermute(outs[step], 'row', pairs[step])]
    all_to_all x10 -> x8, waiting for transfers between devices: 206 us -> 219 us  [body(): lax.all_to_all(spread, 'col', split_axis=0, concat_axis=0, tiled=True)]
    unnamed x116 -> x198, local copies, waits for them, and re-layouts: 32.7 us -> 44.2 us
    pallas_call x10 -> x8, Pallas kernels: 111 us -> 120 us  [third_transform(): pl.pallas_call(third_kernel, grid=(width // tile, members), in_specs=[pl....]
  transfers between devices with their start and end apart: 88 -> 66, of which waited for: 34 -> 24; matrix products, arithmetic and copies ran while one was open for 1% -> 1% of each run, Pallas kernels for 38% -> 32%
where the time goes in v2:
time: 1330 us; the launch traced here: 1320 us
  waiting for transfers between devices  639 us (48%)
  Pallas kernels  451 us (34%)
  starting transfers between devices  166 us (12%)
  local copies, waits for them, and re-layouts  58.4 us (4%)
    ppermute x49, waiting for transfers between devices, first(): lax.ppermute(outs[step], 'row', pairs[step])  250 us
    all_to_all x8, waiting for transfers between devices, body(): lax.all_to_all(spread, 'col', split_axis=0, concat_axis=0, tiled=True)  219 us
    ppermute x3, waiting for transfers between devices, exchange_rows(): from_behind = lax.ppermute(low, 'col', ring('col', False))  159 us
    pallas_call x8, Pallas kernels, first_transform(): pl.pallas_call(functools.partial(first_kernel, groups=outs, chunk=chunk),...  155 us
    pallas_call x8, Pallas kernels, second_transform(): pl.pallas_call(functools.partial(second_kernel, count=count), grid=(membe...  129 us
    pallas_call x8, Pallas kernels, third_transform(): pl.pallas_call(third_kernel, grid=(width // tile, members), in_specs=[pl....  120 us
    all_to_all x8, starting transfers between devices, body(): lax.all_to_all(spread, 'col', split_axis=0, concat_axis=0, tiled=True)  90.5 us
    pallas_call x8, Pallas kernels, write_normals(): pl.pallas_call(normal_kernel, grid=(width,), in_specs=[pl.BlockSpec((widt...  47 us
  transfers between devices with their start and end apart: 66, of which 24 were waited for; matrix products, arithmetic and copies ran while one was open for 1% of the time, Pallas kernels for 32%

profile of v2, /device:TPU:0, one launch (start us, length us, event | category | flops | bytes accessed | tf_op | source)
XLA Modules:
  0.0 1315.8 jit_solution(4004866113676878265)
XLA Ops:
  1.4 17.3 %first.8.rest_0_ = f32[8,3,2,64,128]{4,3,2,1,0:T(8,128)} custom-call(bf16[48,512]{1,0:T(8,128)(2,1)S(1)} %copy-done.38, bf16[3,64,128,512]{3,2,1,0:T(8,128)(2,1)} %x_ref.15), custom_call_target="tpu_custom_call" | custom-call | bytes 42000000 | tf_op jit(solution)/shard_map/first/pallas_call | solution.py:125
  25.5 17.9 %first.9 = (f32[3,4,64,128]{3,2,1,0:T(8,128)S(1)}, f32[3,4,64,128]{3,2,1,0:T(8,128)S(1)}, f32[3,4,64,128]{3,2,1,0:T(8,128)}, f32[3,4,64,128]{3,2,1,0:T(8,128)}, ...) custom-call(bf16[96,512]{1,0:T(8,128)(2,1)S(1)} %reshape.25.table_re, ...), custom_call_target="tpu_custom_call" | custom-call | bytes 48000000 | tf_op jit(solution)/shard_map/first/pallas_call | solution.py:125
  71.1 17.6 %first.10 = (f32[3,6,64,128]{3,2,1,0:T(8,128)S(1)}, f32[3,6,64,128]{3,2,1,0:T(8,128)S(1)}, f32[3,6,64,128]{3,2,1,0:T(8,128)S(1)}, f32[3,6,64,128]{3,2,1,0:T(8,12...) custom-call(bf16[144,512]{1,0:T(8,128)(2,1)S(1)} %reshape.27.table_r, ...), custom_call_target="tpu_custom_call" | custom-call | bytes 54000000 | tf_op jit(solution)/shard_map/first/pallas_call | solution.py:125
  132.1 19.0 %first.11 = (f32[3,10,64,128]{3,2,1,0:T(8,128)S(1)}, f32[3,10,64,128]{3,2,1,0:T(8,128)S(1)}, f32[3,10,64,128]{3,2,1,0:T(8,128)}, f32[3,10,64,128]{3,2,1,0:T(8,12...) custom-call(bf16[240,512]{1,0:T(8,128)(2,1)S(1)} %reshape.26.table_r, ...), custom_call_target="tpu_custom_call" | custom-call | bytes 66000000 | tf_op jit(solution)/shard_map/first/pallas_call | solution.py:125
  163.7 12.9 second.12
  189.5 21.2 %collective-permute-done.2.rest_0_.rest_7_ = f32[3,10,64,128]{3,2,1,0:T(8,128)S(1)} collective-permute-done((f32[3,10,64,128]{3,2,1,0:T(8,128)}, f32[3,10,64,128]{3,2,1,0:T(8,128)S(1)}, u32[]{:S(2)}, u32[]{:S(2)}) %collective-permute-start.2) | collective-permute-done | bytes 983072 | tf_op jit(solution)/shard_map/ppermute | solution.py:355
  214.3 19.1 %first.12 = (f32[3,10,64,128]{3,2,1,0:T(8,128)S(1)}, f32[3,10,64,128]{3,2,1,0:T(8,128)S(1)}, f32[3,10,64,128]{3,2,1,0:T(8,128)S(1)}, f32[3,10,64,128]{3,2,1,0:T(...) custom-call(bf16[240,512]{1,0:T(8,128)(2,1)S(1)} %reshape.31.table_r, ...), custom_call_target="tpu_custom_call" | custom-call | bytes 66000000 | tf_op jit(solution)/shard_map/first/pallas_call | solution.py:125
  252.9 20.7 %collective-permute-done.24.rest_6_ = f32[3,10,64,128]{3,2,1,0:T(8,128)} collective-permute-done((f32[3,10,64,128]{3,2,1,0:T(8,128)}, f32[3,10,64,128]{3,2,1,0:T(8,128)}, u32[]{:S(2)}, u32[]{:S(2)}) %collective-permute-start.24) | collective-permute-done | bytes 983072 | tf_op jit(solution)/shard_map/ppermute | solution.py:355
  273.6 19.8 %second.10 = f32[4,3,10,128,128]{4,3,2,1,0:T(8,128)} custom-call(s32[8]{0:T(128)S(1)} %stack.26.sources_ref, bf16[512,3072]{1,0:T(8,128)(2,1)} %constant.33.clone.table_ref, f32[3,10,64,128]{3,2,1,0:T(8,128)S(1)} %copy-done.22, f32[3,10,64,128]{3,2,1,0:T(8,128)S(1)} %copy-done.32, f32[3,10,64,128]{3,2,1,0:T(8,128)} %collective-permute-done.20.rest_2_, ...), custom_call_target="tpu_custom_call" | custom-call | bytes 63000000 | tf_op jit(solution)/shard_map/second/pallas_call | solution.py:176
  303.6 20.5 %collective-permute-done.3.rest_0_.rest_7_ = f32[3,10,64,128]{3,2,1,0:T(8,128)S(1)} collective-permute-done((f32[3,10,64,128]{3,2,1,0:T(8,128)}, f32[3,10,64,128]{3,2,1,0:T(8,128)S(1)}, u32[]{:S(2)}, u32[]{:S(2)}) %collective-permute-start.3) | collective-permute-done | bytes 983072 | tf_op jit(solution)/shard_map/ppermute | solution.py:355
  328.2 24.7 %first.13 = (f32[3,16,64,128]{3,2,1,0:T(8,128)S(1)}, f32[3,16,64,128]{3,2,1,0:T(8,128)}, f32[3,16,64,128]{3,2,1,0:T(8,128)S(1)}, f32[3,16,64,128]{3,2,1,0:T(8,12...) custom-call(bf16[384,512]{1,0:T(8,128)(2,1)S(1)} %bitcast.9, ...), custom_call_target="tpu_custom_call" | custom-call | bytes 84000000 | tf_op jit(solution)/shard_map/first/pallas_call | solution.py:125
  367.5 20.2 %collective-permute-done.42.rest_6_ = f32[3,10,64,128]{3,2,1,0:T(8,128)S(1)} collective-permute-done((f32[3,10,64,128]{3,2,1,0:T(8,128)}, f32[3,10,64,128]{3,2,1,0:T(8,128)S(1)}, u32[]{:S(2)}, u32[]{:S(2)}) %collective-permute-start.42) | collective-permute-done | bytes 983072 | tf_op jit(solution)/shard_map/ppermute | solution.py:355
  388.7 18.9 %second.13 = f32[4,3,10,128,128]{4,3,2,1,0:T(8,128)} custom-call(s32[8]{0:T(128)S(1)} %stack.26.sources_ref, bf16[512,3072]{1,0:T(8,128)(2,1)} %constant.33.clone.table_ref, f32[3,10,64,128]{3,2,1,0:T(8,128)S(1)} %copy-done.20, f32[3,10,64,128]{3,2,1,0:T(8,128)S(1)} %collective-permute-done.37.rest_1_, ...), custom_call_target="tpu_custom_call" | custom-call | bytes 63000000 | tf_op jit(solution)/shard_map/second/pallas_call | solution.py:176
  407.6 64.1 %all-to-all-done.3.in_ref = f32[4,3,10,128,128]{4,3,2,1,0:T(8,128)} async-done(((f32[4,3,10,128,128]{4,3,2,1,0:T(8,128)}), f32[4,3,10,128,128]{4,3,2,1,0:T(8,128)}, u32[]{:S(2)}, u32[]{:S(2)}) %all-to-all-start.3) | async-done | bytes 7864352 | tf_op jit(solution)/shard_map/all_to_all | solution.py:417
  481.7 33.4 %collective-permute-done.4.rest_0_.rest_7_ = f32[3,16,64,128]{3,2,1,0:T(8,128)S(1)} collective-permute-done((f32[3,16,64,128]{3,2,1,0:T(8,128)}, f32[3,16,64,128]{3,2,1,0:T(8,128)S(1)}, u32[]{:S(2)}, u32[]{:S(2)}) %collective-permute-start.4) | collective-permute-done | bytes 1572896 | tf_op jit(solution)/shard_map/ppermute | solution.py:355
  520.4 22.7 %first.14 = (f32[3,12,64,128]{3,2,1,0:T(8,128)S(1)}, f32[3,12,64,128]{3,2,1,0:T(8,128)S(1)}, f32[3,12,64,128]{3,2,1,0:T(8,128)}, f32[3,12,64,128]{3,2,1,0:T(8,12...) custom-call(bf16[288,512]{1,0:T(8,128)(2,1)S(1)} %reshape.29.table_r, ...), custom_call_target="tpu_custom_call" | custom-call | bytes 72000000 | tf_op jit(solution)/shard_map/first/pallas_call | solution.py:125
  544.1 18.3 %third.10 = (f32[10,128,512]{2,1,0:T(8,128)S(1)}, f32[10,1,512]{2,1,0:T(1,128)S(1)}, f32[10,1,512]{2,1,0:T(1,128)S(1)}) custom-call(bf16[3072,512]{1,0:T(8,128)(2,1)} %constant.34.clone.table_ref, f32[4,3,10,128,128]{4,3,2,1,0:T(8,128)} %all-to-all-done.3.in_ref, f32[3,12,64,128]{3,2,1,0:T(8,128)S(1)} %get-tuple-element.142.rest_0_.rest_9_), custom_call_target="tpu_custom_call" | custom-call | bytes 63000000 | tf_op jit(solution)/shard_map/third/pallas_call | solution.py:231
  565.2 17.5 %collective-permute-done.15.rest_3_ = f32[3,16,64,128]{3,2,1,0:T(8,128)} collective-permute-done((f32[3,16,64,128]{3,2,1,0:T(8,128)}, f32[3,16,64,128]{3,2,1,0:T(8,128)}, u32[]{:S(2)}, u32[]{:S(2)}) %collective-permute-start.15) | collective-permute-done | bytes 1572896 | tf_op jit(solution)/shard_map/ppermute | solution.py:355
  582.7 33.1 %collective-permute-done.18.rest_6_ = f32[3,16,64,128]{3,2,1,0:T(8,128)} collective-permute-done((f32[3,16,64,128]{3,2,1,0:T(8,128)}, f32[3,16,64,128]{3,2,1,0:T(8,128)}, u32[]{:S(2)}, u32[]{:S(2)}) %collective-permute-start.18) | collective-permute-done | bytes 1572896 | tf_op jit(solution)/shard_map/ppermute | solution.py:355
  615.8 29.5 %second.11 = f32[4,3,16,128,128]{4,3,2,1,0:T(8,128)} custom-call(s32[8]{0:T(128)S(1)} %stack.26.sources_ref, bf16[512,3072]{1,0:T(8,128)(2,1)} %constant.33.clone.table_ref, f32[3,16,64,128]{3,2,1,0:T(8,128)S(1)} %copy-done.16, f32[3,16,64,128]{3,2,1,0:T(8,128)S(1)} %collective-permute-done.13.rest_1_, ...), custom_call_target="tpu_custom_call" | custom-call | bytes 99000000 | tf_op jit(solution)/shard_map/second/pallas_call | solution.py:176
  660.0 24.7 %collective-permute-done.5.rest_0_.rest_7_ = f32[3,12,64,128]{3,2,1,0:T(8,128)S(1)} collective-permute-done((f32[3,12,64,128]{3,2,1,0:T(8,128)S(1)}, f32[3,12,64,128]{3,2,1,0:T(8,128)S(1)}, u32[]{:S(2)}, u32[]{:S(2)}) %collective-permute-start.5) | collective-permute-done | bytes 1179680 | tf_op jit(solution)/shard_map/ppermute | solution.py:355
  691.1 17.1 %first.15 = (f32[3,4,64,128]{3,2,1,0:T(8,128)S(1)}, f32[3,4,64,128]{3,2,1,0:T(8,128)S(1)}, f32[3,4,64,128]{3,2,1,0:T(8,128)S(1)}, f32[3,4,64,128]{3,2,1,0:T(8,12...) custom-call(bf16[96,512]{1,0:T(8,128)(2,1)S(1)} %copy-done.35, ...), custom_call_target="tpu_custom_call" | custom-call | bytes 48000000 | tf_op jit(solution)/shard_map/first/pallas_call | solution.py:125
  713.5 17.3 %third.12 = (f32[10,128,512]{2,1,0:T(8,128)S(1)}, f32[10,1,512]{2,1,0:T(1,128)S(1)}, f32[10,1,512]{2,1,0:T(1,128)S(1)}) custom-call(bf16[3072,512]{1,0:T(8,128)(2,1)S(1)} %copy-done.1, f32[4,3,10,128,128]{4,3,2,1,0:T(8,128)} %all-to-all-done.6.in_ref, f32[3,4,64,128]{3,2,1,0:T(8,128)S(1)} %get-tuple-element.112.rest_0_.rest_9_), custom_call_target="tpu_custom_call" | custom-call | bytes 63000000 | tf_op jit(solution)/shard_map/third/pallas_call | solution.py:231
  735.4 23.9 %collective-permute-done.36.rest_6_ = f32[3,12,64,128]{3,2,1,0:T(8,128)} collective-permute-done((f32[3,12,64,128]{3,2,1,0:T(8,128)}, f32[3,12,64,128]{3,2,1,0:T(8,128)}, u32[]{:S(2)}, u32[]{:S(2)}) %collective-permute-start.36) | collective-permute-done | bytes 1179680 | tf_op jit(solution)/shard_map/ppermute | solution.py:355
  759.3 23.1 %second.14.rest_0_ = f32[4,3,12,128,128]{4,3,2,1,0:T(8,128)} custom-call(s32[8]{0:T(128)S(1)} %stack.26.sources_ref, bf16[512,3072]{1,0:T(8,128)(2,1)} %constant.33.clone.table_ref, f32[3,12,64,128]{3,2,1,0:T(8,128)S(1)} %copy-done.18, f32[3,12,64,128]{3,2,1,0:T(8,128)S(1)} %copy-done.30, f32[3,12,64,128]{3,2,1,0:T(8,128)} %collective-permute-done.32.rest_2_, ...), custom_call_target="tpu_custom_call" | custom-call | bytes 75000000 | tf_op jit(solution)/shard_map/second/pallas_call | solution.py:176
  782.4 145.6 %all-to-all-done.4.in_ref = f32[4,3,16,128,128]{4,3,2,1,0:T(8,128)} async-done(((f32[4,3,16,128,128]{4,3,2,1,0:T(8,128)}), f32[4,3,16,128,128]{4,3,2,1,0:T(8,128)}, u32[]{:S(2)}, u32[]{:S(2)}) %all-to-all-start.4) | async-done | bytes 12582944 | tf_op jit(solution)/shard_map/all_to_all | solution.py:417
  944.9 142.3 %collective-permute-done.50 = f32[32,1,512]{2,1,0:T(1,128)S(1)} collective-permute-done((f32[32,1,512]{2,1,0:T(1,128)S(1)}, f32[32,1,512]{2,1,0:T(1,128)S(1)}, u32[]{:S(2)}, u32[]{:S(2)}) %collective-permute-start.50) | collective-permute-done | bytes 65568 | tf_op jit(solution)/shard_map/ppermute | solution.py:366
  1115.3 28.9 %third.13 = (f32[16,128,512]{2,1,0:T(8,128)}, f32[16,1,512]{2,1,0:T(1,128)S(1)}, f32[16,1,512]{2,1,0:T(1,128)S(1)}) custom-call(bf16[3072,512]{1,0:T(8,128)(2,1)S(1)} %copy-done.1, f32[4,3,16,128,128]{4,3,2,1,0:T(8,128)} %all-to-all-done.4.in_ref, f32[4,3,12,128,128]{4,3,2,1,0:T(8,128)} %second.14.rest_0_), custom_call_target="tpu_custom_call" | custom-call | bytes 99000000 | tf_op jit(solution)/shard_map/third/pallas_call | solution.py:231
  1154.5 52.2 %all-to-all-start.7 = ((f32[4,3,4,128,128]{4,3,2,1,0:T(8,128)}), f32[4,3,4,128,128]{4,3,2,1,0:T(8,128)}, u32[]{:S(2)}, u32[]{:S(2)}) async-start(f32[4,3,4,128,128]{4,3,2,1,0:T(8,128)} %second.15.rest_0_), calls=%async_computation.7 | async-start | bytes 6291456 | tf_op jit(solution)/shard_map/all_to_all | solution.py:417
  1210.5 21.2 %third.14 = (f32[12,128,512]{2,1,0:T(8,128)S(1)}, f32[12,1,512]{2,1,0:T(1,128)S(1)}, f32[12,1,512]{2,1,0:T(1,128)S(1)}) custom-call(bf16[3072,512]{1,0:T(8,128)(2,1)} %constant.34.clone.table_ref, f32[4,3,12,128,128]{4,3,2,1,0:T(8,128)} %all-to-all-done.8.in_ref, f32[4,3,4,128,128]{4,3,2,1,0:T(8,128)} %second.15.rest_0_), custom_call_target="tpu_custom_call" | custom-call | bytes 75000000 | tf_op jit(solution)/shard_map/third/pallas_call | solution.py:231
  1242.4 17.2 %collective-permute-done.54 = f32[28,1,512]{2,1,0:T(1,128)S(1)} collective-permute-done((f32[28,1,512]{2,1,0:T(1,128)S(1)}, f32[28,1,512]{2,1,0:T(1,128)S(1)}, u32[]{:S(2)}, u32[]{:S(2)}) %collective-permute-start.54) | collective-permute-done | bytes 57376 | tf_op jit(solution)/shard_map/ppermute | solution.py:366
  1287.3 13.7 %collective-permute-start.55 = (f32[4,1,512]{2,1,0:T(1,128)S(1)}, f32[4,1,512]{2,1,0:T(1,128)S(1)}, u32[]{:S(2)}, u32[]{:S(2)}) collective-permute-start(f32[4,1,512]{2,1,0:T(1,128)S(1)} %get-tuple-element.194), channel_id=1, source_target_pairs={{0,1},{1,2},{2,3},{3,0},{4,5},{5,6},{6,7},{7,4},{8,9},{9,10},{10,1... | collective-permute-start | bytes 24584 | tf_op jit(solution)/shard_map/ppermute | solution.py:365
  (362 shorter events, 318.8 us)
Async XLA Ops:
  104.1 76.4 %all-to-all-start.2 = ((f32[4,3,4,128,128]{4,3,2,1,0:T(8,128)}), f32[4,3,4,128,128]{4,3,2,1,0:T(8,128)}, u32[]{:S(2)}, u32[]{:S(2)}) async-start(f32[4,3,4,128,128]{4,3,2,1,0:T(8,128)} %second.9), calls=%async_computation.2 | async-start | bytes 6291456 | tf_op jit(solution)/shard_map/all_to_all | solution.py:417
  180.5 112.9 %all-to-all-start.5 = ((f32[4,3,6,128,128]{4,3,2,1,0:T(8,128)}), f32[4,3,6,128,128]{4,3,2,1,0:T(8,128)}, u32[]{:S(2)}, u32[]{:S(2)}) async-start(f32[4,3,6,128,128]{4,3,2,1,0:T(8,128)} %second.12), calls=%async_computation.5 | async-start | bytes 9437184 | tf_op jit(solution)/shard_map/all_to_all | solution.py:417
  187.1 59.3 %collective-permute-start.20 = (f32[3,10,64,128]{3,2,1,0:T(8,128)}, f32[3,10,64,128]{3,2,1,0:T(8,128)}, u32[]{:S(2)}, u32[]{:S(2)}) collective-permute-start(f32[3,10,64,128]{3,2,1,0:T(8,128)} %get-tuple-element.128), channel_id=1, source_target_pairs={{0,8},{4,12},{8,0},{12,4},{16,24},{20,28},{24,16},{28,20},{1,9},{5... | collective-permute-start | bytes 2949128 | tf_op jit(solution)/shard_map/ppermute | solution.py:355
  188.5 64.4 %collective-permute-start.21 = (f32[3,10,64,128]{3,2,1,0:T(8,128)S(1)}, f32[3,10,64,128]{3,2,1,0:T(8,128)}, u32[]{:S(2)}, u32[]{:S(2)}) collective-permute-start(f32[3,10,64,128]{3,2,1,0:T(8,128)S(1)} %copy-done.58), channel_id=1, source_target_pairs={{0,12},{4,8},{8,4},{12,0},{16,28},{20,24},{24,20},{28,16},{1,13},{... | collective-permute-start | bytes 2949128 | tf_op jit(solution)/shard_map/ppermute | solution.py:355
  188.5 64.4 %collective-permute-start.22 = (f32[3,10,64,128]{3,2,1,0:T(8,128)S(1)}, f32[3,10,64,128]{3,2,1,0:T(8,128)}, u32[]{:S(2)}, u32[]{:S(2)}) collective-permute-start(f32[3,10,64,128]{3,2,1,0:T(8,128)S(1)} %copy-done.56), channel_id=1, source_target_pairs={{0,16},{4,20},{8,24},{12,28},{16,0},{20,4},{24,8},{28,12},{1,17},{... | collective-permute-start | bytes 2949128 | tf_op jit(solution)/shard_map/ppermute | solution.py:355
  212.5 61.0 %collective-permute-start.24 = (f32[3,10,64,128]{3,2,1,0:T(8,128)}, f32[3,10,64,128]{3,2,1,0:T(8,128)}, u32[]{:S(2)}, u32[]{:S(2)}) collective-permute-start(f32[3,10,64,128]{3,2,1,0:T(8,128)} %get-tuple-element.132), channel_id=1, source_target_pairs={{0,24},{4,28},{8,16},{12,20},{16,8},{20,12},{24,0},{28,4},{1,25},{... | collective-permute-start | bytes 2949128 | tf_op jit(solution)/shard_map/ppermute | solution.py:355
  293.4 178.3 %all-to-all-start.3 = ((f32[4,3,10,128,128]{4,3,2,1,0:T(8,128)}), f32[4,3,10,128,128]{4,3,2,1,0:T(8,128)}, u32[]{:S(2)}, u32[]{:S(2)}) async-start(f32[4,3,10,128,128]{4,3,2,1,0:T(8,128)} %second.10), calls=%async_computation.3 | async-start | bytes 15728640 | tf_op jit(solution)/shard_map/all_to_all | solution.py:417
  300.5 66.9 %collective-permute-start.38 = (f32[3,10,64,128]{3,2,1,0:T(8,128)S(1)}, f32[3,10,64,128]{3,2,1,0:T(8,128)S(1)}, u32[]{:S(2)}, u32[]{:S(2)}) collective-permute-start(f32[3,10,64,128]{3,2,1,0:T(8,128)S(1)} %copy-done.62), channel_id=1, source_target_pairs={{0,8},{4,12},{8,0},{12,4},{16,24},{20,28},{24,16},{28,20},{1,9},{5... | collective-permute-start | bytes 2949128 | tf_op jit(solution)/shard_map/ppermute | solution.py:355
  302.4 65.0 %collective-permute-start.39 = (f32[3,10,64,128]{3,2,1,0:T(8,128)S(1)}, f32[3,10,64,128]{3,2,1,0:T(8,128)S(1)}, u32[]{:S(2)}, u32[]{:S(2)}) collective-permute-start(f32[3,10,64,128]{3,2,1,0:T(8,128)S(1)} %copy-done.60), channel_id=1, source_target_pairs={{0,12},{4,8},{8,4},{12,0},{16,28},{20,24},{24,20},{28,16},{1,13},{... | collective-permute-start | bytes 2949128 | tf_op jit(solution)/shard_map/ppermute | solution.py:355
  302.4 65.0 %collective-permute-start.40 = (f32[3,10,64,128]{3,2,1,0:T(8,128)}, f32[3,10,64,128]{3,2,1,0:T(8,128)S(1)}, u32[]{:S(2)}, u32[]{:S(2)}) collective-permute-start(f32[3,10,64,128]{3,2,1,0:T(8,128)} %get-tuple-element.153), channel_id=1, source_target_pairs={{0,16},{4,20},{8,24},{12,28},{16,0},{20,4},{24,8},{28,12},{1,17},{... | collective-permute-start | bytes 2949128 | tf_op jit(solution)/shard_map/ppermute | solution.py:355
  326.2 61.5 %collective-permute-start.42 = (f32[3,10,64,128]{3,2,1,0:T(8,128)}, f32[3,10,64,128]{3,2,1,0:T(8,128)S(1)}, u32[]{:S(2)}, u32[]{:S(2)}) collective-permute-start(f32[3,10,64,128]{3,2,1,0:T(8,128)} %get-tuple-element.155), channel_id=1, source_target_pairs={{0,24},{4,28},{8,16},{12,20},{16,8},{20,12},{24,0},{28,4},{1,25},{... | collective-permute-start | bytes 2949128 | tf_op jit(solution)/shard_map/ppermute | solution.py:355
  471.7 177.4 %all-to-all-start.6 = ((f32[4,3,10,128,128]{4,3,2,1,0:T(8,128)}), f32[4,3,10,128,128]{4,3,2,1,0:T(8,128)}, u32[]{:S(2)}, u32[]{:S(2)}) async-start(f32[4,3,10,128,128]{4,3,2,1,0:T(8,128)} %second.13), calls=%async_computation.6 | async-start | bytes 15728640 | tf_op jit(solution)/shard_map/all_to_all | solution.py:417
  478.7 86.5 %collective-permute-start.14 = (f32[3,16,64,128]{3,2,1,0:T(8,128)}, f32[3,16,64,128]{3,2,1,0:T(8,128)S(1)}, u32[]{:S(2)}, u32[]{:S(2)}) collective-permute-start(f32[3,16,64,128]{3,2,1,0:T(8,128)} %copy-done.52), channel_id=1, source_target_pairs={{0,8},{4,12},{8,0},{12,4},{16,24},{20,28},{24,16},{28,20},{1,9},{5... | collective-permute-start | bytes 4718600 | tf_op jit(solution)/shard_map/ppermute | solution.py:355
  480.3 102.3 %collective-permute-start.15 = (f32[3,16,64,128]{3,2,1,0:T(8,128)}, f32[3,16,64,128]{3,2,1,0:T(8,128)}, u32[]{:S(2)}, u32[]{:S(2)}) collective-permute-start(f32[3,16,64,128]{3,2,1,0:T(8,128)} %get-tuple-element.123), channel_id=1, source_target_pairs={{0,12},{4,8},{8,4},{12,0},{16,28},{20,24},{24,20},{28,16},{1,13},{... | collective-permute-start | bytes 4718600 | tf_op jit(solution)/shard_map/ppermute | solution.py:355
  480.3 102.3 %collective-permute-start.16 = (f32[3,16,64,128]{3,2,1,0:T(8,128)}, f32[3,16,64,128]{3,2,1,0:T(8,128)}, u32[]{:S(2)}, u32[]{:S(2)}) collective-permute-start(f32[3,16,64,128]{3,2,1,0:T(8,128)} %get-tuple-element.124), channel_id=1, source_target_pairs={{0,16},{4,20},{8,24},{12,28},{16,0},{20,4},{24,8},{28,12},{1,17},{... | collective-permute-start | bytes 4718600 | tf_op jit(solution)/shard_map/ppermute | solution.py:355
  515.1 67.5 %collective-permute-start.17 = (f32[3,16,64,128]{3,2,1,0:T(8,128)}, f32[3,16,64,128]{3,2,1,0:T(8,128)}, u32[]{:S(2)}, u32[]{:S(2)}) collective-permute-start(f32[3,16,64,128]{3,2,1,0:T(8,128)} %get-tuple-element.125), channel_id=1, source_target_pairs={{0,20},{4,16},{8,28},{12,24},{16,4},{20,0},{24,12},{28,8},{1,21},{... | collective-permute-start | bytes 4718600 | tf_op jit(solution)/shard_map/ppermute | solution.py:355
  516.3 99.5 %collective-permute-start.18 = (f32[3,16,64,128]{3,2,1,0:T(8,128)}, f32[3,16,64,128]{3,2,1,0:T(8,128)}, u32[]{:S(2)}, u32[]{:S(2)}) collective-permute-start(f32[3,16,64,128]{3,2,1,0:T(8,128)} %get-tuple-element.126), channel_id=1, source_target_pairs={{0,24},{4,28},{8,16},{12,20},{16,8},{20,12},{24,0},{28,4},{1,25},{... | collective-permute-start | bytes 4718600 | tf_op jit(solution)/shard_map/ppermute | solution.py:355
  649.1 278.9 %all-to-all-start.4 = ((f32[4,3,16,128,128]{4,3,2,1,0:T(8,128)}), f32[4,3,16,128,128]{4,3,2,1,0:T(8,128)}, u32[]{:S(2)}, u32[]{:S(2)}) async-start(f32[4,3,16,128,128]{4,3,2,1,0:T(8,128)} %second.11), calls=%async_computation.4 | async-start | bytes 25165824 | tf_op jit(solution)/shard_map/all_to_all | solution.py:417
  657.1 76.4 %collective-permute-start.32 = (f32[3,12,64,128]{3,2,1,0:T(8,128)}, f32[3,12,64,128]{3,2,1,0:T(8,128)}, u32[]{:S(2)}, u32[]{:S(2)}) collective-permute-start(f32[3,12,64,128]{3,2,1,0:T(8,128)} %get-tuple-element.145), channel_id=1, source_target_pairs={{0,8},{4,12},{8,0},{12,4},{16,24},{20,28},{24,16},{28,20},{1,9},{5... | collective-permute-start | bytes 3538952 | tf_op jit(solution)/shard_map/ppermute | solution.py:355
  658.6 76.8 %collective-permute-start.33 = (f32[3,12,64,128]{3,2,1,0:T(8,128)}, f32[3,12,64,128]{3,2,1,0:T(8,128)}, u32[]{:S(2)}, u32[]{:S(2)}) collective-permute-start(f32[3,12,64,128]{3,2,1,0:T(8,128)} %get-tuple-element.146), channel_id=1, source_target_pairs={{0,12},{4,8},{8,4},{12,0},{16,28},{20,24},{24,20},{28,16},{1,13},{... | collective-permute-start | bytes 3538952 | tf_op jit(solution)/shard_map/ppermute | solution.py:355
  658.6 76.8 %collective-permute-start.34 = (f32[3,12,64,128]{3,2,1,0:T(8,128)}, f32[3,12,64,128]{3,2,1,0:T(8,128)}, u32[]{:S(2)}, u32[]{:S(2)}) collective-permute-start(f32[3,12,64,128]{3,2,1,0:T(8,128)} %get-tuple-element.147), channel_id=1, source_target_pairs={{0,16},{4,20},{8,24},{12,28},{16,0},{20,4},{24,8},{28,12},{1,17},{... | collective-permute-start | bytes 3538952 | tf_op jit(solution)/shard_map/ppermute | solution.py:355
  686.8 72.4 %collective-permute-start.36 = (f32[3,12,64,128]{3,2,1,0:T(8,128)}, f32[3,12,64,128]{3,2,1,0:T(8,128)}, u32[]{:S(2)}, u32[]{:S(2)}) collective-permute-start(f32[3,12,64,128]{3,2,1,0:T(8,128)} %get-tuple-element.149), channel_id=1, source_target_pairs={{0,24},{4,28},{8,16},{12,20},{16,8},{20,12},{24,0},{28,4},{1,25},{... | collective-permute-start | bytes 3538952 | tf_op jit(solution)/shard_map/ppermute | solution.py:355
  928.0 226.5 %all-to-all-start.8 = ((f32[4,3,12,128,128]{4,3,2,1,0:T(8,128)}), f32[4,3,12,128,128]{4,3,2,1,0:T(8,128)}, u32[]{:S(2)}, u32[]{:S(2)}) async-start(f32[4,3,12,128,128]{4,3,2,1,0:T(8,128)} %second.14.rest_0_), calls=%async_computation.8 | async-start | bytes 18874368 | tf_op jit(solution)/shard_map/all_to_all | solution.py:417
  935.9 166.9 %collective-permute-start.6 = (f32[3,4,64,128]{3,2,1,0:T(8,128)}, f32[3,4,64,128]{3,2,1,0:T(8,128)S(1)}, u32[]{:S(2)}, u32[]{:S(2)}) collective-permute-start(f32[3,4,64,128]{3,2,1,0:T(8,128)} %copy-done.81), channel_id=1, source_target_pairs={{0,4},{4,0},{8,12},{12,8},{16,20},{20,16},{24,28},{28,24},{1,5},{5... | collective-permute-start | bytes 1179656 | tf_op jit(solution)/shard_map/ppermute | solution.py:355
  935.9 168.4 %collective-permute-start.7 = (f32[3,4,64,128]{3,2,1,0:T(8,128)}, f32[3,4,64,128]{3,2,1,0:T(8,128)S(1)}, u32[]{:S(2)}, u32[]{:S(2)}) collective-permute-start(f32[3,4,64,128]{3,2,1,0:T(8,128)} %copy-done.80), channel_id=1, source_target_pairs={{0,8},{4,12},{8,0},{12,4},{16,24},{20,28},{24,16},{28,20},{1,9},{5... | collective-permute-start | bytes 1179656 | tf_op jit(solution)/shard_map/ppermute | solution.py:355
  940.3 146.9 %collective-permute-start.50 = (f32[32,1,512]{2,1,0:T(1,128)S(1)}, f32[32,1,512]{2,1,0:T(1,128)S(1)}, u32[]{:S(2)}, u32[]{:S(2)}) collective-permute-start(f32[32,1,512]{2,1,0:T(1,128)S(1)} %constant_dynamic-update-slice_fusion.5), channel_id=1, source_target_pairs={{0,3},{1,0},{2,1},{3,2},{4,7},{5,4},{6,5},{7,6},{8,11},{9,8},{10,9... | collective-permute-start | bytes 196616 | tf_op jit(solution)/shard_map/ppermute | solution.py:366
  944.9 147.2 %collective-permute-start.49 = (f32[32,1,512]{2,1,0:T(1,128)S(1)}, f32[32,1,512]{2,1,0:T(1,128)S(1)}, u32[]{:S(2)}, u32[]{:S(2)}) collective-permute-start(f32[32,1,512]{2,1,0:T(1,128)S(1)} %constant_dynamic-update-slice_fusion), channel_id=1, source_target_pairs={{0,1},{1,2},{2,3},{3,0},{4,5},{5,6},{6,7},{7,4},{8,9},{9,10},{10,1... | collective-permute-start | bytes 196616 | tf_op jit(solution)/shard_map/ppermute | solution.py:365
  944.9 200.5 %collective-permute-start.8 = (f32[3,4,64,128]{3,2,1,0:T(8,128)}, f32[3,4,64,128]{3,2,1,0:T(8,128)S(1)}, u32[]{:S(2)}, u32[]{:S(2)}) collective-permute-start(f32[3,4,64,128]{3,2,1,0:T(8,128)} %copy-done.79), channel_id=1, source_target_pairs={{0,12},{4,8},{8,4},{12,0},{16,28},{20,24},{24,20},{28,16},{1,13},{... | collective-permute-start | bytes 1179656 | tf_op jit(solution)/shard_map/ppermute | solution.py:355
  1087.2 58.2 %collective-permute-start.9 = (f32[3,4,64,128]{3,2,1,0:T(8,128)}, f32[3,4,64,128]{3,2,1,0:T(8,128)S(1)}, u32[]{:S(2)}, u32[]{:S(2)}) collective-permute-start(f32[3,4,64,128]{3,2,1,0:T(8,128)} %copy-done.78), channel_id=1, source_target_pairs={{0,16},{4,20},{8,24},{12,28},{16,0},{20,4},{24,8},{28,12},{1,17},{... | collective-permute-start | bytes 1179656 | tf_op jit(solution)/shard_map/ppermute | solution.py:355
  1092.1 53.3 %collective-permute-start.10 = (f32[3,4,64,128]{3,2,1,0:T(8,128)}, f32[3,4,64,128]{3,2,1,0:T(8,128)S(1)}, u32[]{:S(2)}, u32[]{:S(2)}) collective-permute-start(f32[3,4,64,128]{3,2,1,0:T(8,128)} %copy-done.77), channel_id=1, source_target_pairs={{0,20},{4,16},{8,28},{12,24},{16,4},{20,0},{24,12},{28,8},{1,21},{... | collective-permute-start | bytes 1179656 | tf_op jit(solution)/shard_map/ppermute | solution.py:355
  1154.5 125.1 %all-to-all-start.7 = ((f32[4,3,4,128,128]{4,3,2,1,0:T(8,128)}), f32[4,3,4,128,128]{4,3,2,1,0:T(8,128)}, u32[]{:S(2)}, u32[]{:S(2)}) async-start(f32[4,3,4,128,128]{4,3,2,1,0:T(8,128)} %second.15.rest_0_), calls=%async_computation.7 | async-start | bytes 6291456 | tf_op jit(solution)/shard_map/all_to_all | solution.py:417
  1206.8 57.6 %collective-permute-start.52 = (f32[1,128,512]{2,1,0:T(8,128)S(1)}, f32[1,128,512]{2,1,0:T(8,128)S(1)}, u32[]{:S(2)}, u32[]{:S(2)}) collective-permute-start(f32[1,128,512]{2,1,0:T(8,128)S(1)} %slice.85), channel_id=1, source_target_pairs={{0,4},{4,8},{8,12},{12,16},{16,20},{20,24},{24,28},{28,0},{1,5},{5... | collective-permute-start | bytes 786440 | tf_op jit(solution)/shard_map/ppermute | solution.py:374
  (126 other events, 2114.2 us)

commit v3 on v2

v3 whole, which is shorter than its diff:
```python
import functools
import math

import jax
import jax.numpy as jnp
import ml_dtypes
import numpy as np
from jax import lax
from jax.experimental import pallas as pl
from jax.experimental.pallas import tpu as pltpu
from jax.sharding import PartitionSpec as P

EXACT = lax.Precision.HIGHEST
TABLE_PARTS = (0, 1, 2, 0, 1, 0)
VALUE_PARTS = (0, 0, 0, 1, 1, 2)
VMEM_BYTES = 48 * 1024 * 1024
SCALE = 1.0
PATTERN = (2, 4, 6, 10, 10, 16, 12)
LAST = 4


def fourier_table(length):
    wave_number = np.arange(length)[:, None]
    position = np.arange(length)[None, :]
    nyquist = length // 2
    frequency = np.where(wave_number <= nyquist, wave_number, wave_number - nyquist)
    angle = (frequency * position % length) * (2.0 * math.pi / length)
    edge = (wave_number == 0) | (wave_number == nyquist)
    weight = np.where(edge, math.sqrt(1.0 / length), math.sqrt(2.0 / length))
    table = np.where(wave_number <= nyquist, np.cos(angle), np.sin(angle)) * weight
    return table.astype(np.float32)


def table_parts(table):
    parts = []
    rest = table
    for _ in range(3):
        part = rest.astype(ml_dtypes.bfloat16)
        parts.append(part)
        rest = rest - part.astype(np.float32)
    return parts


def value_parts(value):
    high = value.astype(jnp.bfloat16)
    rest = value - high.astype(jnp.float32)
    middle = rest.astype(jnp.bfloat16)
    low = (rest - middle.astype(jnp.float32)).astype(jnp.bfloat16)
    return high, middle, low


def partner(me, step, count):
    if count & (count - 1) == 0:
        return me ^ step
    return (me + step) % count


def sender(me, step, count):
    if count & (count - 1) == 0:
        return me ^ step
    return (me + count - step) % count


ANY = pl.BlockSpec(memory_space=pl.ANY)


def cost(time):
    return pl.CostEstimate(flops=0, bytes_accessed=int(SCALE * time * 3.0e6), transcendentals=0)


def params():
    return pltpu.CompilerParams(vmem_limit_bytes=VMEM_BYTES)


def first_kernel(table_ref, x_ref, *rest, widths, chunk):
    outs = rest[-len(widths) :]
    rows = table_ref.shape[0] // 3
    tile, inner, length = x_ref.shape
    flat = [out.reshape(width * tile, inner) for out, width in zip(outs, widths)]

    @pl.loop(0, tile // chunk)
    def _(part):
        block = x_ref[pl.ds(chunk * part, chunk)].reshape(chunk * inner, length)
        product = lax.dot_general(
            table_ref[...], block, (((1,), (1,)), ((), ())), preferred_element_type=jnp.float32
        )
        total = product[2 * rows :] + product[rows : 2 * rows] + product[:rows]
        at = 0
        for out, width in zip(flat, widths):
            for j in range(chunk):
                out[pl.ds(chunk * part + j, width, stride=tile), :] = total[
                    at : at + width, j * inner : (j + 1) * inner
                ]
            at += width


def ordered_blocks(array, axis, blocks):
    return jnp.concatenate(
        [lax.dynamic_slice_in_dim(array, block, 1, axis=axis) for block in blocks], axis=axis
    )


def first_transform(spectrum, table, ordered, blocks, first, widths, after):
    members, span_b, span_q, length = spectrum.shape
    groups = ordered.shape[1]
    width = sum(widths)
    if span_q % 128 or span_b % 8:
        chosen = jnp.asarray(table).reshape(length, groups, -1)[:, :, first : first + width]
        chosen = chosen if blocks is None else ordered_blocks(chosen, 1, blocks)
        whole = jnp.einsum("cbqk,ksx->scxbq", spectrum.astype(jnp.float32), chosen, precision=EXACT)
        if blocks is None:
            return whole
        at = np.cumsum([0, *widths])
        return [
            [whole[step, :, at[k] : at[k + 1]] for step in range(groups)] for k in range(len(widths))
        ]
    operand = jnp.asarray(ordered[:, :, first : first + width].reshape(-1, length))
    tile = 16 if span_b % 16 == 0 else 8
    chunk = 8
    while chunk > 2 and operand.shape[0] * chunk * span_q > 2**18:
        chunk //= 2
    if blocks is None:
        parts = [width * groups]
        out_specs = [
            pl.BlockSpec((groups, None, width, tile, span_q), lambda c, b: (0, c, 0, b, 0))
        ]
        out_shape = [jax.ShapeDtypeStruct((groups, members, width, span_b, span_q), jnp.float32)]
    else:
        parts = list(widths) * groups
        out_specs = [
            pl.BlockSpec((None, part, tile, span_q), lambda c, b: (c, 0, b, 0)) for part in parts
        ]
        out_shape = [
            jax.ShapeDtypeStruct((members, part, span_b, span_q), jnp.float32) for part in parts
        ]
    outs = pl.pallas_call(
        functools.partial(first_kernel, widths=parts, chunk=chunk),
        grid=(members, span_b // tile),
        in_specs=[
            pl.BlockSpec(operand.shape, lambda c, b: (0, 0)),
            pl.BlockSpec((None, tile, span_q, length), lambda c, b: (c, b, 0, 0)),
        ]
        + [ANY] * len(after),
        out_specs=out_specs,
        out_shape=out_shape,
        compiler_params=params(),
        cost_estimate=cost(12 + width),
        name="first",
    )(operand, spectrum, *after)
    if blocks is None:
        return outs[0]
    return [outs[k :: len(widths)] for k in range(len(widths))]


def edge_rows(width):
    rows = 8
    while rows < 2 * width:
        rows *= 2
    return rows


def second_kernel(sources_ref, table_ref, *rest, count, planes, span_y):
    ins, out_ref, value_ref = rest[:count], rest[-2], rest[-1]
    tile, span_b, span_q = ins[0].shape
    groups = out_ref.shape[0]
    length = groups * span_y
    first = pl.program_id(1) * tile
    for step in range(count):
        at = pl.multiple_of(sources_ref[step] * span_b, 8)
        for j in range(tile):
            value_ref[pl.ds(at, span_b), j * span_q : (j + 1) * span_q] = ins[step][j]
    parts = value_parts(value_ref[...])
    stacked = jnp.concatenate([parts[p] for p in VALUE_PARTS], axis=0)
    product = jnp.dot(table_ref[...], stacked, preferred_element_type=jnp.float32)

    @pl.when(first == 0)
    def _():
        rest_rows = out_ref.shape[1] - planes * span_y
        out_ref[:, planes * span_y :, :] = jnp.zeros((groups, rest_rows, span_q), jnp.float32)

    for j in range(tile):
        field = product[:, j * span_q : (j + 1) * span_q]
        at = pl.multiple_of((first + j) * span_y, 8)
        out_ref[:, pl.ds(at, span_y), :] = field.reshape(groups, span_y, span_q)
        edge = planes * span_y + 2 * (first + j)
        for g in range(groups):
            before = (g * span_y - 1) % length
            behind = (g + 1) * span_y % length
            out_ref[g, pl.ds(edge, 1), :] = field[before : before + 1]
            out_ref[g, pl.ds(edge + 1, 1), :] = field[behind : behind + 1]


def second_transform(pieces, table, stacked, sources, groups, after):
    count = len(pieces)
    members, width, span_b, span_q = pieces[0].shape
    length = count * span_b
    span_y = length // groups
    edge = edge_rows(width)
    out_shape = (groups, members, width * span_y + edge, span_q)
    if span_q % 128 or span_b % 8 or span_y % 8:
        chosen = ordered_blocks(jnp.asarray(table).reshape(count, span_b, length), 0, sources)
        pieces = jnp.stack([pieces[step] for step in range(count)])
        field = jnp.einsum("scabq,sby->cayq", pieces, chosen, precision=EXACT)
        inner = field.reshape(members, width, groups, span_y, span_q)
        inner = inner.transpose(2, 0, 1, 3, 4).reshape(groups, members, width * span_y, span_q)
        before = jnp.roll(field, 1, axis=2)[:, :, ::span_y]
        behind = jnp.roll(field, -1, axis=2)[:, :, span_y - 1 :: span_y]
        edges = jnp.stack([before, behind], axis=2).transpose(3, 0, 1, 2, 4)
        edges = edges.reshape(groups, members, 2 * width, span_q)
        edges = jnp.pad(edges, ((0, 0), (0, 0), (0, edge - 2 * width), (0, 0)))
        return jnp.concatenate([inner, edges], axis=2)
    tile = 2 if width % 2 == 0 else 1
    if isinstance(pieces, list):
        in_specs = [pl.BlockSpec((None, tile, span_b, span_q), lambda c, a: (c, a, 0, 0))] * count
    else:
        in_specs = [
            pl.BlockSpec((None, None, tile, span_b, span_q), lambda c, a, s=s: (s, c, a, 0, 0))
            for s in range(count)
        ]
        pieces = [pieces] * count
    return pl.pallas_call(
        functools.partial(second_kernel, count=count, planes=width, span_y=span_y),
        grid=(members, width // tile),
        in_specs=[
            pl.BlockSpec(memory_space=pltpu.SMEM),
            pl.BlockSpec(stacked.shape, lambda c, a: (0, 0)),
        ]
        + in_specs
        + [ANY] * len(after),
        out_specs=pl.BlockSpec((groups, None, out_shape[2], span_q), lambda c, a: (0, c, 0, 0)),
        out_shape=jax.ShapeDtypeStruct(out_shape, jnp.float32),
        scratch_shapes=[pltpu.VMEM((length, tile * span_q), jnp.float32)],
        compiler_params=params(),
        cost_estimate=cost(1 + 2 * width),
        name="second",
    )(jnp.stack(sources).astype(jnp.int32), stacked, *pieces, *after)


def third_kernel(table_ref, in_ref, edge_in_ref, *rest):
    out_ref, edge_ref = rest[-2:]
    member = pl.program_id(1)

    def level_of(ref):
        value = jnp.concatenate([ref[g] for g in range(ref.shape[0])], axis=1)
        parts = value_parts(value)
        stacked = jnp.concatenate([parts[p] for p in VALUE_PARTS], axis=1)
        field = jnp.dot(stacked, table_ref[...], preferred_element_type=jnp.float32)
        return 0.5 * (field * field)

    def add(ref, level):
        @pl.when(member == 0)
        def _():
            ref[...] = level

        @pl.when(member > 0)
        def _():
            ref[...] += level

    add(out_ref, level_of(in_ref).reshape(out_ref.shape))

    @pl.when(pl.program_id(0) == 0)
    def _():
        add(edge_ref, level_of(edge_in_ref))


def third_transform(received, width, table, stacked, after):
    groups, members, rows, span_q = received.shape
    edge = edge_rows(width)
    span_y = (rows - edge) // width
    length = groups * span_q
    if span_q % 128 or span_y % 8:
        chosen = jnp.asarray(table).reshape(groups, span_q, length)
        field = jnp.einsum("scrq,sqz->crz", received, chosen, precision=EXACT)
        level = 0.5 * jnp.sum(field * field, axis=0)
        return level[: width * span_y].reshape(width, span_y, length), level[width * span_y :]
    tile = 2 if width % 2 == 0 else 1
    return pl.pallas_call(
        third_kernel,
        grid=(width // tile, members),
        in_specs=[
            pl.BlockSpec(stacked.shape, lambda a, c: (0, 0)),
            pl.BlockSpec((groups, None, tile * span_y, span_q), lambda a, c: (0, c, a, 0)),
            pl.BlockSpec(
                (groups, None, edge, span_q), lambda a, c: (0, c, width * span_y // edge, 0)
            ),
        ]
        + [ANY] * len(after),
        out_specs=[
            pl.BlockSpec((tile, span_y, length), lambda a, c: (a, 0, 0)),
            pl.BlockSpec((edge, length), lambda a, c: (0, 0)),
        ],
        out_shape=[
            jax.ShapeDtypeStruct((width, span_y, length), jnp.float32),
            jax.ShapeDtypeStruct((edge, length), jnp.float32),
        ],
        compiler_params=params(),
        cost_estimate=cost(1 + 2 * width),
        name="third",
    )(stacked, received, received, *after)


def normal_kernel(centre_ref, before_ref, behind_ref, edge_ref, *rest, skip):
    level_ref, normal_ref, token_ref = rest[-3:]
    width, span_y, length = centre_ref.shape
    i = pl.program_id(0) + skip
    centre = centre_ref[i]
    before = jnp.where(i == 0, before_ref[0], centre_ref[jnp.maximum(i - 1, 0)])
    behind = jnp.where(i == width - 1, behind_ref[0], centre_ref[jnp.minimum(i + 1, width - 1)])
    row = lax.broadcasted_iota(jnp.int32, (span_y, length), 0)
    left = jnp.where(row == 0, edge_ref[pl.ds(2 * i, 1), :], pltpu.roll(centre, 1, 0))
    right = jnp.where(
        row == span_y - 1, edge_ref[pl.ds(2 * i + 1, 1), :], pltpu.roll(centre, span_y - 1, 0)
    )
    step_x = 0.5 * (behind - before)
    step_y = 0.5 * (right - left)
    step_z = 0.5 * (pltpu.roll(centre, length - 1, 1) - pltpu.roll(centre, 1, 1))
    magnitude = jnp.sqrt(step_x * step_x + step_y * step_y + step_z * step_z)
    inverse = -1.0 / jnp.maximum(magnitude, 1.0)
    level_ref[0] = centre
    token_ref[...] = jnp.zeros_like(token_ref)
    normal_ref[0, 0] = (step_x * inverse).astype(jnp.bfloat16)
    normal_ref[1, 0] = (step_y * inverse).astype(jnp.bfloat16)
    normal_ref[2, 0] = (step_z * inverse).astype(jnp.bfloat16)


def write_normals(centre, before, behind, edge, skip, count, first, whole, held):
    width, span_y, length = centre.shape
    before, before_at = before
    behind, behind_at = behind
    held = () if held is None else held
    return pl.pallas_call(
        functools.partial(normal_kernel, skip=skip),
        grid=(count,),
        in_specs=[
            pl.BlockSpec((width, span_y, length), lambda i: (0, 0, 0)),
            pl.BlockSpec((1, span_y, length), lambda i: (before_at, 0, 0)),
            pl.BlockSpec((1, span_y, length), lambda i: (behind_at, 0, 0)),
            pl.BlockSpec(edge.shape, lambda i: (0, 0)),
        ]
        + [ANY] * len(held),
        out_specs=[
            pl.BlockSpec((1, span_y, length), lambda i: (first + skip + i, 0, 0)),
            pl.BlockSpec((3, 1, span_y, length), lambda i: (0, first + skip + i, 0, 0)),
            pl.BlockSpec((8, 128), lambda i: (0, 0)),
        ],
        out_shape=[
            jax.ShapeDtypeStruct((whole, span_y, length), jnp.float32),
            jax.ShapeDtypeStruct((3, whole, span_y, length), jnp.bfloat16),
            jax.ShapeDtypeStruct((8, 128), jnp.float32),
        ],
        input_output_aliases={4 + k: k for k in range(len(held))},
        compiler_params=params(),
        cost_estimate=cost(1 + count / 2),
        name="normals",
    )(centre, before, behind, edge, *held)


def slab_widths(planes):
    last = min(LAST, max(planes // 4, 1))
    left = planes - last
    widths = []
    while left:
        width = min(PATTERN[min(len(widths), len(PATTERN) - 1)], left)
        widths.append(width)
        left -= width
    return widths + [last]


def ring(axis, up):
    count = lax.axis_size(axis)
    return [(i, (i + 1) % count if up else (i - 1) % count) for i in range(count)]


def body(spectrum):
    length = spectrum.shape[3]
    rows = lax.axis_size("row")
    cols = lax.axis_size("col")
    planes = length // rows
    table = fourier_table(length)
    parts = table_parts(table)
    first_table = np.stack([part.T.reshape(rows, planes, length) for part in parts])
    second_table = jnp.asarray(np.concatenate([parts[p].T for p in TABLE_PARTS], axis=1))
    third_table = jnp.asarray(np.concatenate([parts[p] for p in TABLE_PARTS], axis=0))

    widths = slab_widths(planes)
    slabs = len(widths)
    split = slabs // 2
    start = planes - sum(widths[:split])
    starts = [(start + sum(widths[:slab])) % planes for slab in range(slabs)]

    me = lax.axis_index("row")
    targets = [partner(me, step, rows) for step in range(rows)]
    sources = [sender(me, step, rows) for step in range(rows)]
    pairs = [[(i, partner(i, step, rows)) for i in range(rows)] for step in range(rows)]
    ordered = ordered_blocks(jnp.asarray(first_table), 1, targets)

    def first(chosen, after):
        outs = first_transform(
            spectrum, table, ordered, targets, starts[chosen[0]], [widths[s] for s in chosen], after
        )
        for slab, out in zip(chosen, outs):
            pieces[slab] = [out[0]] + [
                lax.ppermute(out[step], "row", pairs[step]) for step in range(1, rows)
            ]

    pieces, arrived, levels, edges, halo = {}, {}, {}, {}, {}
    held = None

    def normals(slab, skip=0, count=None):
        nonlocal held
        before = (levels[(slab - 1) % slabs], widths[(slab - 1) % slabs] - 1)
        behind = (levels[(slab + 1) % slabs] if slab + 1 in levels or slab + 1 == slabs else levels[slab], 0)
        if slab == split:
            before = (halo["before"], 0)
        if slab == split - 1:
            behind = (halo["behind"], 0)
        count = widths[slab] - skip if count is None else count
        *held, token = write_normals(
            levels[slab], before, behind, edges[slab], skip, count, starts[slab], planes, held
        )
        return token

    def third(slab, after):
        levels[slab], edges[slab] = third_transform(
            arrived.pop(slab), widths[slab], table, third_table, after
        )
        if slab == split:
            halo["before"] = lax.ppermute(levels[split - 1][-1:], "row", ring("row", True))
            halo["behind"] = lax.ppermute(levels[split][:1], "row", ring("row", False))

    def second(slab, after):
        from_whom = sources if slab else [jnp.int32(step) for step in range(rows)]
        return second_transform(pieces[slab], table, second_table, from_whom, cols, after)

    spectral = first_transform(spectrum, table, first_table, None, starts[0], widths[:1], ())
    pieces[0] = lax.all_to_all(spectral, "row", split_axis=0, concat_axis=0, tiled=True)
    first([1, 2] if split > 2 else [1], (spectral,))
    tokens = {}
    for slab in range(slabs):
        after = [levels[slab - 2]] if slab >= 2 else []
        if slab + 1 < slabs and slab != 1:
            after.append(pieces[slab + 1][0])
        spread = second(slab, after)
        arrived[slab] = lax.all_to_all(spread, "col", split_axis=0, concat_axis=0, tiled=True)
        after = [spread]
        if slab + 2 < slabs and slab + 2 not in pieces:
            first([slab + 2], (pieces[slab + 1][rows - 1],))
            after = [pieces[slab + 2][0]]
        if slab >= 1:
            if slab - 3 in tokens:
                after.append(tokens[slab - 3])
            third(slab - 1, after)
        if slab >= 3:
            tokens[slab - 2] = normals(slab - 2)
    after = [tokens[key] for key in sorted(tokens)[-1:]]
    if widths[slabs - 2] > 1:
        after = [normals(slabs - 2, 0, widths[slabs - 2] - 1)]
    third(slabs - 1, after)
    normals(slabs - 2, widths[slabs - 2] - 1)
    normals(slabs - 1)
    normals(0)
    return tuple(held)


def solution(mesh):
    return jax.shard_map(
        body,
        mesh=mesh,
        in_specs=(P(None, "row", "col", None),),
        out_specs=(P("row", "col", None), P(None, "row", "col", None)),
        check_vma=False,
    )
```

time: 1330 us -> 1260 us (0.947)
  starting transfers between devices: 166 us -> 104 us
  local copies, waits for them, and re-layouts: 58.4 us -> 36 us
    all_to_all x8, waiting for transfers between devices: 219 us -> 361 us  [body(): lax.all_to_all(spread, 'col', split_axis=0, concat_axis=0, tiled=True)]
    ppermute x57 -> x51, waiting for transfers between devices: 418 us -> 291 us  [the longest x49 279 us: first(): lax.ppermute(out[step], 'row', pairs[step])]
    all_to_all x8, starting transfers between devices: 90.5 us -> 43.8 us  [body(): lax.all_to_all(spread, 'col', split_axis=0, concat_axis=0, tiled=True)]
    unnamed x198 -> x161, local copies, waits for them, and re-layouts: 44.2 us -> 28.8 us
    ppermute x57 -> x51, starting transfers between devices: 70.3 us -> 55.2 us  [the longest x49 52.2 us: first(): lax.ppermute(out[step], 'row', pairs[step])]
    pallas_call x8, Pallas kernels: 120 us -> 134 us  [third_transform(): pl.pallas_call(third_kernel, grid=(width // tile, members), in_specs=[pl....]
  transfers between devices with their start and end apart: 66 -> 60, of which waited for: 24 -> 25; matrix products, arithmetic and copies ran while one was open for 1% -> 1% of each run, Pallas kernels for 32% -> 34%
where the time goes in v3:
time: 1260 us
  waiting for transfers between devices  652 us (52%)
  Pallas kernels  464 us (37%)
  starting transfers between devices  104 us (8%)
  local copies, waits for them, and re-layouts  36 us (3%)
    all_to_all x8, waiting for transfers between devices, body(): lax.all_to_all(spread, 'col', split_axis=0, concat_axis=0, tiled=True)  361 us
    ppermute x49, waiting for transfers between devices, first(): lax.ppermute(out[step], 'row', pairs[step])  279 us
    pallas_call x7, Pallas kernels, first_transform(): pl.pallas_call(functools.partial(first_kernel, widths=parts, chunk=chunk)...  140 us
    pallas_call x8, Pallas kernels, second_transform(): pl.pallas_call(functools.partial(second_kernel, count=count, planes=width...  140 us
    pallas_call x8, Pallas kernels, third_transform(): pl.pallas_call(third_kernel, grid=(width // tile, members), in_specs=[pl....  134 us
    ppermute x49, starting transfers between devices, first(): lax.ppermute(out[step], 'row', pairs[step])  52.2 us
    pallas_call x9, Pallas kernels, write_normals(): pl.pallas_call(functools.partial(normal_kernel, skip=skip), grid=(count,)...  49.7 us
    all_to_all x8, starting transfers between devices, body(): lax.all_to_all(spread, 'col', split_axis=0, concat_axis=0, tiled=True)  43.8 us
  transfers between devices with their start and end apart: 60, of which 25 were waited for; matrix products, arithmetic and copies ran while one was open for 1% of the time, Pallas kernels for 34%

profile of v3, /device:TPU:0, one launch (start us, length us, event | category | flops | bytes accessed | tf_op | source)
XLA Modules:
  0.0 1257.7 jit_solution(6260723802862646314)
XLA Ops:
  1.4 17.3 %first.7.rest_0_ = f32[8,3,2,64,128]{4,3,2,1,0:T(8,128)} custom-call(bf16[48,512]{1,0:T(8,128)(2,1)S(1)} %copy-done.44, bf16[3,64,128,512]{3,2,1,0:T(8,128)(2,1)} %x_ref.13), custom_call_target="tpu_custom_call" | custom-call | bytes 42000000 | tf_op jit(solution)/shard_map/first/pallas_call | solution.py:136
  25.8 19.0 %first.8 = (f32[3,4,64,128]{3,2,1,0:T(8,128)S(1)}, f32[3,6,64,128]{3,2,1,0:T(8,128)S(1)}, f32[3,4,64,128]{3,2,1,0:T(8,128)}, f32[3,6,64,128]{3,2,1,0:T(8,128)S(1...) custom-call(bf16[240,512]{1,0:T(8,128)(2,1)S(1)} %reshape.22.table_r, ...), custom_call_target="tpu_custom_call" | custom-call | bytes 66000000 | tf_op jit(solution)/shard_map/first/pallas_call | solution.py:136
  82.7 18.1 %collective-permute-done.28.rest_5_ = f32[3,4,64,128]{3,2,1,0:T(8,128)} collective-permute-done((f32[3,4,64,128]{3,2,1,0:T(8,128)}, f32[3,4,64,128]{3,2,1,0:T(8,128)}, u32[]{:S(2)}, u32[]{:S(2)}) %collective-permute-start.28) | collective-permute-done | bytes 393248 | tf_op jit(solution)/shard_map/ppermute | solution.py:403
  121.2 11.6 collective-permute-done.rest_0_.rest_7_
  137.4 19.5 %first.9 = (f32[3,10,64,128]{3,2,1,0:T(8,128)S(1)}, f32[3,10,64,128]{3,2,1,0:T(8,128)S(1)}, f32[3,10,64,128]{3,2,1,0:T(8,128)}, f32[3,10,64,128]{3,2,1,0:T(8,128...) custom-call(bf16[240,512]{1,0:T(8,128)(2,1)S(1)} %reshape.23.table_r, ...), custom_call_target="tpu_custom_call" | custom-call | bytes 66000000 | tf_op jit(solution)/shard_map/first/pallas_call | solution.py:136
  171.1 13.8 %second.11 = f32[4,3,784,128]{3,2,1,0:T(8,128)} custom-call(s32[8]{0:T(128)S(1)} %stack.26.sources_ref, bf16[512,3072]{1,0:T(8,128)(2,1)} %constant.33.clone.table_ref, f32[3,6,64,128]{3,2,1,0:T(8,128)S(1)} %get-tuple-element.136.rest_0_, f32[3,6,64,128]{3,2,1,0:T(8,128)S(1)} %copy-done.37, f32[3,6,64,128]{3,2,1,0:T(8,128)} %collective-permute-done.32.rest_2_, ...), custom_call_target="tpu_custom_call" | custom-call | bytes 39000000 | tf_op jit(solution)/shard_map/second/pallas_call | solution.py:221
  198.6 20.1 %collective-permute-done.1.rest_0_.rest_7_ = f32[3,10,64,128]{3,2,1,0:T(8,128)S(1)} collective-permute-done((f32[3,10,64,128]{3,2,1,0:T(8,128)S(1)}, f32[3,10,64,128]{3,2,1,0:T(8,128)S(1)}, u32[]{:S(2)}, u32[]{:S(2)}) %collective-permute-start.1) | collective-permute-done | bytes 983072 | tf_op jit(solution)/shard_map/ppermute | solution.py:403
  223.0 19.6 %first.10 = (f32[3,10,64,128]{3,2,1,0:T(8,128)S(1)}, f32[3,10,64,128]{3,2,1,0:T(8,128)S(1)}, f32[3,10,64,128]{3,2,1,0:T(8,128)}, f32[3,10,64,128]{3,2,1,0:T(8,12...) custom-call(bf16[240,512]{1,0:T(8,128)(2,1)S(1)} %reshape.27.table_r, ...), custom_call_target="tpu_custom_call" | custom-call | bytes 66000000 | tf_op jit(solution)/shard_map/first/pallas_call | solution.py:136
  261.4 20.9 %collective-permute-done.23.rest_6_ = f32[3,10,64,128]{3,2,1,0:T(8,128)} collective-permute-done((f32[3,10,64,128]{3,2,1,0:T(8,128)}, f32[3,10,64,128]{3,2,1,0:T(8,128)}, u32[]{:S(2)}, u32[]{:S(2)}) %collective-permute-start.23) | collective-permute-done | bytes 983072 | tf_op jit(solution)/shard_map/ppermute | solution.py:403
  282.3 21.3 %second.10 = f32[4,3,1312,128]{3,2,1,0:T(8,128)} custom-call(s32[8]{0:T(128)S(1)} %stack.26.sources_ref, bf16[512,3072]{1,0:T(8,128)(2,1)} %constant.33.clone.table_ref, f32[3,10,64,128]{3,2,1,0:T(8,128)S(1)} %copy-done.23, f32[3,10,64,128]{3,2,1,0:T(8,128)S(1)} %copy-done.35, f32[3,10,64,128]{3,2,1,0:T(8,128)} %collective-permute-done.19.rest_2_, ...), custom_call_target="tpu_custom_call" | custom-call | bytes 63000000 | tf_op jit(solution)/shard_map/second/pallas_call | solution.py:221
  314.3 20.3 %collective-permute-done.2.rest_0_.rest_7_ = f32[3,10,64,128]{3,2,1,0:T(8,128)S(1)} collective-permute-done((f32[3,10,64,128]{3,2,1,0:T(8,128)S(1)}, f32[3,10,64,128]{3,2,1,0:T(8,128)S(1)}, u32[]{:S(2)}, u32[]{:S(2)}) %collective-permute-start.2) | collective-permute-done | bytes 983072 | tf_op jit(solution)/shard_map/ppermute | solution.py:403
  339.0 24.5 %first.11 = (f32[3,16,64,128]{3,2,1,0:T(8,128)S(1)}, f32[3,16,64,128]{3,2,1,0:T(8,128)S(1)}, f32[3,16,64,128]{3,2,1,0:T(8,128)}, f32[3,16,64,128]{3,2,1,0:T(8,12...) custom-call(bf16[384,512]{1,0:T(8,128)(2,1)S(1)} %bitcast.9, ...), custom_call_target="tpu_custom_call" | custom-call | bytes 84000000 | tf_op jit(solution)/shard_map/first/pallas_call | solution.py:136
  363.6 13.7 %third.10 = (f32[6,128,512]{2,1,0:T(8,128)S(1)}, f32[16,512]{1,0:T(8,128)S(1)}) custom-call(bf16[3072,512]{1,0:T(8,128)(2,1)} %constant.34.clone.table_ref, f32[4,3,784,128]{3,2,1,0:T(8,128)} %all-to-all-done.4.in_ref.edge_in_ref, f32[4,3,784,128]{3,2,1,0:T(8,128)} %all-to-all-done.4.in_ref.edge_in_ref, f32[3,16,64,128]{3,2,1,0:T(8,128)S(1)} %get-tuple-element.113.rest_0_.rest_9_), custom_call_target="tpu_custom_call" | custom-call | bytes 39000000 | tf_op jit(solution)/shard_map/third/pallas_call | solution.py:277
  378.6 19.1 %collective-permute-done.48.rest_6_ = f32[3,10,64,128]{3,2,1,0:T(8,128)S(1)} collective-permute-done((f32[3,10,64,128]{3,2,1,0:T(8,128)}, f32[3,10,64,128]{3,2,1,0:T(8,128)S(1)}, u32[]{:S(2)}, u32[]{:S(2)}) %collective-permute-start.48) | collective-permute-done | bytes 983072 | tf_op jit(solution)/shard_map/ppermute | solution.py:403
  398.7 20.9 %second.13 = f32[4,3,1312,128]{3,2,1,0:T(8,128)} custom-call(s32[8]{0:T(128)S(1)} %stack.26.sources_ref, bf16[512,3072]{1,0:T(8,128)(2,1)} %constant.33.clone.table_ref, f32[3,10,64,128]{3,2,1,0:T(8,128)S(1)} %copy-done.21, f32[3,10,64,128]{3,2,1,0:T(8,128)S(1)} %collective-permute-done.43.rest_1_, f32[3,10,64,128]{3,2,1,0:T(8,128)S(1)} %collective-permute-done.44.rest_2_, ...), custom_call_target="tpu_custom_call" | custom-call | bytes 63000000 | tf_op jit(solution)/shard_map/second/pallas_call | solution.py:221
  419.6 66.4 %all-to-all-done.3.in_ref.edge_in_ref = f32[4,3,1312,128]{3,2,1,0:T(8,128)} async-done(((f32[4,3,1312,128]{3,2,1,0:T(8,128)}), f32[4,3,1312,128]{3,2,1,0:T(8,128)}, u32[]{:S(2)}, u32[]{:S(2)}) %all-to-all-start.3) | async-done | bytes 8060960 | tf_op jit(solution)/shard_map/all_to_all | solution.py:444
  496.3 33.3 %collective-permute-done.3.rest_0_.rest_7_ = f32[3,16,64,128]{3,2,1,0:T(8,128)S(1)} collective-permute-done((f32[3,16,64,128]{3,2,1,0:T(8,128)}, f32[3,16,64,128]{3,2,1,0:T(8,128)S(1)}, u32[]{:S(2)}, u32[]{:S(2)}) %collective-permute-start.3) | collective-permute-done | bytes 1572896 | tf_op jit(solution)/shard_map/ppermute | solution.py:403
  535.5 22.3 %first.12 = (f32[3,12,64,128]{3,2,1,0:T(8,128)S(1)}, f32[3,12,64,128]{3,2,1,0:T(8,128)S(1)}, f32[3,12,64,128]{3,2,1,0:T(8,128)S(1)}, f32[3,12,64,128]{3,2,1,0:T(...) custom-call(bf16[288,512]{1,0:T(8,128)(2,1)S(1)} %reshape.25.table_r, ...), custom_call_target="tpu_custom_call" | custom-call | bytes 72000000 | tf_op jit(solution)/shard_map/first/pallas_call | solution.py:136
  561.2 20.3 %third.11 = (f32[10,128,512]{2,1,0:T(8,128)S(1)}, f32[32,512]{1,0:T(8,128)S(1)}) custom-call(bf16[3072,512]{1,0:T(8,128)(2,1)} %constant.34.clone.table_ref, f32[4,3,1312,128]{3,2,1,0:T(8,128)} %all-to-all-done.3.in_ref.edge_in_ref, f32[4,3,1312,128]{3,2,1,0:T(8,128)} %all-to-all-done.3.in_ref.edge_in_ref, ...), custom_call_target="tpu_custom_call" | custom-call | bytes 63000000 | tf_op jit(solution)/shard_map/third/pallas_call | solution.py:277
  583.7 13.3 %collective-permute-done.14.rest_3_ = f32[3,16,64,128]{3,2,1,0:T(8,128)} collective-permute-done((f32[3,16,64,128]{3,2,1,0:T(8,128)}, f32[3,16,64,128]{3,2,1,0:T(8,128)}, u32[]{:S(2)}, u32[]{:S(2)}) %collective-permute-start.14) | collective-permute-done | bytes 1572896 | tf_op jit(solution)/shard_map/ppermute | solution.py:403
  597.0 33.7 %collective-permute-done.17.rest_6_ = f32[3,16,64,128]{3,2,1,0:T(8,128)} collective-permute-done((f32[3,16,64,128]{3,2,1,0:T(8,128)}, f32[3,16,64,128]{3,2,1,0:T(8,128)}, u32[]{:S(2)}, u32[]{:S(2)}) %collective-permute-start.17) | collective-permute-done | bytes 1572896 | tf_op jit(solution)/shard_map/ppermute | solution.py:403
  630.7 33.0 %second.12 = f32[4,3,2080,128]{3,2,1,0:T(8,128)} custom-call(s32[8]{0:T(128)S(1)} %stack.26.sources_ref, bf16[512,3072]{1,0:T(8,128)(2,1)} %constant.33.clone.table_ref, f32[3,16,64,128]{3,2,1,0:T(8,128)S(1)} %copy-done.17, f32[3,16,64,128]{3,2,1,0:T(8,128)S(1)} %copy-done.31, f32[3,16,64,128]{3,2,1,0:T(8,128)} %collective-permute-done.13.rest_2_, ...), custom_call_target="tpu_custom_call" | custom-call | bytes 99000000 | tf_op jit(solution)/shard_map/second/pallas_call | solution.py:221
  678.5 24.5 %collective-permute-done.4.rest_0_.rest_7_ = f32[3,12,64,128]{3,2,1,0:T(8,128)S(1)} collective-permute-done((f32[3,12,64,128]{3,2,1,0:T(8,128)}, f32[3,12,64,128]{3,2,1,0:T(8,128)S(1)}, u32[]{:S(2)}, u32[]{:S(2)}) %collective-permute-start.4) | collective-permute-done | bytes 1179680 | tf_op jit(solution)/shard_map/ppermute | solution.py:403
  710.4 17.9 %first.13 = (f32[3,4,64,128]{3,2,1,0:T(8,128)S(1)}, f32[3,4,64,128]{3,2,1,0:T(8,128)}, f32[3,4,64,128]{3,2,1,0:T(8,128)}, f32[3,4,64,128]{3,2,1,0:T(8,128)}, f32...) custom-call(bf16[96,512]{1,0:T(8,128)(2,1)S(1)} %reshape.24.table_re, ...), custom_call_target="tpu_custom_call" | custom-call | bytes 48000000 | tf_op jit(solution)/shard_map/first/pallas_call | solution.py:136
  732.4 20.3 %third.12 = (f32[10,128,512]{2,1,0:T(8,128)S(1)}, f32[32,512]{1,0:T(8,128)S(1)}) custom-call(bf16[3072,512]{1,0:T(8,128)(2,1)} %constant.34.clone.table_ref, f32[4,3,1312,128]{3,2,1,0:T(8,128)} %all-to-all-done.6.in_ref.edge_in_ref, f32[4,3,1312,128]{3,2,1,0:T(8,128)} %all-to-all-done.6.in_ref.edge_in_ref, ...), custom_call_target="tpu_custom_call" | custom-call | bytes 63000000 | tf_op jit(solution)/shard_map/third/pallas_call | solution.py:277
  754.9 24.3 %collective-permute-done.42.rest_6_ = f32[3,12,64,128]{3,2,1,0:T(8,128)} collective-permute-done((f32[3,12,64,128]{3,2,1,0:T(8,128)}, f32[3,12,64,128]{3,2,1,0:T(8,128)}, u32[]{:S(2)}, u32[]{:S(2)}) %collective-permute-start.42) | collective-permute-done | bytes 1179680 | tf_op jit(solution)/shard_map/ppermute | solution.py:403
  779.2 25.3 %second.14.rest_0_ = f32[4,3,1568,128]{3,2,1,0:T(8,128)} custom-call(s32[8]{0:T(128)S(1)} %stack.26.sources_ref, bf16[512,3072]{1,0:T(8,128)(2,1)} %constant.33.clone.table_ref, f32[3,12,64,128]{3,2,1,0:T(8,128)S(1)} %copy-done.19, f32[3,12,64,128]{3,2,1,0:T(8,128)S(1)} %copy-done.33, f32[3,12,64,128]{3,2,1,0:T(8,128)} %collective-permute-done.38.rest_2_, ...), custom_call_target="tpu_custom_call" | custom-call | bytes 75000000 | tf_op jit(solution)/shard_map/second/pallas_call | solution.py:221
  804.5 145.9 %all-to-all-done.5.in_ref.edge_in_ref = f32[4,3,2080,128]{3,2,1,0:T(8,128)} async-done(((f32[4,3,2080,128]{3,2,1,0:T(8,128)}), f32[4,3,2080,128]{3,2,1,0:T(8,128)}, u32[]{:S(2)}, u32[]{:S(2)}) %all-to-all-start.5) | async-done | bytes 12779552 | tf_op jit(solution)/shard_map/all_to_all | solution.py:444
  994.2 30.5 %third.13 = (f32[16,128,512]{2,1,0:T(8,128)}, f32[32,512]{1,0:T(8,128)S(1)}) custom-call(bf16[3072,512]{1,0:T(8,128)(2,1)S(1)} %copy-done.1, f32[4,3,2080,128]{3,2,1,0:T(8,128)} %all-to-all-done.5.in_ref.edge_in_ref, f32[4,3,2080,128]{3,2,1,0:T(8,128)} %all-to-all-done.5.in_ref.edge_in_ref, f32[4,3,1568,128]{3,2,1,0:T(8,128)} %second.14.rest_0_, ...), custom_call_target="tpu_custom_call" | custom-call | bytes 99000000 | tf_op jit(solution)/shard_map/third/pallas_call | solution.py:277
  1034.9 130.7 %all-to-all-done.8.in_ref.edge_in_ref = f32[4,3,1568,128]{3,2,1,0:T(8,128)} async-done(((f32[4,3,1568,128]{3,2,1,0:T(8,128)}), f32[4,3,1568,128]{3,2,1,0:T(8,128)}, u32[]{:S(2)}, u32[]{:S(2)}) %all-to-all-start.8) | async-done | bytes 9633824 | tf_op jit(solution)/shard_map/all_to_all | solution.py:444
  1185.6 23.4 %third.14 = (f32[12,128,512]{2,1,0:T(8,128)S(1)}, f32[32,512]{1,0:T(8,128)S(1)}) custom-call(bf16[3072,512]{1,0:T(8,128)(2,1)} %constant.34.clone.table_ref, f32[4,3,1568,128]{3,2,1,0:T(8,128)} %all-to-all-done.8.in_ref.edge_in_ref, f32[4,3,1568,128]{3,2,1,0:T(8,128)} %all-to-all-done.8.in_ref.edge_in_ref, f32[4,3,520,128]{3,2,1,0:T(8,128)} %second.15.rest_0_, ...), custom_call_target="tpu_custom_call" | custom-call | bytes 75000000 | tf_op jit(solution)/shard_map/third/pallas_call | solution.py:277
  1209.0 13.3 %normals.13 = (f32[64,128,512]{2,1,0:T(8,128)}, bf16[3,64,128,512]{3,2,1,0:T(8,128)(2,1)}, f32[8,128]{1,0:T(8,128)}) custom-call(f32[16,128,512]{2,1,0:T(8,128)} %get-tuple-element.168.rest_8_.behind_ref.centre_ref.before_ref, f32[10,128,512]{2,1,0:T(8,128)S(1)} %copy-done.9, ...), custom_call_target="tpu_custom_call", output_to_operand_aliasing={{0}: (4, {}), {1}: (5, {})} | custom-call | bytes 27000000 | tf_op jit(solution)/shard_map/normals/pallas_call | solution.py:331
  (295 shorter events, 298.3 us)
Async XLA Ops:
  57.6 53.4 %all-to-all-start.1 = ((f32[4,3,264,128]{3,2,1,0:T(8,128)}), f32[4,3,264,128]{3,2,1,0:T(8,128)S(1)}, u32[]{:S(2)}, u32[]{:S(2)}) async-start(f32[4,3,264,128]{3,2,1,0:T(8,128)} %second.8), calls=%async_computation.1 | async-start | bytes 3244032 | tf_op jit(solution)/shard_map/all_to_all | solution.py:444
  111.0 77.9 %all-to-all-start.2 = ((f32[4,3,520,128]{3,2,1,0:T(8,128)}), f32[4,3,520,128]{3,2,1,0:T(8,128)}, u32[]{:S(2)}, u32[]{:S(2)}) async-start(f32[4,3,520,128]{3,2,1,0:T(8,128)} %second.9), calls=%async_computation.2 | async-start | bytes 6389760 | tf_op jit(solution)/shard_map/all_to_all | solution.py:444
  119.1 45.2 %collective-permute-start.32 = (f32[3,6,64,128]{3,2,1,0:T(8,128)}, f32[3,6,64,128]{3,2,1,0:T(8,128)}, u32[]{:S(2)}, u32[]{:S(2)}) collective-permute-start(f32[3,6,64,128]{3,2,1,0:T(8,128)} %copy-done.56), channel_id=1, source_target_pairs={{0,8},{4,12},{8,0},{12,4},{16,24},{20,28},{24,16},{28,20},{1,9},{5... | collective-permute-start | bytes 1769480 | tf_op jit(solution)/shard_map/ppermute | solution.py:403
  119.7 44.6 %collective-permute-start.33 = (f32[3,6,64,128]{3,2,1,0:T(8,128)}, f32[3,6,64,128]{3,2,1,0:T(8,128)}, u32[]{:S(2)}, u32[]{:S(2)}) collective-permute-start(f32[3,6,64,128]{3,2,1,0:T(8,128)} %copy-done.55), channel_id=1, source_target_pairs={{0,12},{4,8},{8,4},{12,0},{16,28},{20,24},{24,20},{28,16},{1,13},{... | collective-permute-start | bytes 1769480 | tf_op jit(solution)/shard_map/ppermute | solution.py:403
  188.9 114.6 %all-to-all-start.4 = ((f32[4,3,784,128]{3,2,1,0:T(8,128)}), f32[4,3,784,128]{3,2,1,0:T(8,128)}, u32[]{:S(2)}, u32[]{:S(2)}) async-start(f32[4,3,784,128]{3,2,1,0:T(8,128)} %second.11), calls=%async_computation.4 | async-start | bytes 9633792 | tf_op jit(solution)/shard_map/all_to_all | solution.py:444
  196.7 57.2 %collective-permute-start.19 = (f32[3,10,64,128]{3,2,1,0:T(8,128)}, f32[3,10,64,128]{3,2,1,0:T(8,128)}, u32[]{:S(2)}, u32[]{:S(2)}) collective-permute-start(f32[3,10,64,128]{3,2,1,0:T(8,128)} %get-tuple-element.121), channel_id=1, source_target_pairs={{0,8},{4,12},{8,0},{12,4},{16,24},{20,28},{24,16},{28,20},{1,9},{5... | collective-permute-start | bytes 2949128 | tf_op jit(solution)/shard_map/ppermute | solution.py:403
  197.3 64.1 %collective-permute-start.20 = (f32[3,10,64,128]{3,2,1,0:T(8,128)}, f32[3,10,64,128]{3,2,1,0:T(8,128)}, u32[]{:S(2)}, u32[]{:S(2)}) collective-permute-start(f32[3,10,64,128]{3,2,1,0:T(8,128)} %get-tuple-element.122), channel_id=1, source_target_pairs={{0,12},{4,8},{8,4},{12,0},{16,28},{20,24},{24,20},{28,16},{1,13},{... | collective-permute-start | bytes 2949128 | tf_op jit(solution)/shard_map/ppermute | solution.py:403
  198.1 63.3 %collective-permute-start.21 = (f32[3,10,64,128]{3,2,1,0:T(8,128)}, f32[3,10,64,128]{3,2,1,0:T(8,128)}, u32[]{:S(2)}, u32[]{:S(2)}) collective-permute-start(f32[3,10,64,128]{3,2,1,0:T(8,128)} %get-tuple-element.123), channel_id=1, source_target_pairs={{0,16},{4,20},{8,24},{12,28},{16,0},{20,4},{24,8},{28,12},{1,17},{... | collective-permute-start | bytes 2949128 | tf_op jit(solution)/shard_map/ppermute | solution.py:403
  220.9 61.4 %collective-permute-start.23 = (f32[3,10,64,128]{3,2,1,0:T(8,128)}, f32[3,10,64,128]{3,2,1,0:T(8,128)}, u32[]{:S(2)}, u32[]{:S(2)}) collective-permute-start(f32[3,10,64,128]{3,2,1,0:T(8,128)} %get-tuple-element.125), channel_id=1, source_target_pairs={{0,24},{4,28},{8,16},{12,20},{16,8},{20,12},{24,0},{28,4},{1,25},{... | collective-permute-start | bytes 2949128 | tf_op jit(solution)/shard_map/ppermute | solution.py:403
  303.6 182.4 %all-to-all-start.3 = ((f32[4,3,1312,128]{3,2,1,0:T(8,128)}), f32[4,3,1312,128]{3,2,1,0:T(8,128)}, u32[]{:S(2)}, u32[]{:S(2)}) async-start(f32[4,3,1312,128]{3,2,1,0:T(8,128)} %second.10), calls=%async_computation.3 | async-start | bytes 16121856 | tf_op jit(solution)/shard_map/all_to_all | solution.py:444
  311.7 66.9 %collective-permute-start.44 = (f32[3,10,64,128]{3,2,1,0:T(8,128)}, f32[3,10,64,128]{3,2,1,0:T(8,128)S(1)}, u32[]{:S(2)}, u32[]{:S(2)}) collective-permute-start(f32[3,10,64,128]{3,2,1,0:T(8,128)} %get-tuple-element.154), channel_id=1, source_target_pairs={{0,8},{4,12},{8,0},{12,4},{16,24},{20,28},{24,16},{28,20},{1,9},{5... | collective-permute-start | bytes 2949128 | tf_op jit(solution)/shard_map/ppermute | solution.py:403
  312.3 66.2 %collective-permute-start.45 = (f32[3,10,64,128]{3,2,1,0:T(8,128)}, f32[3,10,64,128]{3,2,1,0:T(8,128)S(1)}, u32[]{:S(2)}, u32[]{:S(2)}) collective-permute-start(f32[3,10,64,128]{3,2,1,0:T(8,128)} %get-tuple-element.155), channel_id=1, source_target_pairs={{0,12},{4,8},{8,4},{12,0},{16,28},{20,24},{24,20},{28,16},{1,13},{... | collective-permute-start | bytes 2949128 | tf_op jit(solution)/shard_map/ppermute | solution.py:403
  313.5 65.0 %collective-permute-start.46 = (f32[3,10,64,128]{3,2,1,0:T(8,128)}, f32[3,10,64,128]{3,2,1,0:T(8,128)S(1)}, u32[]{:S(2)}, u32[]{:S(2)}) collective-permute-start(f32[3,10,64,128]{3,2,1,0:T(8,128)} %get-tuple-element.156), channel_id=1, source_target_pairs={{0,16},{4,20},{8,24},{12,28},{16,0},{20,4},{24,8},{28,12},{1,17},{... | collective-permute-start | bytes 2949128 | tf_op jit(solution)/shard_map/ppermute | solution.py:403
  336.0 61.7 %collective-permute-start.48 = (f32[3,10,64,128]{3,2,1,0:T(8,128)}, f32[3,10,64,128]{3,2,1,0:T(8,128)S(1)}, u32[]{:S(2)}, u32[]{:S(2)}) collective-permute-start(f32[3,10,64,128]{3,2,1,0:T(8,128)} %get-tuple-element.158), channel_id=1, source_target_pairs={{0,24},{4,28},{8,16},{12,20},{16,8},{20,12},{24,0},{28,4},{1,25},{... | collective-permute-start | bytes 2949128 | tf_op jit(solution)/shard_map/ppermute | solution.py:403
  486.0 181.4 %all-to-all-start.6 = ((f32[4,3,1312,128]{3,2,1,0:T(8,128)}), f32[4,3,1312,128]{3,2,1,0:T(8,128)}, u32[]{:S(2)}, u32[]{:S(2)}) async-start(f32[4,3,1312,128]{3,2,1,0:T(8,128)} %second.13), calls=%async_computation.6 | async-start | bytes 16121856 | tf_op jit(solution)/shard_map/all_to_all | solution.py:444
  494.1 89.5 %collective-permute-start.13 = (f32[3,16,64,128]{3,2,1,0:T(8,128)}, f32[3,16,64,128]{3,2,1,0:T(8,128)}, u32[]{:S(2)}, u32[]{:S(2)}) collective-permute-start(f32[3,16,64,128]{3,2,1,0:T(8,128)} %get-tuple-element.115), channel_id=1, source_target_pairs={{0,8},{4,12},{8,0},{12,4},{16,24},{20,28},{24,16},{28,20},{1,9},{5... | collective-permute-start | bytes 4718600 | tf_op jit(solution)/shard_map/ppermute | solution.py:403
  494.6 102.3 %collective-permute-start.14 = (f32[3,16,64,128]{3,2,1,0:T(8,128)}, f32[3,16,64,128]{3,2,1,0:T(8,128)}, u32[]{:S(2)}, u32[]{:S(2)}) collective-permute-start(f32[3,16,64,128]{3,2,1,0:T(8,128)} %get-tuple-element.116), channel_id=1, source_target_pairs={{0,12},{4,8},{8,4},{12,0},{16,28},{20,24},{24,20},{28,16},{1,13},{... | collective-permute-start | bytes 4718600 | tf_op jit(solution)/shard_map/ppermute | solution.py:403
  495.5 101.5 %collective-permute-start.15 = (f32[3,16,64,128]{3,2,1,0:T(8,128)}, f32[3,16,64,128]{3,2,1,0:T(8,128)}, u32[]{:S(2)}, u32[]{:S(2)}) collective-permute-start(f32[3,16,64,128]{3,2,1,0:T(8,128)} %get-tuple-element.117), channel_id=1, source_target_pairs={{0,16},{4,20},{8,24},{12,28},{16,0},{20,4},{24,8},{28,12},{1,17},{... | collective-permute-start | bytes 4718600 | tf_op jit(solution)/shard_map/ppermute | solution.py:403
  529.6 67.4 %collective-permute-start.16 = (f32[3,16,64,128]{3,2,1,0:T(8,128)}, f32[3,16,64,128]{3,2,1,0:T(8,128)}, u32[]{:S(2)}, u32[]{:S(2)}) collective-permute-start(f32[3,16,64,128]{3,2,1,0:T(8,128)} %get-tuple-element.118), channel_id=1, source_target_pairs={{0,20},{4,16},{8,28},{12,24},{16,4},{20,0},{24,12},{28,8},{1,21},{... | collective-permute-start | bytes 4718600 | tf_op jit(solution)/shard_map/ppermute | solution.py:403
  531.9 98.8 %collective-permute-start.17 = (f32[3,16,64,128]{3,2,1,0:T(8,128)}, f32[3,16,64,128]{3,2,1,0:T(8,128)}, u32[]{:S(2)}, u32[]{:S(2)}) collective-permute-start(f32[3,16,64,128]{3,2,1,0:T(8,128)} %get-tuple-element.119), channel_id=1, source_target_pairs={{0,24},{4,28},{8,16},{12,20},{16,8},{20,12},{24,0},{28,4},{1,25},{... | collective-permute-start | bytes 4718600 | tf_op jit(solution)/shard_map/ppermute | solution.py:403
  667.4 283.0 %all-to-all-start.5 = ((f32[4,3,2080,128]{3,2,1,0:T(8,128)}), f32[4,3,2080,128]{3,2,1,0:T(8,128)}, u32[]{:S(2)}, u32[]{:S(2)}) async-start(f32[4,3,2080,128]{3,2,1,0:T(8,128)} %second.12), calls=%async_computation.5 | async-start | bytes 25559040 | tf_op jit(solution)/shard_map/all_to_all | solution.py:444
  676.7 78.2 %collective-permute-start.38 = (f32[3,12,64,128]{3,2,1,0:T(8,128)}, f32[3,12,64,128]{3,2,1,0:T(8,128)}, u32[]{:S(2)}, u32[]{:S(2)}) collective-permute-start(f32[3,12,64,128]{3,2,1,0:T(8,128)} %copy-done.49), channel_id=1, source_target_pairs={{0,8},{4,12},{8,0},{12,4},{16,24},{20,28},{24,16},{28,20},{1,9},{5... | collective-permute-start | bytes 3538952 | tf_op jit(solution)/shard_map/ppermute | solution.py:403
  677.0 77.9 %collective-permute-start.39 = (f32[3,12,64,128]{3,2,1,0:T(8,128)}, f32[3,12,64,128]{3,2,1,0:T(8,128)}, u32[]{:S(2)}, u32[]{:S(2)}) collective-permute-start(f32[3,12,64,128]{3,2,1,0:T(8,128)} %copy-done.48), channel_id=1, source_target_pairs={{0,12},{4,8},{8,4},{12,0},{16,28},{20,24},{24,20},{28,16},{1,13},{... | collective-permute-start | bytes 3538952 | tf_op jit(solution)/shard_map/ppermute | solution.py:403
  678.1 76.9 %collective-permute-start.40 = (f32[3,12,64,128]{3,2,1,0:T(8,128)}, f32[3,12,64,128]{3,2,1,0:T(8,128)}, u32[]{:S(2)}, u32[]{:S(2)}) collective-permute-start(f32[3,12,64,128]{3,2,1,0:T(8,128)} %copy-done.47), channel_id=1, source_target_pairs={{0,16},{4,20},{8,24},{12,28},{16,0},{20,4},{24,8},{28,12},{1,17},{... | collective-permute-start | bytes 3538952 | tf_op jit(solution)/shard_map/ppermute | solution.py:403
  704.0 50.9 %collective-permute-start.41 = (f32[3,12,64,128]{3,2,1,0:T(8,128)}, f32[3,12,64,128]{3,2,1,0:T(8,128)}, u32[]{:S(2)}, u32[]{:S(2)}) collective-permute-start(f32[3,12,64,128]{3,2,1,0:T(8,128)} %get-tuple-element.151), channel_id=1, source_target_pairs={{0,20},{4,16},{8,28},{12,24},{16,4},{20,0},{24,12},{28,8},{1,21},{... | collective-permute-start | bytes 3538952 | tf_op jit(solution)/shard_map/ppermute | solution.py:403
  705.2 74.0 %collective-permute-start.42 = (f32[3,12,64,128]{3,2,1,0:T(8,128)}, f32[3,12,64,128]{3,2,1,0:T(8,128)}, u32[]{:S(2)}, u32[]{:S(2)}) collective-permute-start(f32[3,12,64,128]{3,2,1,0:T(8,128)} %get-tuple-element.152), channel_id=1, source_target_pairs={{0,24},{4,28},{8,16},{12,20},{16,8},{20,12},{24,0},{28,4},{1,25},{... | collective-permute-start | bytes 3538952 | tf_op jit(solution)/shard_map/ppermute | solution.py:403
  950.5 215.1 %all-to-all-start.8 = ((f32[4,3,1568,128]{3,2,1,0:T(8,128)}), f32[4,3,1568,128]{3,2,1,0:T(8,128)}, u32[]{:S(2)}, u32[]{:S(2)}) async-start(f32[4,3,1568,128]{3,2,1,0:T(8,128)} %second.14.rest_0_), calls=%async_computation.8 | async-start | bytes 19267584 | tf_op jit(solution)/shard_map/all_to_all | solution.py:444
  963.1 62.3 %collective-permute-start.5 = (f32[3,4,64,128]{3,2,1,0:T(8,128)}, f32[3,4,64,128]{3,2,1,0:T(8,128)S(1)}, u32[]{:S(2)}, u32[]{:S(2)}) collective-permute-start(f32[3,4,64,128]{3,2,1,0:T(8,128)} %get-tuple-element.106), channel_id=1, source_target_pairs={{0,4},{4,0},{8,12},{12,8},{16,20},{20,16},{24,28},{28,24},{1,5},{5... | collective-permute-start | bytes 1179656 | tf_op jit(solution)/shard_map/ppermute | solution.py:403
  963.1 62.3 %collective-permute-start.6 = (f32[3,4,64,128]{3,2,1,0:T(8,128)}, f32[3,4,64,128]{3,2,1,0:T(8,128)S(1)}, u32[]{:S(2)}, u32[]{:S(2)}) collective-permute-start(f32[3,4,64,128]{3,2,1,0:T(8,128)} %get-tuple-element.107), channel_id=1, source_target_pairs={{0,8},{4,12},{8,0},{12,4},{16,24},{20,28},{24,16},{28,20},{1,9},{5... | collective-permute-start | bytes 1179656 | tf_op jit(solution)/shard_map/ppermute | solution.py:403
  969.4 56.0 %collective-permute-start.7 = (f32[3,4,64,128]{3,2,1,0:T(8,128)}, f32[3,4,64,128]{3,2,1,0:T(8,128)S(1)}, u32[]{:S(2)}, u32[]{:S(2)}) collective-permute-start(f32[3,4,64,128]{3,2,1,0:T(8,128)} %get-tuple-element.108), channel_id=1, source_target_pairs={{0,12},{4,8},{8,4},{12,0},{16,28},{20,24},{24,20},{28,16},{1,13},{... | collective-permute-start | bytes 1179656 | tf_op jit(solution)/shard_map/ppermute | solution.py:403
  977.2 48.2 %collective-permute-start.8 = (f32[3,4,64,128]{3,2,1,0:T(8,128)}, f32[3,4,64,128]{3,2,1,0:T(8,128)S(1)}, u32[]{:S(2)}, u32[]{:S(2)}) collective-permute-start(f32[3,4,64,128]{3,2,1,0:T(8,128)} %get-tuple-element.109), channel_id=1, source_target_pairs={{0,16},{4,20},{8,24},{12,28},{16,0},{20,4},{24,8},{28,12},{1,17},{... | collective-permute-start | bytes 1179656 | tf_op jit(solution)/shard_map/ppermute | solution.py:403
  1165.6 76.2 %all-to-all-start.7 = ((f32[4,3,520,128]{3,2,1,0:T(8,128)}), f32[4,3,520,128]{3,2,1,0:T(8,128)}, u32[]{:S(2)}, u32[]{:S(2)}) async-start(f32[4,3,520,128]{3,2,1,0:T(8,128)} %second.15.rest_0_), calls=%async_computation.7 | async-start | bytes 6389760 | tf_op jit(solution)/shard_map/all_to_all | solution.py:444
  (105 other events, 2089.6 us)

commit v4 on v3

--- a/solution.py
+++ b/solution.py
@@ -15,7 +15,7 @@
 VALUE_PARTS = (0, 0, 0, 1, 1, 2)
 VMEM_BYTES = 48 * 1024 * 1024
 SCALE = 1.0
-PATTERN = (2, 4, 6, 10, 10, 16, 12)
+PATTERN = (6, 6, 10, 10, 16, 12)
 LAST = 4
 
 
@@ -100,20 +100,16 @@
     )
 
 
-def first_transform(spectrum, table, ordered, blocks, first, widths, after):
-    members, span_b, span_q, length = spectrum.shape
+def first_transform(spectrum, table, ordered, blocks, chosen_members, first, width, after):
+    _, span_b, span_q, length = spectrum.shape
+    member, members = chosen_members.start, len(chosen_members)
     groups = ordered.shape[1]
-    width = sum(widths)
     if span_q % 128 or span_b % 8:
+        part = spectrum[member : member + members].astype(jnp.float32)
         chosen = jnp.asarray(table).reshape(length, groups, -1)[:, :, first : first + width]
         chosen = chosen if blocks is None else ordered_blocks(chosen, 1, blocks)
-        whole = jnp.einsum("cbqk,ksx->scxbq", spectrum.astype(jnp.float32), chosen, precision=EXACT)
-        if blocks is None:
-            return whole
-        at = np.cumsum([0, *widths])
-        return [
-            [whole[step, :, at[k] : at[k + 1]] for step in range(groups)] for k in range(len(widths))
-        ]
+        whole = jnp.einsum("cbqk,ksx->scxbq", part, chosen, precision=EXACT)
+        return whole if blocks is None else [whole[step] for step in range(groups)]
     operand = jnp.asarray(ordered[:, :, first : first + width].reshape(-1, length))
     tile = 16 if span_b % 16 == 0 else 8
     chunk = 8
@@ -126,19 +122,17 @@
         ]
         out_shape = [jax.ShapeDtypeStruct((groups, members, width, span_b, span_q), jnp.float32)]
     else:
-        parts = list(widths) * groups
-        out_specs = [
-            pl.BlockSpec((None, part, tile, span_q), lambda c, b: (c, 0, b, 0)) for part in parts
-        ]
+        parts = [width] * groups
+        out_specs = [pl.BlockSpec((None, width, tile, span_q), lambda c, b: (c, 0, b, 0))] * groups
         out_shape = [
-            jax.ShapeDtypeStruct((members, part, span_b, span_q), jnp.float32) for part in parts
-        ]
+            jax.ShapeDtypeStruct((members, width, span_b, span_q), jnp.float32)
+        ] * groups
     outs = pl.pallas_call(
         functools.partial(first_kernel, widths=parts, chunk=chunk),
         grid=(members, span_b // tile),
         in_specs=[
             pl.BlockSpec(operand.shape, lambda c, b: (0, 0)),
-            pl.BlockSpec((None, tile, span_q, length), lambda c, b: (c, b, 0, 0)),
+            pl.BlockSpec((None, tile, span_q, length), lambda c, b: (member + c, b, 0, 0)),
         ]
         + [ANY] * len(after),
         out_specs=out_specs,
@@ -147,9 +141,7 @@
         cost_estimate=cost(12 + width),
         name="first",
     )(operand, spectrum, *after)
-    if blocks is None:
-        return outs[0]
-    return [outs[k :: len(widths)] for k in range(len(widths))]
+    return outs[0] if blocks is None else outs
 
 
 def edge_rows(width):
@@ -236,12 +228,19 @@
     )(jnp.stack(sources).astype(jnp.int32), stacked, *pieces, *after)
 
 
-def third_kernel(table_ref, in_ref, edge_in_ref, *rest):
+def third_kernel(table_ref, *rest, firsts, together):
     out_ref, edge_ref = rest[-2:]
+    ins, edge_ins = rest[: len(firsts)], rest[len(firsts) : 2 * len(firsts)]
     member = pl.program_id(1)
 
-    def level_of(ref):
-        value = jnp.concatenate([ref[g] for g in range(ref.shape[0])], axis=1)
+    def value_of(refs):
+        value = None
+        for ref, first in zip(refs, firsts):
+            here = jnp.concatenate([ref[g] for g in range(ref.shape[0])], axis=1)
+            value = here if value is None else jnp.where(member >= first, here, value)
+        return value
+
+    def level_of(value):
         parts = value_parts(value)
         stacked = jnp.concatenate([parts[p] for p in VALUE_PARTS], axis=1)
         field = jnp.dot(stacked, table_ref[...], preferred_element_type=jnp.float32)
@@ -256,34 +255,46 @@
         def _():
             ref[...] += level
 
-    add(out_ref, level_of(in_ref).reshape(out_ref.shape))
+    if together:
+        level = level_of(jnp.concatenate([value_of(ins), value_of(edge_ins)], axis=0))
+        rows = level.shape[0] - edge_ref.shape[0]
+        add(out_ref, level[:rows].reshape(out_ref.shape))
+        add(edge_ref, level[rows:])
+        return
+    add(out_ref, level_of(value_of(ins)).reshape(out_ref.shape))
 
     @pl.when(pl.program_id(0) == 0)
     def _():
-        add(edge_ref, level_of(edge_in_ref))
+        add(edge_ref, level_of(value_of(edge_ins)))
 
 
 def third_transform(received, width, table, stacked, after):
-    groups, members, rows, span_q = received.shape
+    groups, _, rows, span_q = received[0].shape
     edge = edge_rows(width)
     span_y = (rows - edge) // width
     length = groups * span_q
     if span_q % 128 or span_y % 8:
         chosen = jnp.asarray(table).reshape(groups, span_q, length)
+        received = jnp.concatenate(received, axis=1)
         field = jnp.einsum("scrq,sqz->crz", received, chosen, precision=EXACT)
         level = 0.5 * jnp.sum(field * field, axis=0)
         return level[: width * span_y].reshape(width, span_y, length), level[width * span_y :]
-    tile = 2 if width % 2 == 0 else 1
+    tile = 4 if width == 4 else 2 if width % 2 == 0 else 1
+    counts = [array.shape[1] for array in received]
+    firsts = [sum(counts[:k]) for k in range(len(counts))]
+
+    def spec(block_rows, block_of, first, count):
+        return pl.BlockSpec(
+            (groups, None, block_rows, span_q),
+            lambda a, c: (0, jnp.clip(c - first, 0, count - 1), block_of(a), 0),
+        )
+
     return pl.pallas_call(
-        third_kernel,
-        grid=(width // tile, members),
-        in_specs=[
-            pl.BlockSpec(stacked.shape, lambda a, c: (0, 0)),
-            pl.BlockSpec((groups, None, tile * span_y, span_q), lambda a, c: (0, c, a, 0)),
-            pl.BlockSpec(
-                (groups, None, edge, span_q), lambda a, c: (0, c, width * span_y // edge, 0)
-            ),
-        ]
+        functools.partial(third_kernel, firsts=firsts, together=width == tile),
+        grid=(width // tile, sum(counts)),
+        in_specs=[pl.BlockSpec(stacked.shape, lambda a, c: (0, 0))]
+        + [spec(tile * span_y, lambda a: a, *one) for one in zip(firsts, counts)]
+        + [spec(edge, lambda a: width * span_y // edge, *one) for one in zip(firsts, counts)]
         + [ANY] * len(after),
         out_specs=[
             pl.BlockSpec((tile, span_y, length), lambda a, c: (a, 0, 0)),
@@ -296,7 +307,7 @@
         compiler_params=params(),
         cost_estimate=cost(1 + 2 * width),
         name="third",
-    )(stacked, received, received, *after)
+    )(stacked, *received, *received, *after)
 
 
 def normal_kernel(centre_ref, before_ref, behind_ref, edge_ref, *rest, skip):
@@ -394,22 +405,27 @@
     pairs = [[(i, partner(i, step, rows)) for i in range(rows)] for step in range(rows)]
     ordered = ordered_blocks(jnp.asarray(first_table), 1, targets)
 
-    def first(chosen, after):
+    members = spectrum.shape[0]
+    parts = [(0, range(0, 1)), (0, range(1, members))]
+    parts += [(slab, range(0, members)) for slab in range(1, slabs)]
+
+    def first(part, after):
+        slab, chosen = parts[part]
         outs = first_transform(
-            spectrum, table, ordered, targets, starts[chosen[0]], [widths[s] for s in chosen], after
+            spectrum, table, ordered, targets, chosen, starts[slab], widths[slab], after
         )
-        for slab, out in zip(chosen, outs):
-            pieces[slab] = [out[0]] + [
-                lax.ppermute(out[step], "row", pairs[step]) for step in range(1, rows)
-            ]
+        pieces[part] = [outs[0]] + [
+            lax.ppermute(outs[step], "row", pairs[step]) for step in range(1, rows)
+        ]
 
     pieces, arrived, levels, edges, halo = {}, {}, {}, {}, {}
     held = None
 
     def normals(slab, skip=0, count=None):
         nonlocal held
-        before = (levels[(slab - 1) % slabs], widths[(slab - 1) % slabs] - 1)
-        behind = (levels[(slab + 1) % slabs] if slab + 1 in levels or slab + 1 == slabs else levels[slab], 0)
+        before_slab, behind_slab = (slab - 1) % slabs, (slab + 1) % slabs
+        before = (levels[before_slab], widths[before_slab] - 1) if before_slab in levels else (levels[slab], 0)
+        behind = (levels[behind_slab], 0) if behind_slab in levels else (levels[slab], 0)
         if slab == split:
             before = (halo["before"], 0)
         if slab == split - 1:
@@ -421,44 +437,52 @@
         return token
 
     def third(slab, after):
+        received = [arrived[part] for part in range(len(parts)) if parts[part][0] == slab]
         levels[slab], edges[slab] = third_transform(
-            arrived.pop(slab), widths[slab], table, third_table, after
+            received, widths[slab], table, third_table, after
         )
         if slab == split:
             halo["before"] = lax.ppermute(levels[split - 1][-1:], "row", ring("row", True))
             halo["behind"] = lax.ppermute(levels[split][:1], "row", ring("row", False))
 
-    def second(slab, after):
-        from_whom = sources if slab else [jnp.int32(step) for step in range(rows)]
-        return second_transform(pieces[slab], table, second_table, from_whom, cols, after)
-
-    spectral = first_transform(spectrum, table, first_table, None, starts[0], widths[:1], ())
+    def second(part, after):
+        from_whom = sources if part else [jnp.int32(step) for step in range(rows)]
+        return second_transform(pieces[part], table, second_table, from_whom, cols, after)
+
+    spectral = first_transform(
+        spectrum, table, first_table, None, parts[0][1], starts[0], widths[0], ()
+    )
     pieces[0] = lax.all_to_all(spectral, "row", split_axis=0, concat_axis=0, tiled=True)
-    first([1, 2] if split > 2 else [1], (spectral,))
+    first(1, (spectral,))
     tokens = {}
-    for slab in range(slabs):
-        after = [levels[slab - 2]] if slab >= 2 else []
-        if slab + 1 < slabs and slab != 1:
-            after.append(pieces[slab + 1][0])
-        spread = second(slab, after)
-        arrived[slab] = lax.all_to_all(spread, "col", split_axis=0, concat_axis=0, tiled=True)
+    for part in range(len(parts)):
+        after = []
+        if part >= 2:
+            after.append(levels[part - 3] if part >= 3 else arrived[0])
+        if part + 1 < len(parts):
+            after.append(pieces[part + 1][0])
+        spread = second(part, after)
+        arrived[part] = lax.all_to_all(spread, "col", split_axis=0, concat_axis=0, tiled=True)
         after = [spread]
-        if slab + 2 < slabs and slab + 2 not in pieces:
-            first([slab + 2], (pieces[slab + 1][rows - 1],))
-            after = [pieces[slab + 2][0]]
-        if slab >= 1:
-            if slab - 3 in tokens:
-                after.append(tokens[slab - 3])
-            third(slab - 1, after)
-        if slab >= 3:
-            tokens[slab - 2] = normals(slab - 2)
+        if part + 2 < len(parts):
+            first(part + 2, (pieces[part + 1][rows - 1],))
+            after = [pieces[part + 2][0]]
+        if part >= 2:
+            slab = part - 2
+            if slab - 2 in tokens:
+                after.append(tokens[slab - 2])
+            third(slab, after)
+            if slab >= 2:
+                tokens[slab - 1] = normals(slab - 1)
+            elif slab == 1 and widths[0] > 1:
+                tokens[0] = normals(0, 1)
     after = [tokens[key] for key in sorted(tokens)[-1:]]
     if widths[slabs - 2] > 1:
         after = [normals(slabs - 2, 0, widths[slabs - 2] - 1)]
     third(slabs - 1, after)
     normals(slabs - 2, widths[slabs - 2] - 1)
     normals(slabs - 1)
-    normals(0)
+    normals(0, 0, 1)
     return tuple(held)
 
 

time: 1260 us -> 1250 us (level)
  waiting for transfers between devices: 652 us -> 639 us
    ppermute x49, waiting for transfers between devices: 279 us -> 251 us  [first(): lax.ppermute(outs[step], 'row', pairs[step])]
    pallas_call x8 -> x7, Pallas kernels: 134 us -> 130 us  [third_transform(): pl.pallas_call(functools.partial(third_kernel, firsts=firsts, together=wi...]
    pallas_call x7 -> x8, Pallas kernels: 140 us -> 142 us  [first_transform(): pl.pallas_call(functools.partial(first_kernel, widths=parts, chunk=chunk)...]
    unnamed x161 -> x147, local copies, waits for them, and re-layouts: 28.8 us -> 28.3 us
  transfers between devices with their start and end apart: 60 -> 60, of which waited for: 25 -> 25; matrix products, arithmetic and copies ran while one was open for 1% -> 1% of each run, Pallas kernels for 34% -> 35%
where the time goes in v4:
time: 1250 us; the launch traced here: 1240 us
  waiting for transfers between devices  639 us (51%)
  Pallas kernels  463 us (37%)
  starting transfers between devices  100 us (8%)
  local copies, waits for them, and re-layouts  37.9 us (3%)
    all_to_all x8, waiting for transfers between devices, body(): lax.all_to_all(spread, 'col', split_axis=0, concat_axis=0, tiled=True)  372 us
    ppermute x49, waiting for transfers between devices, first(): lax.ppermute(outs[step], 'row', pairs[step])  251 us
    pallas_call x8, Pallas kernels, first_transform(): pl.pallas_call(functools.partial(first_kernel, widths=parts, chunk=chunk)...  142 us
    pallas_call x8, Pallas kernels, second_transform(): pl.pallas_call(functools.partial(second_kernel, count=count, planes=width...  140 us
    pallas_call x7, Pallas kernels, third_transform(): pl.pallas_call(functools.partial(third_kernel, firsts=firsts, together=wi...  130 us
    ppermute x49, starting transfers between devices, first(): lax.ppermute(outs[step], 'row', pairs[step])  51.1 us
    pallas_call x9, Pallas kernels, write_normals(): pl.pallas_call(functools.partial(normal_kernel, skip=skip), grid=(count,)...  50.1 us
    all_to_all x8, starting transfers between devices, body(): lax.all_to_all(spread, 'col', split_axis=0, concat_axis=0, tiled=True)  43.1 us
  transfers between devices with their start and end apart: 60, of which 25 were waited for; matrix products, arithmetic and copies ran while one was open for 1% of the time, Pallas kernels for 35%

profile of v4, /device:TPU:0, one launch (start us, length us, event | category | flops | bytes accessed | tf_op | source)
XLA Modules:
  0.0 1240.6 jit_solution(8507130110247242138)
XLA Ops:
  15.6 13.0 %first.9 = (f32[2,6,64,128]{3,2,1,0:T(8,128)S(1)}, f32[2,6,64,128]{3,2,1,0:T(8,128)S(1)}, f32[2,6,64,128]{3,2,1,0:T(8,128)}, f32[2,6,64,128]{3,2,1,0:T(8,128)}, ...) custom-call(bf16[144,512]{1,0:T(8,128)(2,1)S(1)} %reshape.25.table_r, ...), custom_call_target="tpu_custom_call" | custom-call | bytes 54000000 | tf_op jit(solution)/shard_map/first/pallas_call | solution.py:130
  61.4 18.3 %first.10 = (f32[3,6,64,128]{3,2,1,0:T(8,128)S(1)}, f32[3,6,64,128]{3,2,1,0:T(8,128)S(1)}, f32[3,6,64,128]{3,2,1,0:T(8,128)S(1)}, f32[3,6,64,128]{3,2,1,0:T(8,12...) custom-call(bf16[144,512]{1,0:T(8,128)(2,1)S(1)} %reshape.26.table_r, ...), custom_call_target="tpu_custom_call" | custom-call | bytes 54000000 | tf_op jit(solution)/shard_map/first/pallas_call | solution.py:130
  123.2 19.4 %first.11 = (f32[3,10,64,128]{3,2,1,0:T(8,128)S(1)}, f32[3,10,64,128]{3,2,1,0:T(8,128)S(1)}, f32[3,10,64,128]{3,2,1,0:T(8,128)}, f32[3,10,64,128]{3,2,1,0:T(8,12...) custom-call(bf16[240,512]{1,0:T(8,128)(2,1)S(1)} %reshape.28.table_r, ...), custom_call_target="tpu_custom_call" | custom-call | bytes 66000000 | tf_op jit(solution)/shard_map/first/pallas_call | solution.py:130
  143.6 12.2 collective-permute-done.36.rest_6_
  155.8 13.8 %second.11 = f32[4,3,784,128]{3,2,1,0:T(8,128)} custom-call(s32[8]{0:T(128)S(1)} %stack.26.sources_ref, bf16[512,3072]{1,0:T(8,128)(2,1)} %constant.33.clone.table_ref, f32[3,6,64,128]{3,2,1,0:T(8,128)S(1)} %get-tuple-element.103.rest_8_.rest_0_, f32[3,6,64,128]{3,2,1,0:T(8,128)S(1)} %collective-permute-done.31.rest_1_, ...), custom_call_target="tpu_custom_call" | custom-call | bytes 39000000 | tf_op jit(solution)/shard_map/second/pallas_call | solution.py:213
  183.2 21.0 %collective-permute-done.8.rest_0_.rest_7_ = f32[3,10,64,128]{3,2,1,0:T(8,128)S(1)} collective-permute-done((f32[3,10,64,128]{3,2,1,0:T(8,128)}, f32[3,10,64,128]{3,2,1,0:T(8,128)S(1)}, u32[]{:S(2)}, u32[]{:S(2)}) %collective-permute-start.8) | collective-permute-done | bytes 983072 | tf_op jit(solution)/shard_map/ppermute | solution.py:418
  208.1 19.3 %first.12 = (f32[3,10,64,128]{3,2,1,0:T(8,128)S(1)}, f32[3,10,64,128]{3,2,1,0:T(8,128)S(1)}, f32[3,10,64,128]{3,2,1,0:T(8,128)}, f32[3,10,64,128]{3,2,1,0:T(8,12...) custom-call(bf16[240,512]{1,0:T(8,128)(2,1)S(1)} %reshape.27.table_r, ...), custom_call_target="tpu_custom_call" | custom-call | bytes 66000000 | tf_op jit(solution)/shard_map/first/pallas_call | solution.py:130
  227.4 14.4 %third.7 = (f32[6,128,512]{2,1,0:T(8,128)S(1)}, f32[16,512]{1,0:T(8,128)S(1)}) custom-call(bf16[3072,512]{1,0:T(8,128)(2,1)} %constant.34.clone.table_ref, f32[4,1,784,128]{3,2,1,0:T(8,128)S(1)} %copy-done.12, f32[4,2,784,128]{3,2,1,0:T(8,128)} %all-to-all-done.2.rest_1_.rest_3_, f32[4,1,784,128]{3,2,1,0:T(8,128)S(1)} %copy-done.12, ...), custom_call_target="tpu_custom_call" | custom-call | bytes 39000000 | tf_op jit(solution)/shard_map/third/pallas_call | solution.py:292
  246.4 20.9 %collective-permute-done.30.rest_6_ = f32[3,10,64,128]{3,2,1,0:T(8,128)} collective-permute-done((f32[3,10,64,128]{3,2,1,0:T(8,128)}, f32[3,10,64,128]{3,2,1,0:T(8,128)}, u32[]{:S(2)}, u32[]{:S(2)}) %collective-permute-start.30) | collective-permute-done | bytes 983072 | tf_op jit(solution)/shard_map/ppermute | solution.py:418
  267.3 21.3 %second.10 = f32[4,3,1312,128]{3,2,1,0:T(8,128)} custom-call(s32[8]{0:T(128)S(1)} %stack.26.sources_ref, bf16[512,3072]{1,0:T(8,128)(2,1)} %constant.33.clone.table_ref, f32[3,10,64,128]{3,2,1,0:T(8,128)S(1)} %get-tuple-element.126.rest_0_.rest_9_, f32[3,10,64,128]{3,2,1,0:T(8,128)S(1)} %collective-permute-done.25.rest_1_, ...), custom_call_target="tpu_custom_call" | custom-call | bytes 63000000 | tf_op jit(solution)/shard_map/second/pallas_call | solution.py:213
  298.9 20.5 %collective-permute-done.9.rest_0_.rest_7_ = f32[3,10,64,128]{3,2,1,0:T(8,128)S(1)} collective-permute-done((f32[3,10,64,128]{3,2,1,0:T(8,128)}, f32[3,10,64,128]{3,2,1,0:T(8,128)S(1)}, u32[]{:S(2)}, u32[]{:S(2)}) %collective-permute-start.9) | collective-permute-done | bytes 983072 | tf_op jit(solution)/shard_map/ppermute | solution.py:418
  323.7 24.6 %first.13 = (f32[3,16,64,128]{3,2,1,0:T(8,128)S(1)}, f32[3,16,64,128]{3,2,1,0:T(8,128)S(1)}, f32[3,16,64,128]{3,2,1,0:T(8,128)}, f32[3,16,64,128]{3,2,1,0:T(8,12...) custom-call(bf16[384,512]{1,0:T(8,128)(2,1)S(1)} %bitcast.9, ...), custom_call_target="tpu_custom_call" | custom-call | bytes 84000000 | tf_op jit(solution)/shard_map/first/pallas_call | solution.py:130
  348.3 13.8 %third.8 = (f32[6,128,512]{2,1,0:T(8,128)S(1)}, f32[16,512]{1,0:T(8,128)S(1)}) custom-call(bf16[3072,512]{1,0:T(8,128)(2,1)} %constant.34.clone.table_ref, f32[4,3,784,128]{3,2,1,0:T(8,128)} %all-to-all-done.4.rest_0_.rest_1_, f32[4,3,784,128]{3,2,1,0:T(8,128)} %all-to-all-done.4.rest_0_.rest_1_, ...), custom_call_target="tpu_custom_call" | custom-call | bytes 39000000 | tf_op jit(solution)/shard_map/third/pallas_call | solution.py:292
  363.3 19.7 %collective-permute-done.48.rest_6_ = f32[3,10,64,128]{3,2,1,0:T(8,128)S(1)} collective-permute-done((f32[3,10,64,128]{3,2,1,0:T(8,128)}, f32[3,10,64,128]{3,2,1,0:T(8,128)S(1)}, u32[]{:S(2)}, u32[]{:S(2)}) %collective-permute-start.48) | collective-permute-done | bytes 983072 | tf_op jit(solution)/shard_map/ppermute | solution.py:418
  383.9 21.0 %second.13 = f32[4,3,1312,128]{3,2,1,0:T(8,128)} custom-call(s32[8]{0:T(128)S(1)} %stack.26.sources_ref, bf16[512,3072]{1,0:T(8,128)(2,1)} %constant.33.clone.table_ref, f32[3,10,64,128]{3,2,1,0:T(8,128)S(1)} %copy-done.23, f32[3,10,64,128]{3,2,1,0:T(8,128)S(1)} %collective-permute-done.43.rest_1_, f32[3,10,64,128]{3,2,1,0:T(8,128)S(1)} %collective-permute-done.44.rest_2_, ...), custom_call_target="tpu_custom_call" | custom-call | bytes 63000000 | tf_op jit(solution)/shard_map/second/pallas_call | solution.py:213
  404.9 66.2 %all-to-all-done.3.rest_0_.rest_1_ = f32[4,3,1312,128]{3,2,1,0:T(8,128)} async-done(((f32[4,3,1312,128]{3,2,1,0:T(8,128)}), f32[4,3,1312,128]{3,2,1,0:T(8,128)}, u32[]{:S(2)}, u32[]{:S(2)}) %all-to-all-start.3) | async-done | bytes 8060960 | tf_op jit(solution)/shard_map/all_to_all | solution.py:465
  481.2 33.2 %collective-permute-done.10.rest_0_.rest_7_ = f32[3,16,64,128]{3,2,1,0:T(8,128)S(1)} collective-permute-done((f32[3,16,64,128]{3,2,1,0:T(8,128)}, f32[3,16,64,128]{3,2,1,0:T(8,128)S(1)}, u32[]{:S(2)}, u32[]{:S(2)}) %collective-permute-start.10) | collective-permute-done | bytes 1572896 | tf_op jit(solution)/shard_map/ppermute | solution.py:418
  519.4 22.3 %first.14 = (f32[3,12,64,128]{3,2,1,0:T(8,128)S(1)}, f32[3,12,64,128]{3,2,1,0:T(8,128)S(1)}, f32[3,12,64,128]{3,2,1,0:T(8,128)S(1)}, f32[3,12,64,128]{3,2,1,0:T(...) custom-call(bf16[288,512]{1,0:T(8,128)(2,1)S(1)} %reshape.30.table_r, ...), custom_call_target="tpu_custom_call" | custom-call | bytes 72000000 | tf_op jit(solution)/shard_map/first/pallas_call | solution.py:130
  546.1 20.3 %third.9 = (f32[10,128,512]{2,1,0:T(8,128)S(1)}, f32[32,512]{1,0:T(8,128)S(1)}) custom-call(bf16[3072,512]{1,0:T(8,128)(2,1)} %constant.34.clone.table_ref, f32[4,3,1312,128]{3,2,1,0:T(8,128)} %all-to-all-done.3.rest_0_.rest_1_, f32[4,3,1312,128]{3,2,1,0:T(8,128)} %all-to-all-done.3.rest_0_.rest_1_, ...), custom_call_target="tpu_custom_call" | custom-call | bytes 63000000 | tf_op jit(solution)/shard_map/third/pallas_call | solution.py:292
  568.6 12.2 collective-permute-done.21.rest_3_
  581.9 33.3 %collective-permute-done.24.rest_6_ = f32[3,16,64,128]{3,2,1,0:T(8,128)} collective-permute-done((f32[3,16,64,128]{3,2,1,0:T(8,128)}, f32[3,16,64,128]{3,2,1,0:T(8,128)}, u32[]{:S(2)}, u32[]{:S(2)}) %collective-permute-start.24) | collective-permute-done | bytes 1572896 | tf_op jit(solution)/shard_map/ppermute | solution.py:418
  615.1 32.9 %second.12 = f32[4,3,2080,128]{3,2,1,0:T(8,128)} custom-call(s32[8]{0:T(128)S(1)} %stack.26.sources_ref, bf16[512,3072]{1,0:T(8,128)(2,1)} %constant.33.clone.table_ref, f32[3,16,64,128]{3,2,1,0:T(8,128)S(1)} %copy-done.19, f32[3,16,64,128]{3,2,1,0:T(8,128)S(1)} %copy-done.28, f32[3,16,64,128]{3,2,1,0:T(8,128)} %collective-permute-done.20.rest_2_, ...), custom_call_target="tpu_custom_call" | custom-call | bytes 99000000 | tf_op jit(solution)/shard_map/second/pallas_call | solution.py:213
  663.7 24.7 %collective-permute-done.11.rest_0_.rest_7_ = f32[3,12,64,128]{3,2,1,0:T(8,128)S(1)} collective-permute-done((f32[3,12,64,128]{3,2,1,0:T(8,128)}, f32[3,12,64,128]{3,2,1,0:T(8,128)S(1)}, u32[]{:S(2)}, u32[]{:S(2)}) %collective-permute-start.11) | collective-permute-done | bytes 1179680 | tf_op jit(solution)/shard_map/ppermute | solution.py:418
  695.9 18.0 %first.15 = (f32[3,4,64,128]{3,2,1,0:T(8,128)S(1)}, f32[3,4,64,128]{3,2,1,0:T(8,128)S(1)}, f32[3,4,64,128]{3,2,1,0:T(8,128)S(1)}, f32[3,4,64,128]{3,2,1,0:T(8,12...) custom-call(bf16[96,512]{1,0:T(8,128)(2,1)S(1)} %copy-done.31, ...), custom_call_target="tpu_custom_call" | custom-call | bytes 48000000 | tf_op jit(solution)/shard_map/first/pallas_call | solution.py:130
  718.0 20.3 %third.10 = (f32[10,128,512]{2,1,0:T(8,128)S(1)}, f32[32,512]{1,0:T(8,128)S(1)}) custom-call(bf16[3072,512]{1,0:T(8,128)(2,1)} %constant.34.clone.table_ref, f32[4,3,1312,128]{3,2,1,0:T(8,128)} %all-to-all-done.6.rest_0_.rest_1_, f32[4,3,1312,128]{3,2,1,0:T(8,128)} %all-to-all-done.6.rest_0_.rest_1_, ...), custom_call_target="tpu_custom_call" | custom-call | bytes 63000000 | tf_op jit(solution)/shard_map/third/pallas_call | solution.py:292
  740.5 22.3 %collective-permute-done.42.rest_6_ = f32[3,12,64,128]{3,2,1,0:T(8,128)} collective-permute-done((f32[3,12,64,128]{3,2,1,0:T(8,128)}, f32[3,12,64,128]{3,2,1,0:T(8,128)}, u32[]{:S(2)}, u32[]{:S(2)}) %collective-permute-start.42) | collective-permute-done | bytes 1179680 | tf_op jit(solution)/shard_map/ppermute | solution.py:418
  762.8 25.2 %second.14.rest_2_ = f32[4,3,1568,128]{3,2,1,0:T(8,128)} custom-call(s32[8]{0:T(128)S(1)} %stack.26.sources_ref, bf16[512,3072]{1,0:T(8,128)(2,1)} %constant.33.clone.table_ref, f32[3,12,64,128]{3,2,1,0:T(8,128)S(1)} %copy-done.21, f32[3,12,64,128]{3,2,1,0:T(8,128)S(1)} %copy-done.30, f32[3,12,64,128]{3,2,1,0:T(8,128)} %collective-permute-done.38.rest_2_, ...), custom_call_target="tpu_custom_call" | custom-call | bytes 75000000 | tf_op jit(solution)/shard_map/second/pallas_call | solution.py:213
  788.1 147.5 %all-to-all-done.5.rest_0_.rest_1_ = f32[4,3,2080,128]{3,2,1,0:T(8,128)} async-done(((f32[4,3,2080,128]{3,2,1,0:T(8,128)}), f32[4,3,2080,128]{3,2,1,0:T(8,128)}, u32[]{:S(2)}, u32[]{:S(2)}) %all-to-all-start.5) | async-done | bytes 12779552 | tf_op jit(solution)/shard_map/all_to_all | solution.py:465
  972.1 30.5 %third.11 = (f32[16,128,512]{2,1,0:T(8,128)}, f32[32,512]{1,0:T(8,128)S(1)}) custom-call(bf16[3072,512]{1,0:T(8,128)(2,1)S(1)} %copy-done, f32[4,3,2080,128]{3,2,1,0:T(8,128)} %all-to-all-done.5.rest_0_.rest_1_, f32[4,3,2080,128]{3,2,1,0:T(8,128)} %all-to-all-done.5.rest_0_.rest_1_, f32[4,3,1568,128]{3,2,1,0:T(8,128)} %second.14.rest_2_, ...), custom_call_target="tpu_custom_call" | custom-call | bytes 99000000 | tf_op jit(solution)/shard_map/third/pallas_call | solution.py:292
  1012.8 137.9 %all-to-all-done.8.rest_0_.rest_1_ = f32[4,3,1568,128]{3,2,1,0:T(8,128)} async-done(((f32[4,3,1568,128]{3,2,1,0:T(8,128)}), f32[4,3,1568,128]{3,2,1,0:T(8,128)}, u32[]{:S(2)}, u32[]{:S(2)}) %all-to-all-start.8) | async-done | bytes 9633824 | tf_op jit(solution)/shard_map/all_to_all | solution.py:465
  1170.8 23.4 %third.12 = (f32[12,128,512]{2,1,0:T(8,128)S(1)}, f32[32,512]{1,0:T(8,128)S(1)}) custom-call(bf16[3072,512]{1,0:T(8,128)(2,1)} %constant.34.clone.table_ref, f32[4,3,1568,128]{3,2,1,0:T(8,128)} %all-to-all-done.8.rest_0_.rest_1_, f32[4,3,1568,128]{3,2,1,0:T(8,128)} %all-to-all-done.8.rest_0_.rest_1_, f32[4,3,520,128]{3,2,1,0:T(8,128)} %second.15.rest_2_, ...), custom_call_target="tpu_custom_call" | custom-call | bytes 75000000 | tf_op jit(solution)/shard_map/third/pallas_call | solution.py:292
  1194.2 13.3 %normals.13 = (f32[64,128,512]{2,1,0:T(8,128)}, bf16[3,64,128,512]{3,2,1,0:T(8,128)(2,1)}, f32[8,128]{1,0:T(8,128)}) custom-call(f32[16,128,512]{2,1,0:T(8,128)} %get-tuple-element.165.rest_8_.behind_ref.centre_ref.before_ref, f32[10,128,512]{2,1,0:T(8,128)S(1)} %copy-done.17, ...), custom_call_target="tpu_custom_call", output_to_operand_aliasing={{0}: (4, {}), {1}: (5, {})} | custom-call | bytes 27000000 | tf_op jit(solution)/shard_map/normals/pallas_call | solution.py:342
  (283 shorter events, 282.5 us)
Async XLA Ops:
  41.4 53.6 %all-to-all-start.1 = ((f32[4,1,784,128]{3,2,1,0:T(8,128)}), f32[4,1,784,128]{3,2,1,0:T(8,128)S(1)}, u32[]{:S(2)}, u32[]{:S(2)}) async-start(f32[4,1,784,128]{3,2,1,0:T(8,128)} %second.8), calls=%async_computation.1 | async-start | bytes 3211264 | tf_op jit(solution)/shard_map/all_to_all | solution.py:465
  96.3 77.7 %all-to-all-start.2 = ((f32[4,2,784,128]{3,2,1,0:T(8,128)}), f32[4,2,784,128]{3,2,1,0:T(8,128)}, u32[]{:S(2)}, u32[]{:S(2)}) async-start(f32[4,2,784,128]{3,2,1,0:T(8,128)} %second.9), calls=%async_computation.2 | async-start | bytes 6422528 | tf_op jit(solution)/shard_map/all_to_all | solution.py:465
  174.0 114.6 %all-to-all-start.4 = ((f32[4,3,784,128]{3,2,1,0:T(8,128)}), f32[4,3,784,128]{3,2,1,0:T(8,128)}, u32[]{:S(2)}, u32[]{:S(2)}) async-start(f32[4,3,784,128]{3,2,1,0:T(8,128)} %second.11), calls=%async_computation.4 | async-start | bytes 9633792 | tf_op jit(solution)/shard_map/all_to_all | solution.py:465
  180.7 62.4 %collective-permute-start.26 = (f32[3,10,64,128]{3,2,1,0:T(8,128)}, f32[3,10,64,128]{3,2,1,0:T(8,128)}, u32[]{:S(2)}, u32[]{:S(2)}) collective-permute-start(f32[3,10,64,128]{3,2,1,0:T(8,128)} %get-tuple-element.128), channel_id=1, source_target_pairs={{0,8},{4,12},{8,0},{12,4},{16,24},{20,28},{24,16},{28,20},{1,9},{5... | collective-permute-start | bytes 2949128 | tf_op jit(solution)/shard_map/ppermute | solution.py:418
  181.3 64.3 %collective-permute-start.27 = (f32[3,10,64,128]{3,2,1,0:T(8,128)}, f32[3,10,64,128]{3,2,1,0:T(8,128)}, u32[]{:S(2)}, u32[]{:S(2)}) collective-permute-start(f32[3,10,64,128]{3,2,1,0:T(8,128)} %get-tuple-element.129), channel_id=1, source_target_pairs={{0,12},{4,8},{8,4},{12,0},{16,28},{20,24},{24,20},{28,16},{1,13},{... | collective-permute-start | bytes 2949128 | tf_op jit(solution)/shard_map/ppermute | solution.py:418
  182.0 63.6 %collective-permute-start.28 = (f32[3,10,64,128]{3,2,1,0:T(8,128)}, f32[3,10,64,128]{3,2,1,0:T(8,128)}, u32[]{:S(2)}, u32[]{:S(2)}) collective-permute-start(f32[3,10,64,128]{3,2,1,0:T(8,128)} %get-tuple-element.130), channel_id=1, source_target_pairs={{0,16},{4,20},{8,24},{12,28},{16,0},{20,4},{24,8},{28,12},{1,17},{... | collective-permute-start | bytes 2949128 | tf_op jit(solution)/shard_map/ppermute | solution.py:418
  204.3 63.0 %collective-permute-start.30 = (f32[3,10,64,128]{3,2,1,0:T(8,128)}, f32[3,10,64,128]{3,2,1,0:T(8,128)}, u32[]{:S(2)}, u32[]{:S(2)}) collective-permute-start(f32[3,10,64,128]{3,2,1,0:T(8,128)} %get-tuple-element.132), channel_id=1, source_target_pairs={{0,24},{4,28},{8,16},{12,20},{16,8},{20,12},{24,0},{28,4},{1,25},{... | collective-permute-start | bytes 2949128 | tf_op jit(solution)/shard_map/ppermute | solution.py:418
  288.6 182.5 %all-to-all-start.3 = ((f32[4,3,1312,128]{3,2,1,0:T(8,128)}), f32[4,3,1312,128]{3,2,1,0:T(8,128)}, u32[]{:S(2)}, u32[]{:S(2)}) async-start(f32[4,3,1312,128]{3,2,1,0:T(8,128)} %second.10), calls=%async_computation.3 | async-start | bytes 16121856 | tf_op jit(solution)/shard_map/all_to_all | solution.py:465
  295.6 67.6 %collective-permute-start.44 = (f32[3,10,64,128]{3,2,1,0:T(8,128)}, f32[3,10,64,128]{3,2,1,0:T(8,128)S(1)}, u32[]{:S(2)}, u32[]{:S(2)}) collective-permute-start(f32[3,10,64,128]{3,2,1,0:T(8,128)} %get-tuple-element.151), channel_id=1, source_target_pairs={{0,8},{4,12},{8,0},{12,4},{16,24},{20,28},{24,16},{28,20},{1,9},{5... | collective-permute-start | bytes 2949128 | tf_op jit(solution)/shard_map/ppermute | solution.py:418
  296.3 67.0 %collective-permute-start.45 = (f32[3,10,64,128]{3,2,1,0:T(8,128)}, f32[3,10,64,128]{3,2,1,0:T(8,128)S(1)}, u32[]{:S(2)}, u32[]{:S(2)}) collective-permute-start(f32[3,10,64,128]{3,2,1,0:T(8,128)} %get-tuple-element.152), channel_id=1, source_target_pairs={{0,12},{4,8},{8,4},{12,0},{16,28},{20,24},{24,20},{28,16},{1,13},{... | collective-permute-start | bytes 2949128 | tf_op jit(solution)/shard_map/ppermute | solution.py:418
  297.5 65.8 %collective-permute-start.46 = (f32[3,10,64,128]{3,2,1,0:T(8,128)}, f32[3,10,64,128]{3,2,1,0:T(8,128)S(1)}, u32[]{:S(2)}, u32[]{:S(2)}) collective-permute-start(f32[3,10,64,128]{3,2,1,0:T(8,128)} %get-tuple-element.153), channel_id=1, source_target_pairs={{0,16},{4,20},{8,24},{12,28},{16,0},{20,4},{24,8},{28,12},{1,17},{... | collective-permute-start | bytes 2949128 | tf_op jit(solution)/shard_map/ppermute | solution.py:418
  319.4 43.9 %collective-permute-start.47 = (f32[3,10,64,128]{3,2,1,0:T(8,128)S(1)}, f32[3,10,64,128]{3,2,1,0:T(8,128)S(1)}, u32[]{:S(2)}, u32[]{:S(2)}) collective-permute-start(f32[3,10,64,128]{3,2,1,0:T(8,128)S(1)} %copy-done.50), channel_id=1, source_target_pairs={{0,20},{4,16},{8,28},{12,24},{16,4},{20,0},{24,12},{28,8},{1,21},{... | collective-permute-start | bytes 2949128 | tf_op jit(solution)/shard_map/ppermute | solution.py:418
  320.4 62.6 %collective-permute-start.48 = (f32[3,10,64,128]{3,2,1,0:T(8,128)}, f32[3,10,64,128]{3,2,1,0:T(8,128)S(1)}, u32[]{:S(2)}, u32[]{:S(2)}) collective-permute-start(f32[3,10,64,128]{3,2,1,0:T(8,128)} %get-tuple-element.155), channel_id=1, source_target_pairs={{0,24},{4,28},{8,16},{12,20},{16,8},{20,12},{24,0},{28,4},{1,25},{... | collective-permute-start | bytes 2949128 | tf_op jit(solution)/shard_map/ppermute | solution.py:418
  471.0 181.5 %all-to-all-start.6 = ((f32[4,3,1312,128]{3,2,1,0:T(8,128)}), f32[4,3,1312,128]{3,2,1,0:T(8,128)}, u32[]{:S(2)}, u32[]{:S(2)}) async-start(f32[4,3,1312,128]{3,2,1,0:T(8,128)} %second.13), calls=%async_computation.6 | async-start | bytes 16121856 | tf_op jit(solution)/shard_map/all_to_all | solution.py:465
  478.0 90.6 %collective-permute-start.20 = (f32[3,16,64,128]{3,2,1,0:T(8,128)}, f32[3,16,64,128]{3,2,1,0:T(8,128)}, u32[]{:S(2)}, u32[]{:S(2)}) collective-permute-start(f32[3,16,64,128]{3,2,1,0:T(8,128)} %get-tuple-element.121), channel_id=1, source_target_pairs={{0,8},{4,12},{8,0},{12,4},{16,24},{20,28},{24,16},{28,20},{1,9},{5... | collective-permute-start | bytes 4718600 | tf_op jit(solution)/shard_map/ppermute | solution.py:418
  478.7 102.0 %collective-permute-start.21 = (f32[3,16,64,128]{3,2,1,0:T(8,128)}, f32[3,16,64,128]{3,2,1,0:T(8,128)}, u32[]{:S(2)}, u32[]{:S(2)}) collective-permute-start(f32[3,16,64,128]{3,2,1,0:T(8,128)} %get-tuple-element.122), channel_id=1, source_target_pairs={{0,12},{4,8},{8,4},{12,0},{16,28},{20,24},{24,20},{28,16},{1,13},{... | collective-permute-start | bytes 4718600 | tf_op jit(solution)/shard_map/ppermute | solution.py:418
  479.3 101.4 %collective-permute-start.22 = (f32[3,16,64,128]{3,2,1,0:T(8,128)}, f32[3,16,64,128]{3,2,1,0:T(8,128)}, u32[]{:S(2)}, u32[]{:S(2)}) collective-permute-start(f32[3,16,64,128]{3,2,1,0:T(8,128)} %get-tuple-element.123), channel_id=1, source_target_pairs={{0,16},{4,20},{8,24},{12,28},{16,0},{20,4},{24,8},{28,12},{1,17},{... | collective-permute-start | bytes 4718600 | tf_op jit(solution)/shard_map/ppermute | solution.py:418
  514.4 67.4 %collective-permute-start.23 = (f32[3,16,64,128]{3,2,1,0:T(8,128)}, f32[3,16,64,128]{3,2,1,0:T(8,128)}, u32[]{:S(2)}, u32[]{:S(2)}) collective-permute-start(f32[3,16,64,128]{3,2,1,0:T(8,128)} %get-tuple-element.124), channel_id=1, source_target_pairs={{0,20},{4,16},{8,28},{12,24},{16,4},{20,0},{24,12},{28,8},{1,21},{... | collective-permute-start | bytes 4718600 | tf_op jit(solution)/shard_map/ppermute | solution.py:418
  516.7 98.4 %collective-permute-start.24 = (f32[3,16,64,128]{3,2,1,0:T(8,128)}, f32[3,16,64,128]{3,2,1,0:T(8,128)}, u32[]{:S(2)}, u32[]{:S(2)}) collective-permute-start(f32[3,16,64,128]{3,2,1,0:T(8,128)} %get-tuple-element.125), channel_id=1, source_target_pairs={{0,24},{4,28},{8,16},{12,20},{16,8},{20,12},{24,0},{28,4},{1,25},{... | collective-permute-start | bytes 4718600 | tf_op jit(solution)/shard_map/ppermute | solution.py:418
  652.6 283.0 %all-to-all-start.5 = ((f32[4,3,2080,128]{3,2,1,0:T(8,128)}), f32[4,3,2080,128]{3,2,1,0:T(8,128)}, u32[]{:S(2)}, u32[]{:S(2)}) async-start(f32[4,3,2080,128]{3,2,1,0:T(8,128)} %second.12), calls=%async_computation.5 | async-start | bytes 25559040 | tf_op jit(solution)/shard_map/all_to_all | solution.py:465
  660.6 79.9 %collective-permute-start.38 = (f32[3,12,64,128]{3,2,1,0:T(8,128)}, f32[3,12,64,128]{3,2,1,0:T(8,128)}, u32[]{:S(2)}, u32[]{:S(2)}) collective-permute-start(f32[3,12,64,128]{3,2,1,0:T(8,128)} %copy-done.47), channel_id=1, source_target_pairs={{0,8},{4,12},{8,0},{12,4},{16,24},{20,28},{24,16},{28,20},{1,9},{5... | collective-permute-start | bytes 3538952 | tf_op jit(solution)/shard_map/ppermute | solution.py:418
  661.2 79.3 %collective-permute-start.39 = (f32[3,12,64,128]{3,2,1,0:T(8,128)}, f32[3,12,64,128]{3,2,1,0:T(8,128)}, u32[]{:S(2)}, u32[]{:S(2)}) collective-permute-start(f32[3,12,64,128]{3,2,1,0:T(8,128)} %copy-done.46), channel_id=1, source_target_pairs={{0,12},{4,8},{8,4},{12,0},{16,28},{20,24},{24,20},{28,16},{1,13},{... | collective-permute-start | bytes 3538952 | tf_op jit(solution)/shard_map/ppermute | solution.py:418
  662.0 78.5 %collective-permute-start.40 = (f32[3,12,64,128]{3,2,1,0:T(8,128)}, f32[3,12,64,128]{3,2,1,0:T(8,128)}, u32[]{:S(2)}, u32[]{:S(2)}) collective-permute-start(f32[3,12,64,128]{3,2,1,0:T(8,128)} %copy-done.45), channel_id=1, source_target_pairs={{0,16},{4,20},{8,24},{12,28},{16,0},{20,4},{24,8},{28,12},{1,17},{... | collective-permute-start | bytes 3538952 | tf_op jit(solution)/shard_map/ppermute | solution.py:418
  689.4 51.1 %collective-permute-start.41 = (f32[3,12,64,128]{3,2,1,0:T(8,128)}, f32[3,12,64,128]{3,2,1,0:T(8,128)}, u32[]{:S(2)}, u32[]{:S(2)}) collective-permute-start(f32[3,12,64,128]{3,2,1,0:T(8,128)} %get-tuple-element.148), channel_id=1, source_target_pairs={{0,20},{4,16},{8,28},{12,24},{16,4},{20,0},{24,12},{28,8},{1,21},{... | collective-permute-start | bytes 3538952 | tf_op jit(solution)/shard_map/ppermute | solution.py:418
  691.2 71.7 %collective-permute-start.42 = (f32[3,12,64,128]{3,2,1,0:T(8,128)}, f32[3,12,64,128]{3,2,1,0:T(8,128)}, u32[]{:S(2)}, u32[]{:S(2)}) collective-permute-start(f32[3,12,64,128]{3,2,1,0:T(8,128)} %get-tuple-element.149), channel_id=1, source_target_pairs={{0,24},{4,28},{8,16},{12,20},{16,8},{20,12},{24,0},{28,4},{1,25},{... | collective-permute-start | bytes 3538952 | tf_op jit(solution)/shard_map/ppermute | solution.py:418
  935.6 215.1 %all-to-all-start.8 = ((f32[4,3,1568,128]{3,2,1,0:T(8,128)}), f32[4,3,1568,128]{3,2,1,0:T(8,128)}, u32[]{:S(2)}, u32[]{:S(2)}) async-start(f32[4,3,1568,128]{3,2,1,0:T(8,128)} %second.14.rest_2_), calls=%async_computation.8 | async-start | bytes 19267584 | tf_op jit(solution)/shard_map/all_to_all | solution.py:465
  944.8 58.5 %collective-permute-start.14 = (f32[3,4,64,128]{3,2,1,0:T(8,128)}, f32[3,4,64,128]{3,2,1,0:T(8,128)S(1)}, u32[]{:S(2)}, u32[]{:S(2)}) collective-permute-start(f32[3,4,64,128]{3,2,1,0:T(8,128)} %get-tuple-element.114), channel_id=1, source_target_pairs={{0,12},{4,8},{8,4},{12,0},{16,28},{20,24},{24,20},{28,16},{1,13},{... | collective-permute-start | bytes 1179656 | tf_op jit(solution)/shard_map/ppermute | solution.py:418
  945.0 58.3 %collective-permute-start.15 = (f32[3,4,64,128]{3,2,1,0:T(8,128)}, f32[3,4,64,128]{3,2,1,0:T(8,128)S(1)}, u32[]{:S(2)}, u32[]{:S(2)}) collective-permute-start(f32[3,4,64,128]{3,2,1,0:T(8,128)} %get-tuple-element.115), channel_id=1, source_target_pairs={{0,16},{4,20},{8,24},{12,28},{16,0},{20,4},{24,8},{28,12},{1,17},{... | collective-permute-start | bytes 1179656 | tf_op jit(solution)/shard_map/ppermute | solution.py:418
  946.1 57.1 %collective-permute-start.16 = (f32[3,4,64,128]{3,2,1,0:T(8,128)}, f32[3,4,64,128]{3,2,1,0:T(8,128)S(1)}, u32[]{:S(2)}, u32[]{:S(2)}) collective-permute-start(f32[3,4,64,128]{3,2,1,0:T(8,128)} %get-tuple-element.116), channel_id=1, source_target_pairs={{0,20},{4,16},{8,28},{12,24},{16,4},{20,0},{24,12},{28,8},{1,21},{... | collective-permute-start | bytes 1179656 | tf_op jit(solution)/shard_map/ppermute | solution.py:418
  953.5 49.7 %collective-permute-start.17 = (f32[3,4,64,128]{3,2,1,0:T(8,128)}, f32[3,4,64,128]{3,2,1,0:T(8,128)S(1)}, u32[]{:S(2)}, u32[]{:S(2)}) collective-permute-start(f32[3,4,64,128]{3,2,1,0:T(8,128)} %get-tuple-element.117), channel_id=1, source_target_pairs={{0,24},{4,28},{8,16},{12,20},{16,8},{20,12},{24,0},{28,4},{1,25},{... | collective-permute-start | bytes 1179656 | tf_op jit(solution)/shard_map/ppermute | solution.py:418
  958.4 44.8 %collective-permute-start.18 = (f32[3,4,64,128]{3,2,1,0:T(8,128)}, f32[3,4,64,128]{3,2,1,0:T(8,128)S(1)}, u32[]{:S(2)}, u32[]{:S(2)}) collective-permute-start(f32[3,4,64,128]{3,2,1,0:T(8,128)} %get-tuple-element.118), channel_id=1, source_target_pairs={{0,28},{4,24},{8,20},{12,16},{16,12},{20,8},{24,4},{28,0},{1,29},{... | collective-permute-start | bytes 1179656 | tf_op jit(solution)/shard_map/ppermute | solution.py:418
  1150.7 76.3 %all-to-all-start.7 = ((f32[4,3,520,128]{3,2,1,0:T(8,128)}), f32[4,3,520,128]{3,2,1,0:T(8,128)}, u32[]{:S(2)}, u32[]{:S(2)}) async-start(f32[4,3,520,128]{3,2,1,0:T(8,128)} %second.15.rest_2_), calls=%async_computation.7 | async-start | bytes 6389760 | tf_op jit(solution)/shard_map/all_to_all | solution.py:465
  (98 other events, 2309.3 us)

commit v5 on v4

--- a/solution.py
+++ b/solution.py
@@ -15,7 +15,7 @@
 VALUE_PARTS = (0, 0, 0, 1, 1, 2)
 VMEM_BYTES = 48 * 1024 * 1024
 SCALE = 1.0
-PATTERN = (6, 6, 10, 10, 16, 12)
+PATTERN = (6, 6, 10, 16, 22)
 LAST = 4
 
 
@@ -405,6 +405,8 @@
     pairs = [[(i, partner(i, step, rows)) for i in range(rows)] for step in range(rows)]
     ordered = ordered_blocks(jnp.asarray(first_table), 1, targets)
 
+    order = sorted(range(1, rows), key=lambda s: (-bin(s >> 1).count("1"), -(s & 1), -s))
+
     members = spectrum.shape[0]
     parts = [(0, range(0, 1)), (0, range(1, members))]
     parts += [(slab, range(0, members)) for slab in range(1, slabs)]
@@ -414,9 +416,9 @@
         outs = first_transform(
             spectrum, table, ordered, targets, chosen, starts[slab], widths[slab], after
         )
-        pieces[part] = [outs[0]] + [
-            lax.ppermute(outs[step], "row", pairs[step]) for step in range(1, rows)
-        ]
+        pieces[part] = [outs[0]] * rows
+        for step in order:
+            pieces[part][step] = lax.ppermute(outs[step], "row", pairs[step])
 
     pieces, arrived, levels, edges, halo = {}, {}, {}, {}, {}
     held = None
@@ -461,11 +463,15 @@
             after.append(levels[part - 3] if part >= 3 else arrived[0])
         if part + 1 < len(parts):
             after.append(pieces[part + 1][0])
+        elif part >= 4:
+            after.append(tokens[part - 4])
+            tokens[part - 3] = normals(part - 3, 0, widths[part - 3] - 1)
+            after.append(tokens[part - 3])
         spread = second(part, after)
         arrived[part] = lax.all_to_all(spread, "col", split_axis=0, concat_axis=0, tiled=True)
         after = [spread]
         if part + 2 < len(parts):
-            first(part + 2, (pieces[part + 1][rows - 1],))
+            first(part + 2, (pieces[part + 1][order[0]],))
             after = [pieces[part + 2][0]]
         if part >= 2:
             slab = part - 2
@@ -473,7 +479,8 @@
                 after.append(tokens[slab - 2])
             third(slab, after)
             if slab >= 2:
-                tokens[slab - 1] = normals(slab - 1)
+                done = widths[slab - 1] - 1 if part + 1 == len(parts) and part >= 4 else 0
+                tokens[slab - 1] = normals(slab - 1, done)
             elif slab == 1 and widths[0] > 1:
                 tokens[0] = normals(0, 1)
     after = [tokens[key] for key in sorted(tokens)[-1:]]

time: 1250 us -> 1240 us (level)
  waiting for transfers between devices: 639 us -> 653 us
    ppermute x49 -> x42, waiting for transfers between devices: 251 us -> 288 us  [first(): pieces[part][step] = lax.ppermute(outs[step], 'row', pairs[step])]
    all_to_all x8 -> x7, waiting for transfers between devices: 372 us -> 355 us  [body(): lax.all_to_all(spread, 'col', split_axis=0, concat_axis=0, tiled=True)]
    ppermute x49 -> x42, starting transfers between devices: 51.1 us -> 46.3 us  [first(): pieces[part][step] = lax.ppermute(outs[step], 'row', pairs[step])]
    all_to_all x8 -> x7, starting transfers between devices: 43.1 us -> 38.8 us  [body(): lax.all_to_all(spread, 'col', split_axis=0, concat_axis=0, tiled=True)]
    unnamed x147 -> x125, local copies, waits for them, and re-layouts: 28.3 us -> 24.4 us
    pallas_call x8 -> x7, Pallas kernels: 142 us -> 139 us  [first_transform(): pl.pallas_call(functools.partial(first_kernel, widths=parts, chunk=chunk)...]
    pallas_call x7 -> x6, Pallas kernels: 130 us -> 127 us  [third_transform(): pl.pallas_call(functools.partial(third_kernel, firsts=firsts, together=wi...]
    pallas_call x8 -> x7, Pallas kernels: 140 us -> 138 us  [second_transform(): pl.pallas_call(functools.partial(second_kernel, count=count, planes=width...]
  transfers between devices with their start and end apart: 60 -> 52, of which waited for: 25 -> 22; matrix products, arithmetic and copies ran while one was open for 1% -> 1% of each run, Pallas kernels for 35% -> 34%
where the time goes in v5:
time: 1240 us
  waiting for transfers between devices  653 us (53%)
  Pallas kernels  455 us (37%)
  starting transfers between devices  93.1 us (8%)
  local copies, waits for them, and re-layouts  32.8 us (3%)
    all_to_all x7, waiting for transfers between devices, body(): lax.all_to_all(spread, 'col', split_axis=0, concat_axis=0, tiled=True)  355 us
    ppermute x42, waiting for transfers between devices, first(): pieces[part][step] = lax.ppermute(outs[step], 'row', pairs[step])  288 us
    pallas_call x7, Pallas kernels, first_transform(): pl.pallas_call(functools.partial(first_kernel, widths=parts, chunk=chunk)...  139 us
    pallas_call x7, Pallas kernels, second_transform(): pl.pallas_call(functools.partial(second_kernel, count=count, planes=width...  138 us
    pallas_call x6, Pallas kernels, third_transform(): pl.pallas_call(functools.partial(third_kernel, firsts=firsts, together=wi...  127 us
    pallas_call x9, Pallas kernels, write_normals(): pl.pallas_call(functools.partial(normal_kernel, skip=skip), grid=(count,)...  50.7 us
    ppermute x42, starting transfers between devices, first(): pieces[part][step] = lax.ppermute(outs[step], 'row', pairs[step])  46.3 us
    all_to_all x7, starting transfers between devices, body(): lax.all_to_all(spread, 'col', split_axis=0, concat_axis=0, tiled=True)  38.8 us
  transfers between devices with their start and end apart: 52, of which 22 were waited for; matrix products, arithmetic and copies ran while one was open for 1% of the time, Pallas kernels for 34%

profile of v5, /device:TPU:0, one launch (start us, length us, event | category | flops | bytes accessed | tf_op | source)
XLA Modules:
  0.0 1235.2 jit_solution(2717478314196384497)
XLA Ops:
  15.6 13.0 %first.8 = (f32[2,6,64,128]{3,2,1,0:T(8,128)S(1)}, f32[2,6,64,128]{3,2,1,0:T(8,128)S(1)}, f32[2,6,64,128]{3,2,1,0:T(8,128)}, f32[2,6,64,128]{3,2,1,0:T(8,128)}, ...) custom-call(bf16[144,512]{1,0:T(8,128)(2,1)S(1)} %reshape.22.table_r, ...), custom_call_target="tpu_custom_call" | custom-call | bytes 54000000 | tf_op jit(solution)/shard_map/first/pallas_call | solution.py:130
  49.9 9.0 collective-permute-done.6.rest_0_.rest_7_
  61.6 18.3 %first.9 = (f32[3,6,64,128]{3,2,1,0:T(8,128)S(1)}, f32[3,6,64,128]{3,2,1,0:T(8,128)S(1)}, f32[3,6,64,128]{3,2,1,0:T(8,128)S(1)}, f32[3,6,64,128]{3,2,1,0:T(8,128...) custom-call(bf16[144,512]{1,0:T(8,128)(2,1)S(1)} %reshape.23.table_r, ...), custom_call_target="tpu_custom_call" | custom-call | bytes 54000000 | tf_op jit(solution)/shard_map/first/pallas_call | solution.py:130
  83.6 10.2 second.8
  104.5 11.7 collective-permute-done.7.rest_0_.rest_7_
  121.0 19.4 %first.10 = (f32[3,10,64,128]{3,2,1,0:T(8,128)S(1)}, f32[3,10,64,128]{3,2,1,0:T(8,128)S(1)}, f32[3,10,64,128]{3,2,1,0:T(8,128)}, f32[3,10,64,128]{3,2,1,0:T(8,12...) custom-call(bf16[240,512]{1,0:T(8,128)(2,1)S(1)} %reshape.25.table_r, ...), custom_call_target="tpu_custom_call" | custom-call | bytes 66000000 | tf_op jit(solution)/shard_map/first/pallas_call | solution.py:130
  142.1 12.4 %collective-permute-done.29.rest_6_ = f32[3,6,64,128]{3,2,1,0:T(8,128)} collective-permute-done((f32[3,6,64,128]{3,2,1,0:T(8,128)}, f32[3,6,64,128]{3,2,1,0:T(8,128)}, u32[]{:S(2)}, u32[]{:S(2)}) %collective-permute-start.29) | collective-permute-done | bytes 589856 | tf_op jit(solution)/shard_map/ppermute | solution.py:421
  154.5 13.8 %second.9 = f32[4,3,784,128]{3,2,1,0:T(8,128)} custom-call(s32[8]{0:T(128)S(1)} %stack.26.sources_ref, bf16[512,3072]{1,0:T(8,128)(2,1)} %constant.33.clone.table_ref, f32[3,6,64,128]{3,2,1,0:T(8,128)S(1)} %get-tuple-element.93.rest_8_.rest_0_, f32[3,6,64,128]{3,2,1,0:T(8,128)S(1)} %collective-permute-done.24.rest_1_, ...), custom_call_target="tpu_custom_call" | custom-call | bytes 39000000 | tf_op jit(solution)/shard_map/second/pallas_call | solution.py:213
  182.3 20.4 %collective-permute-done.8.rest_0_.rest_7_ = f32[3,10,64,128]{3,2,1,0:T(8,128)S(1)} collective-permute-done((f32[3,10,64,128]{3,2,1,0:T(8,128)S(1)}, f32[3,10,64,128]{3,2,1,0:T(8,128)S(1)}, u32[]{:S(2)}, u32[]{:S(2)}) %collective-permute-start.8) | collective-permute-done | bytes 983072 | tf_op jit(solution)/shard_map/ppermute | solution.py:421
  206.9 24.8 %first.11 = (f32[3,16,64,128]{3,2,1,0:T(8,128)S(1)}, f32[3,16,64,128]{3,2,1,0:T(8,128)S(1)}, f32[3,16,64,128]{3,2,1,0:T(8,128)}, f32[3,16,64,128]{3,2,1,0:T(8,12...) custom-call(bf16[384,512]{1,0:T(8,128)(2,1)S(1)} %bitcast.9, ...), custom_call_target="tpu_custom_call" | custom-call | bytes 84000000 | tf_op jit(solution)/shard_map/first/pallas_call | solution.py:130
  232.8 13.9 %third.6 = (f32[6,128,512]{2,1,0:T(8,128)S(1)}, f32[16,512]{1,0:T(8,128)S(1)}) custom-call(bf16[3072,512]{1,0:T(8,128)(2,1)} %constant.34.clone.table_ref, f32[4,1,784,128]{3,2,1,0:T(8,128)S(1)} %copy-done.14, f32[4,2,784,128]{3,2,1,0:T(8,128)} %all-to-all-done.2.rest_1_.rest_3_, f32[4,1,784,128]{3,2,1,0:T(8,128)S(1)} %copy-done.14, ...), custom_call_target="tpu_custom_call" | custom-call | bytes 39000000 | tf_op jit(solution)/shard_map/third/pallas_call | solution.py:292
  247.9 17.7 %collective-permute-done.41.rest_6_ = f32[3,10,64,128]{3,2,1,0:T(8,128)S(1)} collective-permute-done((f32[3,10,64,128]{3,2,1,0:T(8,128)}, f32[3,10,64,128]{3,2,1,0:T(8,128)S(1)}, u32[]{:S(2)}, u32[]{:S(2)}) %collective-permute-start.41) | collective-permute-done | bytes 983072 | tf_op jit(solution)/shard_map/ppermute | solution.py:421
  266.6 20.9 %second.11 = f32[4,3,1312,128]{3,2,1,0:T(8,128)} custom-call(s32[8]{0:T(128)S(1)} %stack.26.sources_ref, bf16[512,3072]{1,0:T(8,128)(2,1)} %constant.33.clone.table_ref, f32[3,10,64,128]{3,2,1,0:T(8,128)S(1)} %get-tuple-element.120.rest_9_.rest_0_, f32[3,10,64,128]{3,2,1,0:T(8,128)S(1)} %collective-permute-done.36.rest_1_, ...), custom_call_target="tpu_custom_call" | custom-call | bytes 63000000 | tf_op jit(solution)/shard_map/second/pallas_call | solution.py:213
  298.4 32.6 %collective-permute-done.9.rest_0_.rest_7_ = f32[3,16,64,128]{3,2,1,0:T(8,128)S(1)} collective-permute-done((f32[3,16,64,128]{3,2,1,0:T(8,128)}, f32[3,16,64,128]{3,2,1,0:T(8,128)S(1)}, u32[]{:S(2)}, u32[]{:S(2)}) %collective-permute-start.9) | collective-permute-done | bytes 1572896 | tf_op jit(solution)/shard_map/ppermute | solution.py:421
  339.7 37.9 %first.12 = (f32[3,22,64,128]{3,2,1,0:T(8,128)S(1)}, f32[3,22,64,128]{3,2,1,0:T(8,128)}, f32[3,22,64,128]{3,2,1,0:T(8,128)}, f32[3,22,64,128]{3,2,1,0:T(8,128)},...) custom-call(bf16[528,512]{1,0:T(8,128)(2,1)S(1)} %reshape.27.table_r, ...), custom_call_target="tpu_custom_call" | custom-call | bytes 102000000 | tf_op jit(solution)/shard_map/first/pallas_call | solution.py:130
  377.7 14.0 %third.7 = (f32[6,128,512]{2,1,0:T(8,128)S(1)}, f32[16,512]{1,0:T(8,128)S(1)}) custom-call(bf16[3072,512]{1,0:T(8,128)(2,1)} %constant.34.clone.table_ref, f32[4,3,784,128]{3,2,1,0:T(8,128)} %all-to-all-done.3.rest_0_.rest_1_, f32[4,3,784,128]{3,2,1,0:T(8,128)} %all-to-all-done.3.rest_0_.rest_1_, ...), custom_call_target="tpu_custom_call" | custom-call | bytes 39000000 | tf_op jit(solution)/shard_map/third/pallas_call | solution.py:292
  399.3 33.3 %collective-permute-done.23.rest_6_ = f32[3,16,64,128]{3,2,1,0:T(8,128)} collective-permute-done((f32[3,16,64,128]{3,2,1,0:T(8,128)}, f32[3,16,64,128]{3,2,1,0:T(8,128)}, u32[]{:S(2)}, u32[]{:S(2)}) %collective-permute-start.23) | collective-permute-done | bytes 1572896 | tf_op jit(solution)/shard_map/ppermute | solution.py:421
  432.6 33.0 %second.10 = f32[4,3,2080,128]{3,2,1,0:T(8,128)} custom-call(s32[8]{0:T(128)S(1)} %stack.26.sources_ref, bf16[512,3072]{1,0:T(8,128)(2,1)} %constant.33.clone.table_ref, f32[3,16,64,128]{3,2,1,0:T(8,128)S(1)} %copy-done.21, f32[3,16,64,128]{3,2,1,0:T(8,128)S(1)} %copy-done.29, f32[3,16,64,128]{3,2,1,0:T(8,128)} %collective-permute-done.19.rest_2_, ...), custom_call_target="tpu_custom_call" | custom-call | bytes 99000000 | tf_op jit(solution)/shard_map/second/pallas_call | solution.py:213
  481.4 45.6 %collective-permute-done.10.rest_0_.rest_7_ = f32[3,22,64,128]{3,2,1,0:T(8,128)S(1)} collective-permute-done((f32[3,22,64,128]{3,2,1,0:T(8,128)}, f32[3,22,64,128]{3,2,1,0:T(8,128)S(1)}, u32[]{:S(2)}, u32[]{:S(2)}) %collective-permute-start.10) | collective-permute-done | bytes 2162720 | tf_op jit(solution)/shard_map/ppermute | solution.py:421
  532.3 17.9 %first.13 = (f32[3,4,64,128]{3,2,1,0:T(8,128)S(1)}, f32[3,4,64,128]{3,2,1,0:T(8,128)}, f32[3,4,64,128]{3,2,1,0:T(8,128)}, f32[3,4,64,128]{3,2,1,0:T(8,128)}, f32...) custom-call(bf16[96,512]{1,0:T(8,128)(2,1)S(1)} %reshape.26.table_re, ...), custom_call_target="tpu_custom_call" | custom-call | bytes 48000000 | tf_op jit(solution)/shard_map/first/pallas_call | solution.py:130
  553.8 20.3 %third.8 = (f32[10,128,512]{2,1,0:T(8,128)S(1)}, f32[32,512]{1,0:T(8,128)S(1)}) custom-call(bf16[3072,512]{1,0:T(8,128)(2,1)} %constant.34.clone.table_ref, f32[4,3,1312,128]{3,2,1,0:T(8,128)} %all-to-all-done.5.rest_0_.rest_1_, f32[4,3,1312,128]{3,2,1,0:T(8,128)} %all-to-all-done.5.rest_0_.rest_1_, ...), custom_call_target="tpu_custom_call" | custom-call | bytes 63000000 | tf_op jit(solution)/shard_map/third/pallas_call | solution.py:292
  576.3 43.2 %collective-permute-done.32.rest_3_ = f32[3,22,64,128]{3,2,1,0:T(8,128)} collective-permute-done((f32[3,22,64,128]{3,2,1,0:T(8,128)}, f32[3,22,64,128]{3,2,1,0:T(8,128)}, u32[]{:S(2)}, u32[]{:S(2)}) %collective-permute-start.32) | collective-permute-done | bytes 2162720 | tf_op jit(solution)/shard_map/ppermute | solution.py:421
  619.8 45.9 %collective-permute-done.35.rest_6_ = f32[3,22,64,128]{3,2,1,0:T(8,128)} collective-permute-done((f32[3,22,64,128]{3,2,1,0:T(8,128)}, f32[3,22,64,128]{3,2,1,0:T(8,128)}, u32[]{:S(2)}, u32[]{:S(2)}) %collective-permute-start.35) | collective-permute-done | bytes 2162720 | tf_op jit(solution)/shard_map/ppermute | solution.py:421
  665.7 44.6 %second.12.rest_2_ = f32[4,3,2880,128]{3,2,1,0:T(8,128)} custom-call(s32[8]{0:T(128)S(1)} %stack.26.sources_ref, bf16[512,3072]{1,0:T(8,128)(2,1)} %constant.33.clone.table_ref, f32[3,22,64,128]{3,2,1,0:T(8,128)S(1)} %copy-done.19, f32[3,22,64,128]{3,2,1,0:T(8,128)S(1)} %copy-done.27, f32[3,22,64,128]{3,2,1,0:T(8,128)} %collective-permute-done.31.rest_2_, ...), custom_call_target="tpu_custom_call" | custom-call | bytes 135000000 | tf_op jit(solution)/shard_map/second/pallas_call | solution.py:213
  710.2 43.4 %all-to-all-done.4.rest_0_.rest_1_ = f32[4,3,2080,128]{3,2,1,0:T(8,128)} async-done(((f32[4,3,2080,128]{3,2,1,0:T(8,128)}), f32[4,3,2080,128]{3,2,1,0:T(8,128)}, u32[]{:S(2)}, u32[]{:S(2)}) %all-to-all-start.4) | async-done | bytes 12779552 | tf_op jit(solution)/shard_map/all_to_all | solution.py:471
  773.5 30.7 %third.9 = (f32[16,128,512]{2,1,0:T(8,128)}, f32[32,512]{1,0:T(8,128)S(1)}) custom-call(bf16[3072,512]{1,0:T(8,128)(2,1)S(1)} %copy-done.3, f32[4,3,2080,128]{3,2,1,0:T(8,128)} %all-to-all-done.4.rest_0_.rest_1_, f32[4,3,2080,128]{3,2,1,0:T(8,128)} %all-to-all-done.4.rest_0_.rest_1_, f32[4,3,2880,128]{3,2,1,0:T(8,128)} %second.12.rest_2_, ...), custom_call_target="tpu_custom_call" | custom-call | bytes 99000000 | tf_op jit(solution)/shard_map/third/pallas_call | solution.py:292
  824.3 9.7 normals.12
  842.4 9.5 second.13.rest_2_
  851.9 291.0 %all-to-all-done.7.rest_0_.rest_1_ = f32[4,3,2880,128]{3,2,1,0:T(8,128)} async-done(((f32[4,3,2880,128]{3,2,1,0:T(8,128)}), f32[4,3,2880,128]{3,2,1,0:T(8,128)}, u32[]{:S(2)}, u32[]{:S(2)}) %all-to-all-start.7) | async-done | bytes 17694752 | tf_op jit(solution)/shard_map/all_to_all | solution.py:471
  1147.8 41.1 %third.10 = (f32[22,128,512]{2,1,0:T(8,128)}, f32[64,512]{1,0:T(8,128)S(1)}) custom-call(bf16[3072,512]{1,0:T(8,128)(2,1)S(1)} %copy-done.3, f32[4,3,2880,128]{3,2,1,0:T(8,128)} %all-to-all-done.7.rest_0_.rest_1_, f32[4,3,2880,128]{3,2,1,0:T(8,128)} %all-to-all-done.7.rest_0_.rest_1_, f32[4,3,520,128]{3,2,1,0:T(8,128)} %second.13.rest_2_, ...), custom_call_target="tpu_custom_call" | custom-call | bytes 135000000 | tf_op jit(solution)/shard_map/third/pallas_call | solution.py:292
  1191.1 15.7 %normals.14 = (f32[64,128,512]{2,1,0:T(8,128)}, bf16[3,64,128,512]{3,2,1,0:T(8,128)(2,1)}, f32[8,128]{1,0:T(8,128)S(1)}) custom-call(f32[22,128,512]{2,1,0:T(8,128)} %get-tuple-element.151.behind_ref.centre_ref.before_ref, f32[16,128,512]{2,1,0:T(8,128)S(1)} %copy-done.1, ...), custom_call_target="tpu_custom_call", output_to_operand_aliasing={{0}: (4, {}), {1}: (5, {})} | custom-call | bytes 34500000 | tf_op jit(solution)/shard_map/normals/pallas_call | solution.py:342
  1206.8 12.0 all-to-all-done.6.rest_0_.rest_1_
  (241 shorter events, 206.6 us)
Async XLA Ops:
  41.4 52.4 %all-to-all-start.1 = ((f32[4,1,784,128]{3,2,1,0:T(8,128)}), f32[4,1,784,128]{3,2,1,0:T(8,128)S(1)}, u32[]{:S(2)}, u32[]{:S(2)}) async-start(f32[4,1,784,128]{3,2,1,0:T(8,128)} %second.7), calls=%async_computation.1 | async-start | bytes 3211264 | tf_op jit(solution)/shard_map/all_to_all | solution.py:471
  95.0 77.7 %all-to-all-start.2 = ((f32[4,2,784,128]{3,2,1,0:T(8,128)}), f32[4,2,784,128]{3,2,1,0:T(8,128)}, u32[]{:S(2)}, u32[]{:S(2)}) async-start(f32[4,2,784,128]{3,2,1,0:T(8,128)} %second.8), calls=%async_computation.2 | async-start | bytes 6422528 | tf_op jit(solution)/shard_map/all_to_all | solution.py:471
  101.6 39.9 %collective-permute-start.25 = (f32[3,6,64,128]{3,2,1,0:T(8,128)}, f32[3,6,64,128]{3,2,1,0:T(8,128)}, u32[]{:S(2)}, u32[]{:S(2)}) collective-permute-start(f32[3,6,64,128]{3,2,1,0:T(8,128)} %copy-done.49), channel_id=1, source_target_pairs={{0,8},{4,12},{8,0},{12,4},{16,24},{20,28},{24,16},{28,20},{1,9},{5... | collective-permute-start | bytes 1769480 | tf_op jit(solution)/shard_map/ppermute | solution.py:421
  102.3 39.1 %collective-permute-start.26 = (f32[3,6,64,128]{3,2,1,0:T(8,128)}, f32[3,6,64,128]{3,2,1,0:T(8,128)}, u32[]{:S(2)}, u32[]{:S(2)}) collective-permute-start(f32[3,6,64,128]{3,2,1,0:T(8,128)} %copy-done.48), channel_id=1, source_target_pairs={{0,12},{4,8},{8,4},{12,0},{16,28},{20,24},{24,20},{28,16},{1,13},{... | collective-permute-start | bytes 1769480 | tf_op jit(solution)/shard_map/ppermute | solution.py:421
  103.0 38.5 %collective-permute-start.27 = (f32[3,6,64,128]{3,2,1,0:T(8,128)}, f32[3,6,64,128]{3,2,1,0:T(8,128)}, u32[]{:S(2)}, u32[]{:S(2)}) collective-permute-start(f32[3,6,64,128]{3,2,1,0:T(8,128)} %copy-done.47), channel_id=1, source_target_pairs={{0,16},{4,20},{8,24},{12,28},{16,0},{20,4},{24,8},{28,12},{1,17},{... | collective-permute-start | bytes 1769480 | tf_op jit(solution)/shard_map/ppermute | solution.py:421
  172.7 114.9 %all-to-all-start.3 = ((f32[4,3,784,128]{3,2,1,0:T(8,128)}), f32[4,3,784,128]{3,2,1,0:T(8,128)}, u32[]{:S(2)}, u32[]{:S(2)}) async-start(f32[4,3,784,128]{3,2,1,0:T(8,128)} %second.9), calls=%async_computation.3 | async-start | bytes 9633792 | tf_op jit(solution)/shard_map/all_to_all | solution.py:471
  179.4 68.5 %collective-permute-start.37 = (f32[3,10,64,128]{3,2,1,0:T(8,128)}, f32[3,10,64,128]{3,2,1,0:T(8,128)S(1)}, u32[]{:S(2)}, u32[]{:S(2)}) collective-permute-start(f32[3,10,64,128]{3,2,1,0:T(8,128)} %get-tuple-element.130), channel_id=1, source_target_pairs={{0,8},{4,12},{8,0},{12,4},{16,24},{20,28},{24,16},{28,20},{1,9},{5... | collective-permute-start | bytes 2949128 | tf_op jit(solution)/shard_map/ppermute | solution.py:421
  180.0 67.9 %collective-permute-start.38 = (f32[3,10,64,128]{3,2,1,0:T(8,128)}, f32[3,10,64,128]{3,2,1,0:T(8,128)S(1)}, u32[]{:S(2)}, u32[]{:S(2)}) collective-permute-start(f32[3,10,64,128]{3,2,1,0:T(8,128)} %get-tuple-element.131), channel_id=1, source_target_pairs={{0,12},{4,8},{8,4},{12,0},{16,28},{20,24},{24,20},{28,16},{1,13},{... | collective-permute-start | bytes 2949128 | tf_op jit(solution)/shard_map/ppermute | solution.py:421
  180.7 67.2 %collective-permute-start.39 = (f32[3,10,64,128]{3,2,1,0:T(8,128)}, f32[3,10,64,128]{3,2,1,0:T(8,128)S(1)}, u32[]{:S(2)}, u32[]{:S(2)}) collective-permute-start(f32[3,10,64,128]{3,2,1,0:T(8,128)} %get-tuple-element.132), channel_id=1, source_target_pairs={{0,16},{4,20},{8,24},{12,28},{16,0},{20,4},{24,8},{28,12},{1,17},{... | collective-permute-start | bytes 2949128 | tf_op jit(solution)/shard_map/ppermute | solution.py:421
  202.7 45.2 %collective-permute-start.40 = (f32[3,10,64,128]{3,2,1,0:T(8,128)}, f32[3,10,64,128]{3,2,1,0:T(8,128)S(1)}, u32[]{:S(2)}, u32[]{:S(2)}) collective-permute-start(f32[3,10,64,128]{3,2,1,0:T(8,128)} %get-tuple-element.133), channel_id=1, source_target_pairs={{0,20},{4,16},{8,28},{12,24},{16,4},{20,0},{24,12},{28,8},{1,21},{... | collective-permute-start | bytes 2949128 | tf_op jit(solution)/shard_map/ppermute | solution.py:421
  203.3 62.4 %collective-permute-start.41 = (f32[3,10,64,128]{3,2,1,0:T(8,128)}, f32[3,10,64,128]{3,2,1,0:T(8,128)S(1)}, u32[]{:S(2)}, u32[]{:S(2)}) collective-permute-start(f32[3,10,64,128]{3,2,1,0:T(8,128)} %get-tuple-element.134), channel_id=1, source_target_pairs={{0,24},{4,28},{8,16},{12,20},{16,8},{20,12},{24,0},{28,4},{1,25},{... | collective-permute-start | bytes 2949128 | tf_op jit(solution)/shard_map/ppermute | solution.py:421
  287.6 182.6 %all-to-all-start.5 = ((f32[4,3,1312,128]{3,2,1,0:T(8,128)}), f32[4,3,1312,128]{3,2,1,0:T(8,128)}, u32[]{:S(2)}, u32[]{:S(2)}) async-start(f32[4,3,1312,128]{3,2,1,0:T(8,128)} %second.11), calls=%async_computation.5 | async-start | bytes 16121856 | tf_op jit(solution)/shard_map/all_to_all | solution.py:471
  293.5 37.5 %collective-permute-start.9 = (f32[3,16,64,128]{3,2,1,0:T(8,128)}, f32[3,16,64,128]{3,2,1,0:T(8,128)S(1)}, u32[]{:S(2)}, u32[]{:S(2)}) collective-permute-start(f32[3,16,64,128]{3,2,1,0:T(8,128)} %get-tuple-element.98), channel_id=1, source_target_pairs={{0,28},{4,24},{8,20},{12,16},{16,12},{20,8},{24,4},{28,0},{1,29},{... | collective-permute-start | bytes 4718600 | tf_op jit(solution)/shard_map/ppermute | solution.py:421
  294.7 38.9 %collective-permute-start.18 = (f32[3,16,64,128]{3,2,1,0:T(8,128)S(1)}, f32[3,16,64,128]{3,2,1,0:T(8,128)S(1)}, u32[]{:S(2)}, u32[]{:S(2)}) collective-permute-start(f32[3,16,64,128]{3,2,1,0:T(8,128)S(1)} %copy-done.42), channel_id=1, source_target_pairs={{0,4},{4,0},{8,12},{12,8},{16,20},{20,16},{24,28},{28,24},{1,5},{5... | collective-permute-start | bytes 4718600 | tf_op jit(solution)/shard_map/ppermute | solution.py:421
  294.7 98.1 %collective-permute-start.19 = (f32[3,16,64,128]{3,2,1,0:T(8,128)}, f32[3,16,64,128]{3,2,1,0:T(8,128)}, u32[]{:S(2)}, u32[]{:S(2)}) collective-permute-start(f32[3,16,64,128]{3,2,1,0:T(8,128)} %get-tuple-element.109), channel_id=1, source_target_pairs={{0,8},{4,12},{8,0},{12,4},{16,24},{20,28},{24,16},{28,20},{1,9},{5... | collective-permute-start | bytes 4718600 | tf_op jit(solution)/shard_map/ppermute | solution.py:421
  296.1 102.0 %collective-permute-start.20 = (f32[3,16,64,128]{3,2,1,0:T(8,128)}, f32[3,16,64,128]{3,2,1,0:T(8,128)}, u32[]{:S(2)}, u32[]{:S(2)}) collective-permute-start(f32[3,16,64,128]{3,2,1,0:T(8,128)} %get-tuple-element.110), channel_id=1, source_target_pairs={{0,12},{4,8},{8,4},{12,0},{16,28},{20,24},{24,20},{28,16},{1,13},{... | collective-permute-start | bytes 4718600 | tf_op jit(solution)/shard_map/ppermute | solution.py:421
  296.6 101.6 %collective-permute-start.21 = (f32[3,16,64,128]{3,2,1,0:T(8,128)}, f32[3,16,64,128]{3,2,1,0:T(8,128)}, u32[]{:S(2)}, u32[]{:S(2)}) collective-permute-start(f32[3,16,64,128]{3,2,1,0:T(8,128)} %get-tuple-element.111), channel_id=1, source_target_pairs={{0,16},{4,20},{8,24},{12,28},{16,0},{20,4},{24,8},{28,12},{1,17},{... | collective-permute-start | bytes 4718600 | tf_op jit(solution)/shard_map/ppermute | solution.py:421
  332.1 67.2 %collective-permute-start.22 = (f32[3,16,64,128]{3,2,1,0:T(8,128)}, f32[3,16,64,128]{3,2,1,0:T(8,128)}, u32[]{:S(2)}, u32[]{:S(2)}) collective-permute-start(f32[3,16,64,128]{3,2,1,0:T(8,128)} %get-tuple-element.112), channel_id=1, source_target_pairs={{0,20},{4,16},{8,28},{12,24},{16,4},{20,0},{24,12},{28,8},{1,21},{... | collective-permute-start | bytes 4718600 | tf_op jit(solution)/shard_map/ppermute | solution.py:421
  334.8 97.8 %collective-permute-start.23 = (f32[3,16,64,128]{3,2,1,0:T(8,128)}, f32[3,16,64,128]{3,2,1,0:T(8,128)}, u32[]{:S(2)}, u32[]{:S(2)}) collective-permute-start(f32[3,16,64,128]{3,2,1,0:T(8,128)} %get-tuple-element.113), channel_id=1, source_target_pairs={{0,24},{4,28},{8,16},{12,20},{16,8},{20,12},{24,0},{28,4},{1,25},{... | collective-permute-start | bytes 4718600 | tf_op jit(solution)/shard_map/ppermute | solution.py:421
  470.2 283.5 %all-to-all-start.4 = ((f32[4,3,2080,128]{3,2,1,0:T(8,128)}), f32[4,3,2080,128]{3,2,1,0:T(8,128)}, u32[]{:S(2)}, u32[]{:S(2)}) async-start(f32[4,3,2080,128]{3,2,1,0:T(8,128)} %second.10), calls=%async_computation.4 | async-start | bytes 25559040 | tf_op jit(solution)/shard_map/all_to_all | solution.py:471
  476.5 50.6 %collective-permute-start.10 = (f32[3,22,64,128]{3,2,1,0:T(8,128)}, f32[3,22,64,128]{3,2,1,0:T(8,128)S(1)}, u32[]{:S(2)}, u32[]{:S(2)}) collective-permute-start(f32[3,22,64,128]{3,2,1,0:T(8,128)} %get-tuple-element.99), channel_id=1, source_target_pairs={{0,28},{4,24},{8,20},{12,16},{16,12},{20,8},{24,4},{28,0},{1,29},{... | collective-permute-start | bytes 6488072 | tf_op jit(solution)/shard_map/ppermute | solution.py:421
  477.2 50.6 %collective-permute-start.30 = (f32[3,22,64,128]{3,2,1,0:T(8,128)}, f32[3,22,64,128]{3,2,1,0:T(8,128)S(1)}, u32[]{:S(2)}, u32[]{:S(2)}) collective-permute-start(f32[3,22,64,128]{3,2,1,0:T(8,128)} %get-tuple-element.123), channel_id=1, source_target_pairs={{0,4},{4,0},{8,12},{12,8},{16,20},{20,16},{24,28},{28,24},{1,5},{5... | collective-permute-start | bytes 6488072 | tf_op jit(solution)/shard_map/ppermute | solution.py:421
  477.9 98.4 %collective-permute-start.31 = (f32[3,22,64,128]{3,2,1,0:T(8,128)}, f32[3,22,64,128]{3,2,1,0:T(8,128)}, u32[]{:S(2)}, u32[]{:S(2)}) collective-permute-start(f32[3,22,64,128]{3,2,1,0:T(8,128)} %get-tuple-element.124), channel_id=1, source_target_pairs={{0,8},{4,12},{8,0},{12,4},{16,24},{20,28},{24,16},{28,20},{1,9},{5... | collective-permute-start | bytes 6488072 | tf_op jit(solution)/shard_map/ppermute | solution.py:421
  479.3 140.2 %collective-permute-start.32 = (f32[3,22,64,128]{3,2,1,0:T(8,128)}, f32[3,22,64,128]{3,2,1,0:T(8,128)}, u32[]{:S(2)}, u32[]{:S(2)}) collective-permute-start(f32[3,22,64,128]{3,2,1,0:T(8,128)} %get-tuple-element.125), channel_id=1, source_target_pairs={{0,12},{4,8},{8,4},{12,0},{16,28},{20,24},{24,20},{28,16},{1,13},{... | collective-permute-start | bytes 6488072 | tf_op jit(solution)/shard_map/ppermute | solution.py:421
  479.3 140.2 %collective-permute-start.33 = (f32[3,22,64,128]{3,2,1,0:T(8,128)}, f32[3,22,64,128]{3,2,1,0:T(8,128)}, u32[]{:S(2)}, u32[]{:S(2)}) collective-permute-start(f32[3,22,64,128]{3,2,1,0:T(8,128)} %get-tuple-element.126), channel_id=1, source_target_pairs={{0,16},{4,20},{8,24},{12,28},{16,0},{20,4},{24,8},{28,12},{1,17},{... | collective-permute-start | bytes 6488072 | tf_op jit(solution)/shard_map/ppermute | solution.py:421
  527.0 92.7 %collective-permute-start.34 = (f32[3,22,64,128]{3,2,1,0:T(8,128)}, f32[3,22,64,128]{3,2,1,0:T(8,128)}, u32[]{:S(2)}, u32[]{:S(2)}) collective-permute-start(f32[3,22,64,128]{3,2,1,0:T(8,128)} %get-tuple-element.127), channel_id=1, source_target_pairs={{0,20},{4,16},{8,28},{12,24},{16,4},{20,0},{24,12},{28,8},{1,21},{... | collective-permute-start | bytes 6488072 | tf_op jit(solution)/shard_map/ppermute | solution.py:421
  529.1 136.5 %collective-permute-start.35 = (f32[3,22,64,128]{3,2,1,0:T(8,128)}, f32[3,22,64,128]{3,2,1,0:T(8,128)}, u32[]{:S(2)}, u32[]{:S(2)}) collective-permute-start(f32[3,22,64,128]{3,2,1,0:T(8,128)} %get-tuple-element.128), channel_id=1, source_target_pairs={{0,24},{4,28},{8,16},{12,20},{16,8},{20,12},{24,0},{28,4},{1,25},{... | collective-permute-start | bytes 6488072 | tf_op jit(solution)/shard_map/ppermute | solution.py:421
  753.7 389.2 %all-to-all-start.7 = ((f32[4,3,2880,128]{3,2,1,0:T(8,128)}), f32[4,3,2880,128]{3,2,1,0:T(8,128)}, u32[]{:S(2)}, u32[]{:S(2)}) async-start(f32[4,3,2880,128]{3,2,1,0:T(8,128)} %second.12.rest_2_), calls=%async_computation.7 | async-start | bytes 35389440 | tf_op jit(solution)/shard_map/all_to_all | solution.py:471
  760.9 47.0 %collective-permute-start.11 = (f32[3,4,64,128]{3,2,1,0:T(8,128)}, f32[3,4,64,128]{3,2,1,0:T(8,128)S(1)}, u32[]{:S(2)}, u32[]{:S(2)}) collective-permute-start(f32[3,4,64,128]{3,2,1,0:T(8,128)} %get-tuple-element.101), channel_id=1, source_target_pairs={{0,4},{4,0},{8,12},{12,8},{16,20},{20,16},{24,28},{28,24},{1,5},{5... | collective-permute-start | bytes 1179656 | tf_op jit(solution)/shard_map/ppermute | solution.py:421
  760.9 47.5 %collective-permute-start.12 = (f32[3,4,64,128]{3,2,1,0:T(8,128)}, f32[3,4,64,128]{3,2,1,0:T(8,128)S(1)}, u32[]{:S(2)}, u32[]{:S(2)}) collective-permute-start(f32[3,4,64,128]{3,2,1,0:T(8,128)} %get-tuple-element.102), channel_id=1, source_target_pairs={{0,8},{4,12},{8,0},{12,4},{16,24},{20,28},{24,16},{28,20},{1,9},{5... | collective-permute-start | bytes 1179656 | tf_op jit(solution)/shard_map/ppermute | solution.py:421
  763.9 44.5 %collective-permute-start.43 = (f32[1,128,512]{2,1,0:T(8,128)S(1)}, f32[1,128,512]{2,1,0:T(8,128)S(1)}, u32[]{:S(2)}, u32[]{:S(2)}) collective-permute-start(f32[1,128,512]{2,1,0:T(8,128)S(1)} %slice.31), channel_id=1, source_target_pairs={{0,4},{4,8},{8,12},{12,16},{16,20},{20,24},{24,28},{28,0},{1,5},{5... | collective-permute-start | bytes 786440 | tf_op jit(solution)/shard_map/ppermute | solution.py:447
  1142.9 75.9 %all-to-all-start.6 = ((f32[4,3,520,128]{3,2,1,0:T(8,128)}), f32[4,3,520,128]{3,2,1,0:T(8,128)}, u32[]{:S(2)}, u32[]{:S(2)}) async-start(f32[4,3,520,128]{3,2,1,0:T(8,128)} %second.13.rest_2_), calls=%async_computation.6 | async-start | bytes 6389760 | tf_op jit(solution)/shard_map/all_to_all | solution.py:471
  (79 other events, 1822.4 us)

commit v6 on v5

--- a/solution.py
+++ b/solution.py
@@ -310,7 +310,7 @@
     )(stacked, *received, *received, *after)
 
 
-def normal_kernel(centre_ref, before_ref, behind_ref, edge_ref, *rest, skip):
+def normal_kernel(centre_ref, before_ref, behind_ref, edge_ref, *rest, skip, base):
     level_ref, normal_ref, token_ref = rest[-3:]
     width, span_y, length = centre_ref.shape
     i = pl.program_id(0) + skip
@@ -318,9 +318,9 @@
     before = jnp.where(i == 0, before_ref[0], centre_ref[jnp.maximum(i - 1, 0)])
     behind = jnp.where(i == width - 1, behind_ref[0], centre_ref[jnp.minimum(i + 1, width - 1)])
     row = lax.broadcasted_iota(jnp.int32, (span_y, length), 0)
-    left = jnp.where(row == 0, edge_ref[pl.ds(2 * i, 1), :], pltpu.roll(centre, 1, 0))
+    left = jnp.where(row == 0, edge_ref[pl.ds(2 * (base + i), 1), :], pltpu.roll(centre, 1, 0))
     right = jnp.where(
-        row == span_y - 1, edge_ref[pl.ds(2 * i + 1, 1), :], pltpu.roll(centre, span_y - 1, 0)
+        row == span_y - 1, edge_ref[pl.ds(2 * (base + i) + 1, 1), :], pltpu.roll(centre, span_y - 1, 0)
     )
     step_x = 0.5 * (behind - before)
     step_y = 0.5 * (right - left)
@@ -336,14 +336,19 @@
 
 def write_normals(centre, before, behind, edge, skip, count, first, whole, held):
     width, span_y, length = centre.shape
+    span, base = width, 0
+    if count == 1:
+        span, base = 1, skip
+        before = (centre, skip - 1) if skip else before
+        behind = (centre, skip + 1) if skip < width - 1 else behind
     before, before_at = before
     behind, behind_at = behind
     held = () if held is None else held
     return pl.pallas_call(
-        functools.partial(normal_kernel, skip=skip),
+        functools.partial(normal_kernel, skip=skip - base, base=base),
         grid=(count,),
         in_specs=[
-            pl.BlockSpec((width, span_y, length), lambda i: (0, 0, 0)),
+            pl.BlockSpec((span, span_y, length), lambda i: (base, 0, 0)),
             pl.BlockSpec((1, span_y, length), lambda i: (before_at, 0, 0)),
             pl.BlockSpec((1, span_y, length), lambda i: (behind_at, 0, 0)),
             pl.BlockSpec(edge.shape, lambda i: (0, 0)),

time: 1240 us -> 1240 us (level)
    unnamed x125 -> x119, local copies, waits for them, and re-layouts: 24.4 us -> 25 us
where the time goes in v6:
time: 1240 us; the launch traced here: 1230 us
  waiting for transfers between devices  653 us (53%)
  Pallas kernels  453 us (37%)
  starting transfers between devices  92.3 us (7%)
  local copies, waits for them, and re-layouts  33.5 us (3%)
    all_to_all x7, waiting for transfers between devices, body(): lax.all_to_all(spread, 'col', split_axis=0, concat_axis=0, tiled=True)  356 us
    ppermute x42, waiting for transfers between devices, first(): pieces[part][step] = lax.ppermute(outs[step], 'row', pairs[step])  289 us
    pallas_call x7, Pallas kernels, first_transform(): pl.pallas_call(functools.partial(first_kernel, widths=parts, chunk=chunk)...  139 us
    pallas_call x7, Pallas kernels, second_transform(): pl.pallas_call(functools.partial(second_kernel, count=count, planes=width...  138 us
    pallas_call x6, Pallas kernels, third_transform(): pl.pallas_call(functools.partial(third_kernel, firsts=firsts, together=wi...  127 us
    pallas_call x9, Pallas kernels, write_normals(): pl.pallas_call(functools.partial(normal_kernel, skip=skip - base, base=ba...  48.9 us
    ppermute x42, starting transfers between devices, first(): pieces[part][step] = lax.ppermute(outs[step], 'row', pairs[step])  45.4 us
    all_to_all x7, starting transfers between devices, body(): lax.all_to_all(spread, 'col', split_axis=0, concat_axis=0, tiled=True)  38.8 us
  transfers between devices with their start and end apart: 52, of which 22 were waited for; matrix products, arithmetic and copies ran while one was open for 1% of the time, Pallas kernels for 34%

profile of v6, /device:TPU:0, one launch (start us, length us, event | category | flops | bytes accessed | tf_op | source)
XLA Modules:
  0.0 1233.3 jit_solution(12849347571507688390)
XLA Ops:
  15.6 13.1 %first.8 = (f32[2,6,64,128]{3,2,1,0:T(8,128)S(1)}, f32[2,6,64,128]{3,2,1,0:T(8,128)S(1)}, f32[2,6,64,128]{3,2,1,0:T(8,128)}, f32[2,6,64,128]{3,2,1,0:T(8,128)}, ...) custom-call(bf16[144,512]{1,0:T(8,128)(2,1)S(1)} %reshape.22.table_r, ...), custom_call_target="tpu_custom_call" | custom-call | bytes 54000000 | tf_op jit(solution)/shard_map/first/pallas_call | solution.py:130
  49.9 9.0 collective-permute-done.6.rest_0_.rest_7_
  61.6 18.2 %first.9 = (f32[3,6,64,128]{3,2,1,0:T(8,128)S(1)}, f32[3,6,64,128]{3,2,1,0:T(8,128)S(1)}, f32[3,6,64,128]{3,2,1,0:T(8,128)S(1)}, f32[3,6,64,128]{3,2,1,0:T(8,128...) custom-call(bf16[144,512]{1,0:T(8,128)(2,1)S(1)} %reshape.23.table_r, ...), custom_call_target="tpu_custom_call" | custom-call | bytes 54000000 | tf_op jit(solution)/shard_map/first/pallas_call | solution.py:130
  83.5 10.2 second.8
  104.4 11.6 collective-permute-done.7.rest_0_.rest_7_
  121.0 19.4 %first.10 = (f32[3,10,64,128]{3,2,1,0:T(8,128)S(1)}, f32[3,10,64,128]{3,2,1,0:T(8,128)S(1)}, f32[3,10,64,128]{3,2,1,0:T(8,128)}, f32[3,10,64,128]{3,2,1,0:T(8,12...) custom-call(bf16[240,512]{1,0:T(8,128)(2,1)S(1)} %reshape.25.table_r, ...), custom_call_target="tpu_custom_call" | custom-call | bytes 66000000 | tf_op jit(solution)/shard_map/first/pallas_call | solution.py:130
  142.1 12.4 %collective-permute-done.29.rest_6_ = f32[3,6,64,128]{3,2,1,0:T(8,128)} collective-permute-done((f32[3,6,64,128]{3,2,1,0:T(8,128)}, f32[3,6,64,128]{3,2,1,0:T(8,128)}, u32[]{:S(2)}, u32[]{:S(2)}) %collective-permute-start.29) | collective-permute-done | bytes 589856 | tf_op jit(solution)/shard_map/ppermute | solution.py:426
  154.5 13.8 %second.9 = f32[4,3,784,128]{3,2,1,0:T(8,128)} custom-call(s32[8]{0:T(128)S(1)} %stack.26.sources_ref, bf16[512,3072]{1,0:T(8,128)(2,1)} %constant.33.clone.table_ref, f32[3,6,64,128]{3,2,1,0:T(8,128)S(1)} %get-tuple-element.93.rest_8_.rest_0_, f32[3,6,64,128]{3,2,1,0:T(8,128)S(1)} %collective-permute-done.24.rest_1_, ...), custom_call_target="tpu_custom_call" | custom-call | bytes 39000000 | tf_op jit(solution)/shard_map/second/pallas_call | solution.py:213
  182.3 20.4 %collective-permute-done.8.rest_0_.rest_7_ = f32[3,10,64,128]{3,2,1,0:T(8,128)S(1)} collective-permute-done((f32[3,10,64,128]{3,2,1,0:T(8,128)S(1)}, f32[3,10,64,128]{3,2,1,0:T(8,128)S(1)}, u32[]{:S(2)}, u32[]{:S(2)}) %collective-permute-start.8) | collective-permute-done | bytes 983072 | tf_op jit(solution)/shard_map/ppermute | solution.py:426
  206.9 24.7 %first.11 = (f32[3,16,64,128]{3,2,1,0:T(8,128)S(1)}, f32[3,16,64,128]{3,2,1,0:T(8,128)S(1)}, f32[3,16,64,128]{3,2,1,0:T(8,128)}, f32[3,16,64,128]{3,2,1,0:T(8,12...) custom-call(bf16[384,512]{1,0:T(8,128)(2,1)S(1)} %bitcast.9, ...), custom_call_target="tpu_custom_call" | custom-call | bytes 84000000 | tf_op jit(solution)/shard_map/first/pallas_call | solution.py:130
  232.8 13.9 %third.6 = (f32[6,128,512]{2,1,0:T(8,128)S(1)}, f32[16,512]{1,0:T(8,128)S(1)}) custom-call(bf16[3072,512]{1,0:T(8,128)(2,1)} %constant.34.clone.table_ref, f32[4,1,784,128]{3,2,1,0:T(8,128)S(1)} %copy-done.8, f32[4,2,784,128]{3,2,1,0:T(8,128)} %all-to-all-done.2.rest_1_.rest_3_, f32[4,1,784,128]{3,2,1,0:T(8,128)S(1)} %copy-done.8, ...), custom_call_target="tpu_custom_call" | custom-call | bytes 39000000 | tf_op jit(solution)/shard_map/third/pallas_call | solution.py:292
  247.9 18.0 %collective-permute-done.41.rest_6_ = f32[3,10,64,128]{3,2,1,0:T(8,128)S(1)} collective-permute-done((f32[3,10,64,128]{3,2,1,0:T(8,128)}, f32[3,10,64,128]{3,2,1,0:T(8,128)S(1)}, u32[]{:S(2)}, u32[]{:S(2)}) %collective-permute-start.41) | collective-permute-done | bytes 983072 | tf_op jit(solution)/shard_map/ppermute | solution.py:426
  266.8 20.9 %second.11 = f32[4,3,1312,128]{3,2,1,0:T(8,128)} custom-call(s32[8]{0:T(128)S(1)} %stack.26.sources_ref, bf16[512,3072]{1,0:T(8,128)(2,1)} %constant.33.clone.table_ref, f32[3,10,64,128]{3,2,1,0:T(8,128)S(1)} %get-tuple-element.120.rest_9_.rest_0_, f32[3,10,64,128]{3,2,1,0:T(8,128)S(1)} %collective-permute-done.36.rest_1_, ...), custom_call_target="tpu_custom_call" | custom-call | bytes 63000000 | tf_op jit(solution)/shard_map/second/pallas_call | solution.py:213
  298.4 32.9 %collective-permute-done.9.rest_0_.rest_7_ = f32[3,16,64,128]{3,2,1,0:T(8,128)S(1)} collective-permute-done((f32[3,16,64,128]{3,2,1,0:T(8,128)}, f32[3,16,64,128]{3,2,1,0:T(8,128)S(1)}, u32[]{:S(2)}, u32[]{:S(2)}) %collective-permute-start.9) | collective-permute-done | bytes 1572896 | tf_op jit(solution)/shard_map/ppermute | solution.py:426
  339.7 38.0 %first.12 = (f32[3,22,64,128]{3,2,1,0:T(8,128)S(1)}, f32[3,22,64,128]{3,2,1,0:T(8,128)}, f32[3,22,64,128]{3,2,1,0:T(8,128)}, f32[3,22,64,128]{3,2,1,0:T(8,128)},...) custom-call(bf16[528,512]{1,0:T(8,128)(2,1)S(1)} %reshape.27.table_r, ...), custom_call_target="tpu_custom_call" | custom-call | bytes 102000000 | tf_op jit(solution)/shard_map/first/pallas_call | solution.py:130
  377.7 14.0 %third.7 = (f32[6,128,512]{2,1,0:T(8,128)S(1)}, f32[16,512]{1,0:T(8,128)S(1)}) custom-call(bf16[3072,512]{1,0:T(8,128)(2,1)} %constant.34.clone.table_ref, f32[4,3,784,128]{3,2,1,0:T(8,128)} %all-to-all-done.3.rest_0_.rest_1_, f32[4,3,784,128]{3,2,1,0:T(8,128)} %all-to-all-done.3.rest_0_.rest_1_, ...), custom_call_target="tpu_custom_call" | custom-call | bytes 39000000 | tf_op jit(solution)/shard_map/third/pallas_call | solution.py:292
  399.4 33.5 %collective-permute-done.23.rest_6_ = f32[3,16,64,128]{3,2,1,0:T(8,128)} collective-permute-done((f32[3,16,64,128]{3,2,1,0:T(8,128)}, f32[3,16,64,128]{3,2,1,0:T(8,128)}, u32[]{:S(2)}, u32[]{:S(2)}) %collective-permute-start.23) | collective-permute-done | bytes 1572896 | tf_op jit(solution)/shard_map/ppermute | solution.py:426
  432.9 32.9 %second.10 = f32[4,3,2080,128]{3,2,1,0:T(8,128)} custom-call(s32[8]{0:T(128)S(1)} %stack.26.sources_ref, bf16[512,3072]{1,0:T(8,128)(2,1)} %constant.33.clone.table_ref, f32[3,16,64,128]{3,2,1,0:T(8,128)S(1)} %copy-done.18, f32[3,16,64,128]{3,2,1,0:T(8,128)S(1)} %copy-done.26, f32[3,16,64,128]{3,2,1,0:T(8,128)} %collective-permute-done.19.rest_2_, ...), custom_call_target="tpu_custom_call" | custom-call | bytes 99000000 | tf_op jit(solution)/shard_map/second/pallas_call | solution.py:213
  481.5 45.7 %collective-permute-done.10.rest_0_.rest_7_ = f32[3,22,64,128]{3,2,1,0:T(8,128)S(1)} collective-permute-done((f32[3,22,64,128]{3,2,1,0:T(8,128)}, f32[3,22,64,128]{3,2,1,0:T(8,128)S(1)}, u32[]{:S(2)}, u32[]{:S(2)}) %collective-permute-start.10) | collective-permute-done | bytes 2162720 | tf_op jit(solution)/shard_map/ppermute | solution.py:426
  532.3 17.9 %first.13 = (f32[3,4,64,128]{3,2,1,0:T(8,128)S(1)}, f32[3,4,64,128]{3,2,1,0:T(8,128)}, f32[3,4,64,128]{3,2,1,0:T(8,128)}, f32[3,4,64,128]{3,2,1,0:T(8,128)}, f32...) custom-call(bf16[96,512]{1,0:T(8,128)(2,1)S(1)} %reshape.26.table_re, ...), custom_call_target="tpu_custom_call" | custom-call | bytes 48000000 | tf_op jit(solution)/shard_map/first/pallas_call | solution.py:130
  553.8 20.3 %third.8 = (f32[10,128,512]{2,1,0:T(8,128)S(1)}, f32[32,512]{1,0:T(8,128)S(1)}) custom-call(bf16[3072,512]{1,0:T(8,128)(2,1)} %constant.34.clone.table_ref, f32[4,3,1312,128]{3,2,1,0:T(8,128)} %all-to-all-done.5.rest_0_.rest_1_, f32[4,3,1312,128]{3,2,1,0:T(8,128)} %all-to-all-done.5.rest_0_.rest_1_, ...), custom_call_target="tpu_custom_call" | custom-call | bytes 63000000 | tf_op jit(solution)/shard_map/third/pallas_call | solution.py:292
  576.3 43.2 %collective-permute-done.32.rest_3_ = f32[3,22,64,128]{3,2,1,0:T(8,128)} collective-permute-done((f32[3,22,64,128]{3,2,1,0:T(8,128)}, f32[3,22,64,128]{3,2,1,0:T(8,128)}, u32[]{:S(2)}, u32[]{:S(2)}) %collective-permute-start.32) | collective-permute-done | bytes 2162720 | tf_op jit(solution)/shard_map/ppermute | solution.py:426
  619.9 45.9 %collective-permute-done.35.rest_6_ = f32[3,22,64,128]{3,2,1,0:T(8,128)} collective-permute-done((f32[3,22,64,128]{3,2,1,0:T(8,128)}, f32[3,22,64,128]{3,2,1,0:T(8,128)}, u32[]{:S(2)}, u32[]{:S(2)}) %collective-permute-start.35) | collective-permute-done | bytes 2162720 | tf_op jit(solution)/shard_map/ppermute | solution.py:426
  665.7 44.7 %second.12.rest_2_ = f32[4,3,2880,128]{3,2,1,0:T(8,128)} custom-call(s32[8]{0:T(128)S(1)} %stack.26.sources_ref, bf16[512,3072]{1,0:T(8,128)(2,1)} %constant.33.clone.table_ref, f32[3,22,64,128]{3,2,1,0:T(8,128)S(1)} %copy-done.16, f32[3,22,64,128]{3,2,1,0:T(8,128)S(1)} %copy-done.24, f32[3,22,64,128]{3,2,1,0:T(8,128)} %collective-permute-done.31.rest_2_, ...), custom_call_target="tpu_custom_call" | custom-call | bytes 135000000 | tf_op jit(solution)/shard_map/second/pallas_call | solution.py:213
  710.4 43.3 %all-to-all-done.4.rest_0_.rest_1_ = f32[4,3,2080,128]{3,2,1,0:T(8,128)} async-done(((f32[4,3,2080,128]{3,2,1,0:T(8,128)}), f32[4,3,2080,128]{3,2,1,0:T(8,128)}, u32[]{:S(2)}, u32[]{:S(2)}) %all-to-all-start.4) | async-done | bytes 12779552 | tf_op jit(solution)/shard_map/all_to_all | solution.py:476
  773.5 30.7 %third.9 = (f32[16,128,512]{2,1,0:T(8,128)}, f32[32,512]{1,0:T(8,128)S(1)}) custom-call(bf16[3072,512]{1,0:T(8,128)(2,1)S(1)} %copy-done.2, f32[4,3,2080,128]{3,2,1,0:T(8,128)} %all-to-all-done.4.rest_0_.rest_1_, f32[4,3,2080,128]{3,2,1,0:T(8,128)} %all-to-all-done.4.rest_0_.rest_1_, f32[4,3,2880,128]{3,2,1,0:T(8,128)} %second.12.rest_2_, ...), custom_call_target="tpu_custom_call" | custom-call | bytes 99000000 | tf_op jit(solution)/shard_map/third/pallas_call | solution.py:292
  824.2 9.7 normals.12
  842.3 9.5 second.13.rest_2_
  851.8 291.2 %all-to-all-done.7.rest_0_.rest_1_ = f32[4,3,2880,128]{3,2,1,0:T(8,128)} async-done(((f32[4,3,2880,128]{3,2,1,0:T(8,128)}), f32[4,3,2880,128]{3,2,1,0:T(8,128)}, u32[]{:S(2)}, u32[]{:S(2)}) %all-to-all-start.7) | async-done | bytes 17694752 | tf_op jit(solution)/shard_map/all_to_all | solution.py:476
  1147.8 41.1 %third.10 = (f32[22,128,512]{2,1,0:T(8,128)}, f32[64,512]{1,0:T(8,128)S(1)}) custom-call(bf16[3072,512]{1,0:T(8,128)(2,1)S(1)} %copy-done.2, f32[4,3,2880,128]{3,2,1,0:T(8,128)} %all-to-all-done.7.rest_0_.rest_1_, f32[4,3,2880,128]{3,2,1,0:T(8,128)} %all-to-all-done.7.rest_0_.rest_1_, f32[4,3,520,128]{3,2,1,0:T(8,128)} %second.13.rest_2_, ...), custom_call_target="tpu_custom_call" | custom-call | bytes 135000000 | tf_op jit(solution)/shard_map/third/pallas_call | solution.py:292
  1191.1 15.7 %normals.14 = (f32[64,128,512]{2,1,0:T(8,128)}, bf16[3,64,128,512]{3,2,1,0:T(8,128)(2,1)}, f32[8,128]{1,0:T(8,128)S(1)}) custom-call(f32[22,128,512]{2,1,0:T(8,128)} %get-tuple-element.151.behind_ref.centre_ref.before_ref, f32[16,128,512]{2,1,0:T(8,128)S(1)} %copy-done.1, ...), custom_call_target="tpu_custom_call", output_to_operand_aliasing={{0}: (4, {}), {1}: (5, {})} | custom-call | bytes 34500000 | tf_op jit(solution)/shard_map/normals/pallas_call | solution.py:347
  1206.9 12.0 all-to-all-done.6.rest_0_.rest_1_
  (235 shorter events, 204.2 us)
Async XLA Ops:
  41.4 52.3 %all-to-all-start.1 = ((f32[4,1,784,128]{3,2,1,0:T(8,128)}), f32[4,1,784,128]{3,2,1,0:T(8,128)S(1)}, u32[]{:S(2)}, u32[]{:S(2)}) async-start(f32[4,1,784,128]{3,2,1,0:T(8,128)} %second.7), calls=%async_computation.1 | async-start | bytes 3211264 | tf_op jit(solution)/shard_map/all_to_all | solution.py:476
  94.9 77.8 %all-to-all-start.2 = ((f32[4,2,784,128]{3,2,1,0:T(8,128)}), f32[4,2,784,128]{3,2,1,0:T(8,128)}, u32[]{:S(2)}, u32[]{:S(2)}) async-start(f32[4,2,784,128]{3,2,1,0:T(8,128)} %second.8), calls=%async_computation.2 | async-start | bytes 6422528 | tf_op jit(solution)/shard_map/all_to_all | solution.py:476
  101.5 39.8 %collective-permute-start.25 = (f32[3,6,64,128]{3,2,1,0:T(8,128)}, f32[3,6,64,128]{3,2,1,0:T(8,128)}, u32[]{:S(2)}, u32[]{:S(2)}) collective-permute-start(f32[3,6,64,128]{3,2,1,0:T(8,128)} %copy-done.46), channel_id=1, source_target_pairs={{0,8},{4,12},{8,0},{12,4},{16,24},{20,28},{24,16},{28,20},{1,9},{5... | collective-permute-start | bytes 1769480 | tf_op jit(solution)/shard_map/ppermute | solution.py:426
  102.3 39.0 %collective-permute-start.26 = (f32[3,6,64,128]{3,2,1,0:T(8,128)}, f32[3,6,64,128]{3,2,1,0:T(8,128)}, u32[]{:S(2)}, u32[]{:S(2)}) collective-permute-start(f32[3,6,64,128]{3,2,1,0:T(8,128)} %copy-done.45), channel_id=1, source_target_pairs={{0,12},{4,8},{8,4},{12,0},{16,28},{20,24},{24,20},{28,16},{1,13},{... | collective-permute-start | bytes 1769480 | tf_op jit(solution)/shard_map/ppermute | solution.py:426
  102.9 38.4 %collective-permute-start.27 = (f32[3,6,64,128]{3,2,1,0:T(8,128)}, f32[3,6,64,128]{3,2,1,0:T(8,128)}, u32[]{:S(2)}, u32[]{:S(2)}) collective-permute-start(f32[3,6,64,128]{3,2,1,0:T(8,128)} %copy-done.44), channel_id=1, source_target_pairs={{0,16},{4,20},{8,24},{12,28},{16,0},{20,4},{24,8},{28,12},{1,17},{... | collective-permute-start | bytes 1769480 | tf_op jit(solution)/shard_map/ppermute | solution.py:426
  172.7 115.0 %all-to-all-start.3 = ((f32[4,3,784,128]{3,2,1,0:T(8,128)}), f32[4,3,784,128]{3,2,1,0:T(8,128)}, u32[]{:S(2)}, u32[]{:S(2)}) async-start(f32[4,3,784,128]{3,2,1,0:T(8,128)} %second.9), calls=%async_computation.3 | async-start | bytes 9633792 | tf_op jit(solution)/shard_map/all_to_all | solution.py:476
  179.4 68.5 %collective-permute-start.37 = (f32[3,10,64,128]{3,2,1,0:T(8,128)}, f32[3,10,64,128]{3,2,1,0:T(8,128)S(1)}, u32[]{:S(2)}, u32[]{:S(2)}) collective-permute-start(f32[3,10,64,128]{3,2,1,0:T(8,128)} %get-tuple-element.130), channel_id=1, source_target_pairs={{0,8},{4,12},{8,0},{12,4},{16,24},{20,28},{24,16},{28,20},{1,9},{5... | collective-permute-start | bytes 2949128 | tf_op jit(solution)/shard_map/ppermute | solution.py:426
  180.0 67.9 %collective-permute-start.38 = (f32[3,10,64,128]{3,2,1,0:T(8,128)}, f32[3,10,64,128]{3,2,1,0:T(8,128)S(1)}, u32[]{:S(2)}, u32[]{:S(2)}) collective-permute-start(f32[3,10,64,128]{3,2,1,0:T(8,128)} %get-tuple-element.131), channel_id=1, source_target_pairs={{0,12},{4,8},{8,4},{12,0},{16,28},{20,24},{24,20},{28,16},{1,13},{... | collective-permute-start | bytes 2949128 | tf_op jit(solution)/shard_map/ppermute | solution.py:426
  180.7 67.2 %collective-permute-start.39 = (f32[3,10,64,128]{3,2,1,0:T(8,128)}, f32[3,10,64,128]{3,2,1,0:T(8,128)S(1)}, u32[]{:S(2)}, u32[]{:S(2)}) collective-permute-start(f32[3,10,64,128]{3,2,1,0:T(8,128)} %get-tuple-element.132), channel_id=1, source_target_pairs={{0,16},{4,20},{8,24},{12,28},{16,0},{20,4},{24,8},{28,12},{1,17},{... | collective-permute-start | bytes 2949128 | tf_op jit(solution)/shard_map/ppermute | solution.py:426
  202.8 45.1 %collective-permute-start.40 = (f32[3,10,64,128]{3,2,1,0:T(8,128)}, f32[3,10,64,128]{3,2,1,0:T(8,128)S(1)}, u32[]{:S(2)}, u32[]{:S(2)}) collective-permute-start(f32[3,10,64,128]{3,2,1,0:T(8,128)} %get-tuple-element.133), channel_id=1, source_target_pairs={{0,20},{4,16},{8,28},{12,24},{16,4},{20,0},{24,12},{28,8},{1,21},{... | collective-permute-start | bytes 2949128 | tf_op jit(solution)/shard_map/ppermute | solution.py:426
  203.3 62.6 %collective-permute-start.41 = (f32[3,10,64,128]{3,2,1,0:T(8,128)}, f32[3,10,64,128]{3,2,1,0:T(8,128)S(1)}, u32[]{:S(2)}, u32[]{:S(2)}) collective-permute-start(f32[3,10,64,128]{3,2,1,0:T(8,128)} %get-tuple-element.134), channel_id=1, source_target_pairs={{0,24},{4,28},{8,16},{12,20},{16,8},{20,12},{24,0},{28,4},{1,25},{... | collective-permute-start | bytes 2949128 | tf_op jit(solution)/shard_map/ppermute | solution.py:426
  287.7 182.6 %all-to-all-start.5 = ((f32[4,3,1312,128]{3,2,1,0:T(8,128)}), f32[4,3,1312,128]{3,2,1,0:T(8,128)}, u32[]{:S(2)}, u32[]{:S(2)}) async-start(f32[4,3,1312,128]{3,2,1,0:T(8,128)} %second.11), calls=%async_computation.5 | async-start | bytes 16121856 | tf_op jit(solution)/shard_map/all_to_all | solution.py:476
  293.7 37.6 %collective-permute-start.9 = (f32[3,16,64,128]{3,2,1,0:T(8,128)}, f32[3,16,64,128]{3,2,1,0:T(8,128)S(1)}, u32[]{:S(2)}, u32[]{:S(2)}) collective-permute-start(f32[3,16,64,128]{3,2,1,0:T(8,128)} %get-tuple-element.98), channel_id=1, source_target_pairs={{0,28},{4,24},{8,20},{12,16},{16,12},{20,8},{24,4},{28,0},{1,29},{... | collective-permute-start | bytes 4718600 | tf_op jit(solution)/shard_map/ppermute | solution.py:426
  294.8 38.9 %collective-permute-start.18 = (f32[3,16,64,128]{3,2,1,0:T(8,128)S(1)}, f32[3,16,64,128]{3,2,1,0:T(8,128)S(1)}, u32[]{:S(2)}, u32[]{:S(2)}) collective-permute-start(f32[3,16,64,128]{3,2,1,0:T(8,128)S(1)} %copy-done.39), channel_id=1, source_target_pairs={{0,4},{4,0},{8,12},{12,8},{16,20},{20,16},{24,28},{28,24},{1,5},{5... | collective-permute-start | bytes 4718600 | tf_op jit(solution)/shard_map/ppermute | solution.py:426
  294.8 98.1 %collective-permute-start.19 = (f32[3,16,64,128]{3,2,1,0:T(8,128)}, f32[3,16,64,128]{3,2,1,0:T(8,128)}, u32[]{:S(2)}, u32[]{:S(2)}) collective-permute-start(f32[3,16,64,128]{3,2,1,0:T(8,128)} %get-tuple-element.109), channel_id=1, source_target_pairs={{0,8},{4,12},{8,0},{12,4},{16,24},{20,28},{24,16},{28,20},{1,9},{5... | collective-permute-start | bytes 4718600 | tf_op jit(solution)/shard_map/ppermute | solution.py:426
  296.1 102.0 %collective-permute-start.20 = (f32[3,16,64,128]{3,2,1,0:T(8,128)}, f32[3,16,64,128]{3,2,1,0:T(8,128)}, u32[]{:S(2)}, u32[]{:S(2)}) collective-permute-start(f32[3,16,64,128]{3,2,1,0:T(8,128)} %get-tuple-element.110), channel_id=1, source_target_pairs={{0,12},{4,8},{8,4},{12,0},{16,28},{20,24},{24,20},{28,16},{1,13},{... | collective-permute-start | bytes 4718600 | tf_op jit(solution)/shard_map/ppermute | solution.py:426
  296.7 101.5 %collective-permute-start.21 = (f32[3,16,64,128]{3,2,1,0:T(8,128)}, f32[3,16,64,128]{3,2,1,0:T(8,128)}, u32[]{:S(2)}, u32[]{:S(2)}) collective-permute-start(f32[3,16,64,128]{3,2,1,0:T(8,128)} %get-tuple-element.111), channel_id=1, source_target_pairs={{0,16},{4,20},{8,24},{12,28},{16,0},{20,4},{24,8},{28,12},{1,17},{... | collective-permute-start | bytes 4718600 | tf_op jit(solution)/shard_map/ppermute | solution.py:426
  332.5 66.9 %collective-permute-start.22 = (f32[3,16,64,128]{3,2,1,0:T(8,128)}, f32[3,16,64,128]{3,2,1,0:T(8,128)}, u32[]{:S(2)}, u32[]{:S(2)}) collective-permute-start(f32[3,16,64,128]{3,2,1,0:T(8,128)} %get-tuple-element.112), channel_id=1, source_target_pairs={{0,20},{4,16},{8,28},{12,24},{16,4},{20,0},{24,12},{28,8},{1,21},{... | collective-permute-start | bytes 4718600 | tf_op jit(solution)/shard_map/ppermute | solution.py:426
  334.8 98.0 %collective-permute-start.23 = (f32[3,16,64,128]{3,2,1,0:T(8,128)}, f32[3,16,64,128]{3,2,1,0:T(8,128)}, u32[]{:S(2)}, u32[]{:S(2)}) collective-permute-start(f32[3,16,64,128]{3,2,1,0:T(8,128)} %get-tuple-element.113), channel_id=1, source_target_pairs={{0,24},{4,28},{8,16},{12,20},{16,8},{20,12},{24,0},{28,4},{1,25},{... | collective-permute-start | bytes 4718600 | tf_op jit(solution)/shard_map/ppermute | solution.py:426
  470.3 283.5 %all-to-all-start.4 = ((f32[4,3,2080,128]{3,2,1,0:T(8,128)}), f32[4,3,2080,128]{3,2,1,0:T(8,128)}, u32[]{:S(2)}, u32[]{:S(2)}) async-start(f32[4,3,2080,128]{3,2,1,0:T(8,128)} %second.10), calls=%async_computation.4 | async-start | bytes 25559040 | tf_op jit(solution)/shard_map/all_to_all | solution.py:476
  476.7 50.5 %collective-permute-start.10 = (f32[3,22,64,128]{3,2,1,0:T(8,128)}, f32[3,22,64,128]{3,2,1,0:T(8,128)S(1)}, u32[]{:S(2)}, u32[]{:S(2)}) collective-permute-start(f32[3,22,64,128]{3,2,1,0:T(8,128)} %get-tuple-element.99), channel_id=1, source_target_pairs={{0,28},{4,24},{8,20},{12,16},{16,12},{20,8},{24,4},{28,0},{1,29},{... | collective-permute-start | bytes 6488072 | tf_op jit(solution)/shard_map/ppermute | solution.py:426
  477.4 50.6 %collective-permute-start.30 = (f32[3,22,64,128]{3,2,1,0:T(8,128)}, f32[3,22,64,128]{3,2,1,0:T(8,128)S(1)}, u32[]{:S(2)}, u32[]{:S(2)}) collective-permute-start(f32[3,22,64,128]{3,2,1,0:T(8,128)} %get-tuple-element.123), channel_id=1, source_target_pairs={{0,4},{4,0},{8,12},{12,8},{16,20},{20,16},{24,28},{28,24},{1,5},{5... | collective-permute-start | bytes 6488072 | tf_op jit(solution)/shard_map/ppermute | solution.py:426
  478.0 98.3 %collective-permute-start.31 = (f32[3,22,64,128]{3,2,1,0:T(8,128)}, f32[3,22,64,128]{3,2,1,0:T(8,128)}, u32[]{:S(2)}, u32[]{:S(2)}) collective-permute-start(f32[3,22,64,128]{3,2,1,0:T(8,128)} %get-tuple-element.124), channel_id=1, source_target_pairs={{0,8},{4,12},{8,0},{12,4},{16,24},{20,28},{24,16},{28,20},{1,9},{5... | collective-permute-start | bytes 6488072 | tf_op jit(solution)/shard_map/ppermute | solution.py:426
  479.3 140.2 %collective-permute-start.32 = (f32[3,22,64,128]{3,2,1,0:T(8,128)}, f32[3,22,64,128]{3,2,1,0:T(8,128)}, u32[]{:S(2)}, u32[]{:S(2)}) collective-permute-start(f32[3,22,64,128]{3,2,1,0:T(8,128)} %get-tuple-element.125), channel_id=1, source_target_pairs={{0,12},{4,8},{8,4},{12,0},{16,28},{20,24},{24,20},{28,16},{1,13},{... | collective-permute-start | bytes 6488072 | tf_op jit(solution)/shard_map/ppermute | solution.py:426
  479.4 140.2 %collective-permute-start.33 = (f32[3,22,64,128]{3,2,1,0:T(8,128)}, f32[3,22,64,128]{3,2,1,0:T(8,128)}, u32[]{:S(2)}, u32[]{:S(2)}) collective-permute-start(f32[3,22,64,128]{3,2,1,0:T(8,128)} %get-tuple-element.126), channel_id=1, source_target_pairs={{0,16},{4,20},{8,24},{12,28},{16,0},{20,4},{24,8},{28,12},{1,17},{... | collective-permute-start | bytes 6488072 | tf_op jit(solution)/shard_map/ppermute | solution.py:426
  527.1 92.7 %collective-permute-start.34 = (f32[3,22,64,128]{3,2,1,0:T(8,128)}, f32[3,22,64,128]{3,2,1,0:T(8,128)}, u32[]{:S(2)}, u32[]{:S(2)}) collective-permute-start(f32[3,22,64,128]{3,2,1,0:T(8,128)} %get-tuple-element.127), channel_id=1, source_target_pairs={{0,20},{4,16},{8,28},{12,24},{16,4},{20,0},{24,12},{28,8},{1,21},{... | collective-permute-start | bytes 6488072 | tf_op jit(solution)/shard_map/ppermute | solution.py:426
  529.2 136.5 %collective-permute-start.35 = (f32[3,22,64,128]{3,2,1,0:T(8,128)}, f32[3,22,64,128]{3,2,1,0:T(8,128)}, u32[]{:S(2)}, u32[]{:S(2)}) collective-permute-start(f32[3,22,64,128]{3,2,1,0:T(8,128)} %get-tuple-element.128), channel_id=1, source_target_pairs={{0,24},{4,28},{8,16},{12,20},{16,8},{20,12},{24,0},{28,4},{1,25},{... | collective-permute-start | bytes 6488072 | tf_op jit(solution)/shard_map/ppermute | solution.py:426
  753.8 389.2 %all-to-all-start.7 = ((f32[4,3,2880,128]{3,2,1,0:T(8,128)}), f32[4,3,2880,128]{3,2,1,0:T(8,128)}, u32[]{:S(2)}, u32[]{:S(2)}) async-start(f32[4,3,2880,128]{3,2,1,0:T(8,128)} %second.12.rest_2_), calls=%async_computation.7 | async-start | bytes 35389440 | tf_op jit(solution)/shard_map/all_to_all | solution.py:476
  761.0 46.8 %collective-permute-start.11 = (f32[3,4,64,128]{3,2,1,0:T(8,128)}, f32[3,4,64,128]{3,2,1,0:T(8,128)S(1)}, u32[]{:S(2)}, u32[]{:S(2)}) collective-permute-start(f32[3,4,64,128]{3,2,1,0:T(8,128)} %get-tuple-element.101), channel_id=1, source_target_pairs={{0,4},{4,0},{8,12},{12,8},{16,20},{20,16},{24,28},{28,24},{1,5},{5... | collective-permute-start | bytes 1179656 | tf_op jit(solution)/shard_map/ppermute | solution.py:426
  761.0 47.4 %collective-permute-start.12 = (f32[3,4,64,128]{3,2,1,0:T(8,128)}, f32[3,4,64,128]{3,2,1,0:T(8,128)S(1)}, u32[]{:S(2)}, u32[]{:S(2)}) collective-permute-start(f32[3,4,64,128]{3,2,1,0:T(8,128)} %get-tuple-element.102), channel_id=1, source_target_pairs={{0,8},{4,12},{8,0},{12,4},{16,24},{20,28},{24,16},{28,20},{1,9},{5... | collective-permute-start | bytes 1179656 | tf_op jit(solution)/shard_map/ppermute | solution.py:426
  764.0 44.5 %collective-permute-start.43 = (f32[1,128,512]{2,1,0:T(8,128)S(1)}, f32[1,128,512]{2,1,0:T(8,128)S(1)}, u32[]{:S(2)}, u32[]{:S(2)}) collective-permute-start(f32[1,128,512]{2,1,0:T(8,128)S(1)} %slice.31), channel_id=1, source_target_pairs={{0,4},{4,8},{8,12},{12,16},{16,20},{20,24},{24,28},{28,0},{1,5},{5... | collective-permute-start | bytes 786440 | tf_op jit(solution)/shard_map/ppermute | solution.py:452
  1143.0 75.9 %all-to-all-start.6 = ((f32[4,3,520,128]{3,2,1,0:T(8,128)}), f32[4,3,520,128]{3,2,1,0:T(8,128)}, u32[]{:S(2)}, u32[]{:S(2)}) async-start(f32[4,3,520,128]{3,2,1,0:T(8,128)} %second.13.rest_2_), calls=%async_computation.6 | async-start | bytes 6389760 | tf_op jit(solution)/shard_map/all_to_all | solution.py:476
  (76 other events, 1715.7 us)
